TPU v7x, 32 devices: a whole 2x2x4 slice. The times are simulated.
32 devices in a mesh: gx: 8 (over y, x, core), gy: 4 (over z).
Axes of the slice: x: 2, y: 2, z: 4, core: 2. Of those that a mesh axis runs over, the one named last changes fastest.
Arguments:
- velocity: float32 [2, 10, 768, 1536], P(None, None, 'gx', 'gy'), may hold values from -6 to 6
- viscosity: float32 [10, 768, 1536], P(None, 'gx', 'gy'), may hold values from 0.05 to 0.8
- friction: float32 [768, 1536], P('gx', 'gy'), may hold values from 0.1 to 2
- ice_mask: int32 [8, 4], P('gx', 'gy'), may hold values from 0 to 1, as said below
- obs_tiles: float32 [8, 4, 8, 4, 4, 3, 128], P('gx', 'gy'), as said below
- obs_cell: int32 [8, 4, 8, 4, 4], P('gx', 'gy'), may hold values from 0 to 287, as said below
- obs_count: int32 [8, 4, 8, 4], P('gx', 'gy'), may hold values from 0 to 4, as said below
Outputs:
- adjoint: float32 [2, 10, 768, 1536], P(None, None, 'gx', 'gy')
- friction_gradient: float32 [768, 1536], P('gx', 'gy')
Inputs may be any that keep to these rules, and one draw needn't show every extreme that they name: `ice_mask`: some block is ice-covered in every draw. `obs_count`: zero for every owner block whose ice_mask is 0; in every draw some owner block receives 4 live tiles from every sending block. `obs_cell`: slots at or beyond the live count also hold anchors in range. `obs_tiles`: channel 2 holds weights between 0.3 and 3.
All inputs are finite; a program needn't handle non-finite values.
Results may differ from a plain program's by a relative error of at most 0.00002.
Values sent between devices are 32-bit elements; how exact they have to be, the bound alone decides.
No kernel may reach another device: no remote copies, remote signals or barrier semaphores. Data moves between devices by JAX's collectives and lax.ppermute only.
A program may use at most 128 MiB of HBM per device.

v0:
```python
import jax
import jax.numpy as jnp
from jax import lax
from jax.sharding import PartitionSpec as P

SWEEPS = 3


VERTICAL_GAIN = 2.0
RELAX_WEIGHT = 0.8


def padded_2(block, sides, width):
    for axis, dim in sides:
        count = lax.axis_size(axis)
        forward = [(i, i + 1) for i in range(count - 1)]
        backward = [(target, source) for source, target in forward]
        low = lax.ppermute(
            lax.slice_in_dim(block, block.shape[dim] - width, None, axis=dim), axis, forward
        )
        high = lax.ppermute(lax.slice_in_dim(block, 0, width, axis=dim), axis, backward)
        block = jnp.concatenate([low, block, high], axis=dim)
    return block


def column_factors(padded_visc, friction_field):
    center = padded_visc[:, 1:-1, 1:-1]
    west_face = 0.5 * (center + padded_visc[:, :-2, 1:-1])
    east_face = 0.5 * (center + padded_visc[:, 2:, 1:-1])
    south_face = 0.5 * (center + padded_visc[:, 1:-1, :-2])
    north_face = 0.5 * (center + padded_visc[:, 1:-1, 2:])
    upper_face = VERTICAL_GAIN * 0.5 * (center[:-1] + center[1:])
    layer_count = center.shape[0]
    diagonal = west_face + east_face + south_face + north_face
    pivots = []
    ratios = []
    for level in range(layer_count):
        entry = diagonal[level]
        if level == 0:
            entry = entry + friction_field
        if level < layer_count - 1:
            entry = entry + upper_face[level]
        if level > 0:
            entry = entry + upper_face[level - 1] + upper_face[level - 1] * ratios[level - 1]
        pivots.append(entry)
        if level < layer_count - 1:
            ratios.append(-upper_face[level] / entry)
    return (west_face, east_face, south_face, north_face, upper_face, pivots, ratios)


def relax(padded_adj, rhs_field, factors, icefield):
    west_face, east_face, south_face, north_face, upper_face, pivots, ratios = factors
    center = padded_adj[..., 1:-1, 1:-1]
    driven = (
        rhs_field + west_face * padded_adj[..., :-2, 1:-1] + east_face * padded_adj[..., 2:, 1:-1]
    )
    driven = (
        driven + south_face * padded_adj[..., 1:-1, :-2] + north_face * padded_adj[..., 1:-1, 2:]
    )
    layer_count = len(pivots)
    forward = []
    for level in range(layer_count):
        value = driven[:, level]
        if level > 0:
            value = value + upper_face[level - 1] * forward[level - 1]
        forward.append(value / pivots[level])
    solved = [forward[-1]]
    for level in range(layer_count - 2, -1, -1):
        solved.insert(0, forward[level] - ratios[level] * solved[0])
    stacked = jnp.stack(solved, axis=1)
    blended = (1.0 - RELAX_WEIGHT) * center + RELAX_WEIGHT * stacked
    return jnp.where(icefield > 0.0, icefield * blended, 0.0)


def pad_cycle(field_value):
    widths = [(0, 0)] * (field_value.ndim - 2) + [(1, 1), (1, 1)]
    return jnp.pad(field_value, widths)


def per_device(velocity, viscosity, friction, ice_mask, obs_tiles, obs_cell, obs_count):
    layer_count = velocity.shape[1]
    rows_dev = velocity.shape[2]
    cols_dev = velocity.shape[3]
    tile_len = obs_tiles.shape[-1]
    slot_count = obs_cell.shape[-1]
    icefield = jnp.broadcast_to(ice_mask.astype(jnp.float32), (rows_dev, cols_dev))
    live_slot = (
        jnp.arange(slot_count, dtype=jnp.int32)[None, None, None, None, :] < obs_count[..., None]
    ).astype(jnp.float32)
    weighted = obs_tiles[..., 2, :] * live_slot[..., None]
    outgoing = jnp.concatenate([obs_tiles[..., :2, :], weighted[..., None, :]], axis=-2)
    tiles_in, cells_in = (
        lax.all_to_all(
            lax.all_to_all(outgoing, "gx", split_axis=2, concat_axis=0, tiled=True),
            "gy",
            split_axis=3,
            concat_axis=1,
            tiled=True,
        ),
        lax.all_to_all(
            lax.all_to_all(obs_cell, "gx", split_axis=2, concat_axis=0, tiled=True),
            "gy",
            split_axis=3,
            concat_axis=1,
            tiled=True,
        ),
    )
    tiles_flat = tiles_in.reshape(-1, 3, tile_len)
    cells_flat = cells_in.reshape(-1)
    surface = velocity[:, layer_count - 1].reshape(2, -1, tile_len)
    sampled = surface[:, cells_flat, :]
    observed = jnp.moveaxis(tiles_flat[:, :2, :], 1, 0)
    contrib = tiles_flat[:, 2, :][None] * (sampled - observed)
    top_layer = jnp.zeros(surface.shape, jnp.float32).at[:, cells_flat].add(contrib)
    top_plane = top_layer.reshape(2, rows_dev, cols_dev)
    rhs_field = jnp.zeros(velocity.shape, jnp.float32).at[:, layer_count - 1].set(top_plane)
    visc_padded = padded_2(viscosity, (("gx", 1), ("gy", 2)), 1)
    factors = column_factors(visc_padded, friction)
    adjoint = jnp.zeros(velocity.shape, jnp.float32)
    for sweep_index in range(SWEEPS):
        if sweep_index == 0:
            padded = pad_cycle(adjoint)
        else:
            padded = padded_2(adjoint, (("gx", 2), ("gy", 3)), 1)
        adjoint = relax(padded, rhs_field, factors, icefield)
    gradient = -icefield * (adjoint[0, 0] * velocity[0, 0] + adjoint[1, 0] * velocity[1, 0])
    return (adjoint, gradient)


def solution(mesh):
    placed = (
        P(None, None, "gx", "gy"),
        P(None, "gx", "gy"),
        P("gx", "gy"),
        P("gx", "gy"),
        P("gx", "gy", None, None, None, None, None),
        P("gx", "gy", None, None, None),
        P("gx", "gy", None, None),
    )
    return jax.shard_map(
        per_device,
        mesh=mesh,
        in_specs=placed,
        out_specs=(P(None, None, "gx", "gy"), P("gx", "gy")),
        check_vma=False,
    )
```

profile of v0, /device:TPU:1, one launch (start us, length us, event | category | flops | bytes accessed | tf_op | source)
XLA Modules:
  0.0 221.6 jit_solution(9838443924022955917)
XLA Ops:
  2.3 2.0 collective-permute-start.1
  4.3 4.5 %collective-permute-start = (f32[10,1,384]{2,1,0:T(1,128)}, f32[10,1,384]{2,1,0:T(1,128)}, u32[]{:S(2)}, u32[]{:S(2)}) collective-permute-start(f32[10,1,384]{2,1,0:T(1,128)} %get-tuple-element.92), channel_id=1, source_target_pairs={{0,4},{4,8},{8,12},{12,16},{16,20},{20,24},{24,28},{1,5},{5,9},{9,... | collective-permute-start | bytes 46088 | tf_op jit(solution)/shard_map/ppermute | solution.py:18
  10.1 3.9 %all-to-all-start = ((s32[1,1,8,4,4]{4,3,1,0,2:T(4,128)}), s32[1,1,8,4,4]{4,3,1,0,2:T(4,128)}, u32[]{:S(2)}, u32[]{:S(2)}) async-start(s32[1,1,8,4,4]{4,3,1,0,2:T(4,128)} %copy.99), calls=%async_computation | async-start | bytes 32768 | tf_op jit(solution)/shard_map/all_to_all | solution.py:101
  14.0 1.8 copy.97
  19.4 2.4 %slice_bitcast_fusion.15 = (f32[96,384]{0,1:T(8,128)S(1)}, f32[96,384]{0,1:T(8,128)}, f32[96,384]{0,1:T(8,128)S(1)}, f32[96,384]{0,1:T(8,128)S(1)}, f32[96,384]{...) fusion(f32[9,96,384]{1,2,0:T(8,128)} %slice_add_fusion), kind=kLoop, calls=%fused_computation.198 | loop fusion | bytes 2654208 | tf_op jit(solution)/shard_map/squeeze | solution.py:42
  23.6 1.7 copy.127
  29.0 4.6 %all-to-all-start.1 = ((s32[8,1,1,4,4]{0,4,2,1,3:T(4,128)}), s32[8,1,1,4,4]{0,4,2,1,3:T(4,128)S(1)}, u32[]{:S(2)}, u32[]{:S(2)}) async-start(s32[8,1,1,4,4]{0,4,2,1,3:T(4,128)} %copy.101), calls=%async_computation.1 | async-start | bytes 16384 | tf_op jit(solution)/shard_map/all_to_all | solution.py:100
  38.1 5.6 %all-to-all-start.2 = ((f32[1,1,8,4,4,3,128]{6,4,5,3,1,0,2:T(4,128)}), f32[1,1,8,4,4,3,128]{6,4,5,3,1,0,2:T(4,128)S(1)}, u32[]{:S(2)}, u32[]{:S(2)}) async-start(f32[1,1,8,4,4,3,128]{6,4,5,3,1,0,2:T(4,128)} %pad_maximum_fusion.30), calls=%async_computation.2 | async-start | bytes 393216 | tf_op jit(solution)/shard_map/all_to_all | solution.py:94
  43.9 2.6 %copy.112 = f32[10,1,384]{1,2,0:T(8,128)} copy(f32[10,1,384]{2,1,0:T(1,128)} %collective-permute-done.1) | data formatting | bytes 30720 | tf_op jit(solution)/shard_map/ppermute | solution.py:21
  46.5 2.6 %copy.95 = f32[10,1,384]{1,2,0:T(8,128)} copy(f32[10,1,384]{2,1,0:T(1,128)} %collective-permute-done) | data formatting | bytes 30720 | tf_op jit(solution)/shard_map/ppermute | solution.py:18
  50.0 2.2 %collective-permute-start.2 = (f32[10,98,1]{1,2,0:T(1,128)S(1)}, f32[10,98,1]{1,2,0:T(1,128)S(1)}, u32[]{:S(2)}, u32[]{:S(2)}) collective-permute-start(f32[10,98,1]{1,2,0:T(1,128)S(1)} %get-tuple-element.74), channel_id=1, source_target_pairs={{0,1},{1,2},{2,3},{4,5},{5,6},{6,7},{8,9},{9,10},{10,11},{12,13},{... | collective-permute-start | bytes 11768 | tf_op jit(solution)/shard_map/ppermute | solution.py:18
  53.6 2.4 %gather_fusion = f32[128,2,128]{2,1,0:T(2,128)} fusion(f32[2,288,128]{2,0,1:T(2,128)} %copy.108, s32[1024]{0:T(1024)S(1)} %pad_clamp_fusion), kind=kCustom, calls=%fused_computation | custom fusion | bytes 262656 | tf_op jit(solution)/shard_map/gather | solution.py:111
  56.6 10.6 %add_add_fusion = (f32[10,96,384]{1,2,0:T(8,128)S(1)}, f32[10,96,384]{1,2,0:T(8,128)}, f32[10,96,384]{1,2,0:T(8,128)}, f32[10,96,384]{1,2,0:T(8,128)}, f32[10,96,384]{1,2,0:T(8,128)}) fusion(f32[10,96,384]{1,2,0:T(8,128)S(1)} %copy.97, f32[10,1,384]{1,2,0:T(8,128)} %copy.112, f32[10,1,384]{1,2,0:T(8,128)} %copy.95, ...), kind=kLoop, calls=%fused_computation.62 | loop fusion | flops 7004160 | bytes 8885920 | tf_op jit(solution)/shard_map/add | solution.py:34
  71.6 3.0 %copy.114 = f32[10,96,384]{2,1,0:T(8,128)} copy(f32[10,96,384]{1,2,0:T(8,128)} %get-tuple-element.69) | data formatting | bytes 2949120 | tf_op jit(solution)/shard_map/mul | solution.py:29
  74.5 2.7 %copy.119 = f32[10,96,384]{2,1,0:T(8,128)} copy(f32[10,96,384]{1,2,0:T(8,128)} %get-tuple-element.70) | data formatting | bytes 2949120 | tf_op jit(solution)/shard_map/mul | solution.py:30
  80.2 1.7 copy.132
  84.8 1.7 copy.125
  86.5 1.7 copy.126
  88.2 1.7 copy.128
  100.2 4.2 %all-to-all-start.3 = ((f32[8,1,1,4,4,3,128]{6,4,5,0,2,1,3:T(4,128)}), f32[8,1,1,4,4,3,128]{6,4,5,0,2,1,3:T(4,128)}, u32[]{:S(2)}, u32[]{:S(2)}) async-start(f32[8,1,1,4,4,3,128]{6,4,5,0,2,1,3:T(4,128)} %copy.106), calls=%async_computation.3 | async-start | bytes 393216 | tf_op jit(solution)/shard_map/all_to_all | solution.py:93
  104.6 3.3 %fusion = f32[2,10,96,384]{3,2,0,1:T(8,128)} fusion(f32[2,10,96,384]{3,2,0,1:T(8,128)S(1)} %broadcast.816, f32[10,96,384]{2,1,0:T(8,128)} %copy.98), kind=kLoop, calls=%fused_computation.6 | loop fusion | flops 737280 | bytes 7372800 | tf_op jit(solution)/shard_map/mul | solution.py:55
  110.6 1.7 fusion.90
  113.1 13.2 %scatter_fusion = f32[2,288,128]{2,0,1:T(2,128)} fusion(f32[2,288,128]{2,0,1:T(2,128)} %broadcast_in_dim.16, s32[128]{0:T(128)S(1)} %fusion.92, f32[128,2,128]{2,1,0:T(2,128)} %fusion.90), kind=kCustom, calls=%fused_computation.1 | custom fusion | flops 32768 | bytes 393728 | tf_op jit(solution)/shard_map/scatter-add | solution.py:114
  126.2 1.7 copy.110
  128.0 1.7 reshape.140
  129.7 1.8 fusion.58
  131.7 4.3 %fusion.4 = f32[2,10,96,384]{3,2,0,1:T(8,128)S(1)} fusion(f32[2,10,96,384]{3,2,0,1:T(8,128)} %fusion.58, f32[2,10,96,384]{3,2,0,1:T(8,128)S(1)} %broadcast.816, f32[10,96,384]{2,1,0:T(8,128)} %copy.121, f32[10,96,384]{2,1,0:T(8,128)} %copy.119, f32[10,96,384]{2,1,0:T(8,128)} %copy.114), kind=kLoop, calls=%fused_computation.10 | loop fusion | flops 4423680 | bytes 13271040 | tf_op jit(solution)/shard_map/add | solution.py:58
  138.9 6.3 %collective-permute-start.4 = (f32[2,10,1,384]{3,2,0,1:T(1,128)S(1)}, f32[2,10,1,384]{3,2,0,1:T(1,128)S(1)}, u32[]{:S(2)}, u32[]{:S(2)}) collective-permute-start(f32[2,10,1,384]{3,2,0,1:T(1,128)S(1)} %get-tuple-element.81), channel_id=1, source_target_pairs={{0,4},{4,8},{8,12},{12,16},{16,20},{20,24},{24,28},{1,5},{5,9},{9,... | collective-permute-start | bytes 92168 | tf_op jit(solution)/shard_map/ppermute | solution.py:18
  145.2 1.9 collective-permute-start.5
  147.2 3.3 %collective-permute-done.5 = f32[2,10,1,384]{3,2,0,1:T(1,128)S(1)} collective-permute-done((f32[2,10,1,384]{3,2,0,1:T(1,128)S(1)}, f32[2,10,1,384]{3,2,0,1:T(1,128)S(1)}, u32[]{:S(2)}, u32[]{:S(2)}) %collective-permute-start.5) | collective-permute-done | bytes 30752 | tf_op jit(solution)/shard_map/ppermute | solution.py:21
  150.4 1.8 pad_maximum_fusion.29
  153.8 3.3 %collective-permute-start.6 = (f32[2,10,98,1]{2,0,3,1:T(2,128)S(1)}, f32[2,10,98,1]{2,0,3,1:T(2,128)}, u32[]{:S(2)}, u32[]{:S(2)}) collective-permute-start(f32[2,10,98,1]{2,0,3,1:T(2,128)S(1)} %copy.153), channel_id=1, source_target_pairs={{0,1},{1,2},{2,3},{4,5},{5,6},{6,7},{8,9},{9,10},{10,11},{12,13},{... | collective-permute-start | bytes 23528 | tf_op jit(solution)/shard_map/ppermute | solution.py:18
  157.1 2.2 copy.155
  160.7 3.4 %fusion.20 = f32[2,10,96,384]{3,2,0,1:T(8,128)} fusion(f32[2,10,96,384]{3,2,0,1:T(8,128)S(1)} %multiply_select_fusion.2, f32[2,10,1,384]{3,2,0,1:T(1,128)} %copy-done.88, f32[10,96,384]{2,1,0:T(8,128)} %copy.98), kind=kLoop, calls=%fused_computation.42 | loop fusion | flops 1474560 | bytes 7403520 | tf_op jit(solution)/shard_map/mul | solution.py:55
  165.8 2.2 copy.154
  168.0 2.1 copy.156
  170.3 5.8 %fusion.15 = f32[2,10,96,384]{3,2,0,1:T(8,128)S(1)} fusion(f32[2,10,98,1]{3,2,0,1:T(8,128)} %copy.156, f32[2,10,1,384]{3,2,0,1:T(1,128)} %copy-done.91, f32[2,10,96,384]{3,2,0,1:T(8,128)S(1)} %multiply_select_fusion.2, f32[2,10,1,384]{3,2,0,1:T(1,128)} %copy-done.88, f32[2,10,98,1]{3,2,0,1:T(8,128)} %copy.154, f32[2,10,96,384]{3,2,0,1:T(8,128)} %fusion.48, ...), kind=kLoop, calls=%fused_computation.30 | loop fusion | flops 9584640 | bytes 13348160 | tf_op jit(solution)/shard_map/add | solution.py:58
  180.2 2.2 collective-permute-start.8
  182.4 2.7 %collective-permute-start.9 = (f32[2,10,1,384]{3,2,0,1:T(1,128)}, f32[2,10,1,384]{3,2,0,1:T(1,128)}, u32[]{:S(2)}, u32[]{:S(2)}) collective-permute-start(f32[2,10,1,384]{3,2,0,1:T(1,128)} %get-tuple-element.80), channel_id=1, source_target_pairs={{4,0},{8,4},{12,8},{16,12},{20,16},{24,20},{28,24},{5,1},{9,5},{13... | collective-permute-start | bytes 92168 | tf_op jit(solution)/shard_map/ppermute | solution.py:21
  185.2 3.2 %collective-permute-done.9 = f32[2,10,1,384]{3,2,0,1:T(1,128)} collective-permute-done((f32[2,10,1,384]{3,2,0,1:T(1,128)}, f32[2,10,1,384]{3,2,0,1:T(1,128)}, u32[]{:S(2)}, u32[]{:S(2)}) %collective-permute-start.9) | collective-permute-done | bytes 30752 | tf_op jit(solution)/shard_map/ppermute | solution.py:21
  188.3 2.5 %pad_maximum_fusion.26 = (f32[2,10,98,1]{3,2,0,1:T(8,128)}, f32[2,10,98,1]{3,2,0,1:T(8,128)}) fusion(f32[2,10,1,384]{3,2,0,1:T(1,128)} %collective-permute-done.9, f32[2,10,96,384]{3,2,0,1:T(8,128)S(1)} %multiply_select_fusion.1, f32[2,10,1,384]{3,2,0,1:T(1,128)} %collective-permute-done.8), kind=kLoop, calls=%fused_computation.66 | loop fusion | flops 7840 | bytes 3026240 | tf_op jit(solution)/shard_map/slice | solution.py:19
  192.4 4.6 %collective-permute-start.10 = (f32[2,10,98,1]{2,0,3,1:T(2,128)S(1)}, f32[2,10,98,1]{2,0,3,1:T(2,128)}, u32[]{:S(2)}, u32[]{:S(2)}) collective-permute-start(f32[2,10,98,1]{2,0,3,1:T(2,128)S(1)} %copy.157), channel_id=1, source_target_pairs={{0,1},{1,2},{2,3},{4,5},{5,6},{6,7},{8,9},{9,10},{10,11},{12,13},{... | collective-permute-start | bytes 23528 | tf_op jit(solution)/shard_map/ppermute | solution.py:18
  197.0 2.2 copy.159
  200.8 3.4 %fusion.13 = f32[2,10,96,384]{3,2,0,1:T(8,128)} fusion(f32[2,10,96,384]{3,2,0,1:T(8,128)S(1)} %multiply_select_fusion.1, f32[2,10,1,384]{3,2,0,1:T(1,128)} %collective-permute-done.8, f32[10,96,384]{2,1,0:T(8,128)} %copy.98), kind=kLoop, calls=%fused_computation.27 | loop fusion | flops 1474560 | bytes 7403520 | tf_op jit(solution)/shard_map/mul | solution.py:55
  205.9 2.1 copy.158
  208.0 2.1 copy.160
  210.4 5.8 %fusion.8 = f32[2,10,96,384]{3,2,0,1:T(8,128)S(1)} fusion(f32[2,10,98,1]{3,2,0,1:T(8,128)} %copy.160, f32[2,10,1,384]{3,2,0,1:T(1,128)} %collective-permute-done.9, f32[2,10,96,384]{3,2,0,1:T(8,128)S(1)} %multiply_select_fusion.1, f32[2,10,1,384]{3,2,0,1:T(1,128)} %collective-permute-done.8, f32[2,10,98,1]{3,2,0,1:T(8,128)} %copy.158, ...), kind=kLoop, calls=%fused_computation.15 | loop fusion | flops 9584640 | bytes 13348160 | tf_op jit(solution)/shard_map/add | solution.py:58
  218.0 1.8 copy.163
  (294 shorter events, 62.7 us)
Async XLA Ops:
  0.6 15.2 %copy-start.89 = (f32[1,1,8,4,4,3,128]{6,4,5,3,2,1,0:T(4,128)S(1)}, f32[1,1,8,4,4,3,128]{6,4,5,3,2,1,0:T(4,128)}, u32[]{:S(2)}) copy-start(f32[1,1,8,4,4,3,128]{6,4,5,3,2,1,0:T(4,128)} %param.13) | copy-start | bytes 589828
  0.6 15.3 %copy-start.92 = (s32[1,1,8,4]{2,3,1,0:T(4,128)S(1)}, s32[1,1,8,4]{2,3,1,0:T(4,128)}, u32[]{:S(2)}) copy-start(s32[1,1,8,4]{2,3,1,0:T(4,128)} %param.15) | copy-start | bytes 388
  0.6 15.5 %slice-start = ((f32[2,10,96,384]{3,2,1,0:T(8,128)}), f32[2,1,96,384]{3,2,1,0:T(8,128)S(1)}, s32[]{:S(2)}) async-start(f32[2,10,96,384]{3,2,1,0:T(8,128)} %param.9), calls=%async_computation.4 | async-start | bytes 589824 | tf_op jit(solution)/shard_map/slice | solution.py:110
  2.3 41.6 %collective-permute-start.1 = (f32[10,1,384]{2,1,0:T(1,128)}, f32[10,1,384]{2,1,0:T(1,128)}, u32[]{:S(2)}, u32[]{:S(2)}) collective-permute-start(f32[10,1,384]{2,1,0:T(1,128)} %get-tuple-element.93), channel_id=1, source_target_pairs={{4,0},{8,4},{12,8},{16,12},{20,16},{24,20},{28,24},{5,1},{9,5},{13... | collective-permute-start | bytes 46088 | tf_op jit(solution)/shard_map/ppermute | solution.py:21
  4.3 42.2 %collective-permute-start = (f32[10,1,384]{2,1,0:T(1,128)}, f32[10,1,384]{2,1,0:T(1,128)}, u32[]{:S(2)}, u32[]{:S(2)}) collective-permute-start(f32[10,1,384]{2,1,0:T(1,128)} %get-tuple-element.92), channel_id=1, source_target_pairs={{0,4},{4,8},{8,12},{12,16},{16,20},{20,24},{24,28},{1,5},{5,9},{9,... | collective-permute-start | bytes 46088 | tf_op jit(solution)/shard_map/ppermute | solution.py:18
  10.1 17.5 %all-to-all-start = ((s32[1,1,8,4,4]{4,3,1,0,2:T(4,128)}), s32[1,1,8,4,4]{4,3,1,0,2:T(4,128)}, u32[]{:S(2)}, u32[]{:S(2)}) async-start(s32[1,1,8,4,4]{4,3,1,0,2:T(4,128)} %copy.99), calls=%async_computation | async-start | bytes 32768 | tf_op jit(solution)/shard_map/all_to_all | solution.py:101
  29.0 9.0 %all-to-all-start.1 = ((s32[8,1,1,4,4]{0,4,2,1,3:T(4,128)}), s32[8,1,1,4,4]{0,4,2,1,3:T(4,128)S(1)}, u32[]{:S(2)}, u32[]{:S(2)}) async-start(s32[8,1,1,4,4]{0,4,2,1,3:T(4,128)} %copy.101), calls=%async_computation.1 | async-start | bytes 16384 | tf_op jit(solution)/shard_map/all_to_all | solution.py:100
  38.1 61.4 %all-to-all-start.2 = ((f32[1,1,8,4,4,3,128]{6,4,5,3,1,0,2:T(4,128)}), f32[1,1,8,4,4,3,128]{6,4,5,3,1,0,2:T(4,128)S(1)}, u32[]{:S(2)}, u32[]{:S(2)}) async-start(f32[1,1,8,4,4,3,128]{6,4,5,3,1,0,2:T(4,128)} %pad_maximum_fusion.30), calls=%async_computation.2 | async-start | bytes 393216 | tf_op jit(solution)/shard_map/all_to_all | solution.py:94
  50.0 5.9 %collective-permute-start.2 = (f32[10,98,1]{1,2,0:T(1,128)S(1)}, f32[10,98,1]{1,2,0:T(1,128)S(1)}, u32[]{:S(2)}, u32[]{:S(2)}) collective-permute-start(f32[10,98,1]{1,2,0:T(1,128)S(1)} %get-tuple-element.74), channel_id=1, source_target_pairs={{0,1},{1,2},{2,3},{4,5},{5,6},{6,7},{8,9},{9,10},{10,11},{12,13},{... | collective-permute-start | bytes 11768 | tf_op jit(solution)/shard_map/ppermute | solution.py:18
  52.3 4.4 %collective-permute-start.3 = (f32[10,98,1]{1,2,0:T(1,128)S(1)}, f32[10,98,1]{1,2,0:T(1,128)S(1)}, u32[]{:S(2)}, u32[]{:S(2)}) collective-permute-start(f32[10,98,1]{1,2,0:T(1,128)S(1)} %get-tuple-element.73), channel_id=1, source_target_pairs={{1,0},{2,1},{3,2},{5,4},{6,5},{7,6},{9,8},{10,9},{11,10},{13,12},{... | collective-permute-start | bytes 11768 | tf_op jit(solution)/shard_map/ppermute | solution.py:21
  56.0 11.3 %copy-start = (f32[9,96,384]{1,2,0:T(8,128)S(1)}, f32[9,96,384]{1,2,0:T(8,128)}, u32[]{:S(2)}) copy-start(f32[9,96,384]{1,2,0:T(8,128)} %slice_add_fusion) | copy-start | bytes 3981316
  56.0 11.3 %copy-start.80 = (f32[96,384]{0,1:T(8,128)S(1)}, f32[96,384]{0,1:T(8,128)}, u32[]{:S(2)}) copy-start(f32[96,384]{0,1:T(8,128)} %copy.122) | copy-start | bytes 442372
  79.0 12.6 %copy-start.87 = (f32[96,384]{0,1:T(8,128)S(1)}, f32[96,384]{0,1:T(8,128)}, u32[]{:S(2)}) copy-start(f32[96,384]{0,1:T(8,128)} %get-tuple-element.63) | copy-start | bytes 442372
  79.0 13.4 %copy-start.86 = (f32[96,384]{0,1:T(8,128)S(1)}, f32[96,384]{0,1:T(8,128)}, u32[]{:S(2)}) copy-start(f32[96,384]{0,1:T(8,128)} %get-tuple-element.61) | copy-start | bytes 442372
  79.0 14.2 %copy-start.85 = (f32[96,384]{0,1:T(8,128)S(1)}, f32[96,384]{0,1:T(8,128)}, u32[]{:S(2)}) copy-start(f32[96,384]{0,1:T(8,128)} %get-tuple-element.60) | copy-start | bytes 442372
  79.0 15.0 %copy-start.84 = (f32[96,384]{0,1:T(8,128)S(1)}, f32[96,384]{0,1:T(8,128)}, u32[]{:S(2)}) copy-start(f32[96,384]{0,1:T(8,128)} %get-tuple-element.59) | copy-start | bytes 442372
  79.0 15.8 %copy-start.83 = (f32[96,384]{0,1:T(8,128)S(1)}, f32[96,384]{0,1:T(8,128)}, u32[]{:S(2)}) copy-start(f32[96,384]{0,1:T(8,128)} %get-tuple-element.57) | copy-start | bytes 442372
  79.0 16.5 %copy-start.82 = (f32[96,384]{0,1:T(8,128)S(1)}, f32[96,384]{0,1:T(8,128)}, u32[]{:S(2)}) copy-start(f32[96,384]{0,1:T(8,128)} %get-tuple-element.56) | copy-start | bytes 442372
  79.0 17.3 %copy-start.81 = (f32[96,384]{0,1:T(8,128)S(1)}, f32[96,384]{0,1:T(8,128)}, u32[]{:S(2)}) copy-start(f32[96,384]{0,1:T(8,128)} %get-tuple-element.55) | copy-start | bytes 442372
  100.2 9.4 %all-to-all-start.3 = ((f32[8,1,1,4,4,3,128]{6,4,5,0,2,1,3:T(4,128)}), f32[8,1,1,4,4,3,128]{6,4,5,0,2,1,3:T(4,128)}, u32[]{:S(2)}, u32[]{:S(2)}) async-start(f32[8,1,1,4,4,3,128]{6,4,5,0,2,1,3:T(4,128)} %copy.106), calls=%async_computation.3 | async-start | bytes 393216 | tf_op jit(solution)/shard_map/all_to_all | solution.py:93
  138.9 8.2 %collective-permute-start.4 = (f32[2,10,1,384]{3,2,0,1:T(1,128)S(1)}, f32[2,10,1,384]{3,2,0,1:T(1,128)S(1)}, u32[]{:S(2)}, u32[]{:S(2)}) collective-permute-start(f32[2,10,1,384]{3,2,0,1:T(1,128)S(1)} %get-tuple-element.81), channel_id=1, source_target_pairs={{0,4},{4,8},{8,12},{12,16},{16,20},{20,24},{24,28},{1,5},{5,9},{9,... | collective-permute-start | bytes 92168 | tf_op jit(solution)/shard_map/ppermute | solution.py:18
  145.2 5.2 %collective-permute-start.5 = (f32[2,10,1,384]{3,2,0,1:T(1,128)S(1)}, f32[2,10,1,384]{3,2,0,1:T(1,128)S(1)}, u32[]{:S(2)}, u32[]{:S(2)}) collective-permute-start(f32[2,10,1,384]{3,2,0,1:T(1,128)S(1)} %get-tuple-element.82), channel_id=1, source_target_pairs={{4,0},{8,4},{12,8},{16,12},{20,16},{24,20},{28,24},{5,1},{9,5},{13... | collective-permute-start | bytes 92168 | tf_op jit(solution)/shard_map/ppermute | solution.py:21
  153.8 12.0 %collective-permute-start.6 = (f32[2,10,98,1]{2,0,3,1:T(2,128)S(1)}, f32[2,10,98,1]{2,0,3,1:T(2,128)}, u32[]{:S(2)}, u32[]{:S(2)}) collective-permute-start(f32[2,10,98,1]{2,0,3,1:T(2,128)S(1)} %copy.153), channel_id=1, source_target_pairs={{0,1},{1,2},{2,3},{4,5},{5,6},{6,7},{8,9},{9,10},{10,11},{12,13},{... | collective-permute-start | bytes 23528 | tf_op jit(solution)/shard_map/ppermute | solution.py:18
  159.3 8.7 %collective-permute-start.7 = (f32[2,10,98,1]{2,0,3,1:T(2,128)}, f32[2,10,98,1]{2,0,3,1:T(2,128)}, u32[]{:S(2)}, u32[]{:S(2)}) collective-permute-start(f32[2,10,98,1]{2,0,3,1:T(2,128)} %copy.155), channel_id=1, source_target_pairs={{1,0},{2,1},{3,2},{5,4},{6,5},{7,6},{9,8},{10,9},{11,10},{13,12},{... | collective-permute-start | bytes 23528 | tf_op jit(solution)/shard_map/ppermute | solution.py:21
  170.1 6.0 %copy-start.20 = (f32[96,384]{1,0:T(8,128)S(1)}, f32[96,384]{1,0:T(8,128)}, u32[]{:S(2)}) copy-start(f32[96,384]{1,0:T(8,128)} %copy.133) | copy-start | bytes 442372
  170.1 6.0 %copy-start.23 = (f32[96,384]{1,0:T(8,128)S(1)}, f32[96,384]{1,0:T(8,128)}, u32[]{:S(2)}) copy-start(f32[96,384]{1,0:T(8,128)} %copy.136) | copy-start | bytes 442372
  170.1 6.0 %copy-start.26 = (f32[96,384]{1,0:T(8,128)S(1)}, f32[96,384]{1,0:T(8,128)}, u32[]{:S(2)}) copy-start(f32[96,384]{1,0:T(8,128)} %copy.139) | copy-start | bytes 442372
  170.1 6.0 %copy-start.29 = (f32[96,384]{1,0:T(8,128)S(1)}, f32[96,384]{1,0:T(8,128)}, u32[]{:S(2)}) copy-start(f32[96,384]{1,0:T(8,128)} %copy.142) | copy-start | bytes 442372
  170.1 6.0 %copy-start.32 = (f32[96,384]{1,0:T(8,128)S(1)}, f32[96,384]{1,0:T(8,128)}, u32[]{:S(2)}) copy-start(f32[96,384]{1,0:T(8,128)} %copy.145) | copy-start | bytes 442372
  170.1 6.0 %copy-start.35 = (f32[96,384]{1,0:T(8,128)S(1)}, f32[96,384]{1,0:T(8,128)}, u32[]{:S(2)}) copy-start(f32[96,384]{1,0:T(8,128)} %copy.148) | copy-start | bytes 442372
  170.1 6.0 %copy-start.38 = (f32[96,384]{1,0:T(8,128)S(1)}, f32[96,384]{1,0:T(8,128)}, u32[]{:S(2)}) copy-start(f32[96,384]{1,0:T(8,128)} %copy.125) | copy-start | bytes 442372
  170.1 6.0 %copy-start.41 = (f32[96,384]{1,0:T(8,128)S(1)}, f32[96,384]{1,0:T(8,128)}, u32[]{:S(2)}) copy-start(f32[96,384]{1,0:T(8,128)} %copy.126) | copy-start | bytes 442372
  170.1 6.0 %copy-start.44 = (f32[96,384]{1,0:T(8,128)S(1)}, f32[96,384]{1,0:T(8,128)}, u32[]{:S(2)}) copy-start(f32[96,384]{1,0:T(8,128)} %copy.128) | copy-start | bytes 442372
  170.2 6.0 %copy-start.47 = (f32[96,384]{1,0:T(8,128)S(1)}, f32[96,384]{1,0:T(8,128)}, u32[]{:S(2)}) copy-start(f32[96,384]{1,0:T(8,128)} %copy.129) | copy-start | bytes 442372
  170.2 6.0 %copy-start.50 = (f32[96,384]{1,0:T(8,128)S(1)}, f32[96,384]{1,0:T(8,128)}, u32[]{:S(2)}) copy-start(f32[96,384]{1,0:T(8,128)} %copy.131) | copy-start | bytes 442372
  170.2 6.0 %copy-start.53 = (f32[96,384]{1,0:T(8,128)S(1)}, f32[96,384]{1,0:T(8,128)}, u32[]{:S(2)}) copy-start(f32[96,384]{1,0:T(8,128)} %copy.134) | copy-start | bytes 442372
  180.2 4.9 %collective-permute-start.8 = (f32[2,10,1,384]{3,2,0,1:T(1,128)}, f32[2,10,1,384]{3,2,0,1:T(1,128)}, u32[]{:S(2)}, u32[]{:S(2)}) collective-permute-start(f32[2,10,1,384]{3,2,0,1:T(1,128)} %get-tuple-element.79), channel_id=1, source_target_pairs={{0,4},{4,8},{8,12},{12,16},{16,20},{20,24},{24,28},{1,5},{5,9},{9,... | collective-permute-start | bytes 92168 | tf_op jit(solution)/shard_map/ppermute | solution.py:18
  182.4 5.9 %collective-permute-start.9 = (f32[2,10,1,384]{3,2,0,1:T(1,128)}, f32[2,10,1,384]{3,2,0,1:T(1,128)}, u32[]{:S(2)}, u32[]{:S(2)}) collective-permute-start(f32[2,10,1,384]{3,2,0,1:T(1,128)} %get-tuple-element.80), channel_id=1, source_target_pairs={{4,0},{8,4},{12,8},{16,12},{20,16},{24,20},{28,24},{5,1},{9,5},{13... | collective-permute-start | bytes 92168 | tf_op jit(solution)/shard_map/ppermute | solution.py:21
  192.4 13.5 %collective-permute-start.10 = (f32[2,10,98,1]{2,0,3,1:T(2,128)S(1)}, f32[2,10,98,1]{2,0,3,1:T(2,128)}, u32[]{:S(2)}, u32[]{:S(2)}) collective-permute-start(f32[2,10,98,1]{2,0,3,1:T(2,128)S(1)} %copy.157), channel_id=1, source_target_pairs={{0,1},{1,2},{2,3},{4,5},{5,6},{6,7},{8,9},{9,10},{10,11},{12,13},{... | collective-permute-start | bytes 23528 | tf_op jit(solution)/shard_map/ppermute | solution.py:18
  199.2 8.8 %collective-permute-start.11 = (f32[2,10,98,1]{2,0,3,1:T(2,128)}, f32[2,10,98,1]{2,0,3,1:T(2,128)}, u32[]{:S(2)}, u32[]{:S(2)}) collective-permute-start(f32[2,10,98,1]{2,0,3,1:T(2,128)} %copy.159), channel_id=1, source_target_pairs={{1,0},{2,1},{3,2},{5,4},{6,5},{7,6},{9,8},{10,9},{11,10},{13,12},{... | collective-permute-start | bytes 23528 | tf_op jit(solution)/shard_map/ppermute | solution.py:21
  210.1 6.0 %copy-start.21 = (f32[96,384]{1,0:T(8,128)S(1)}, f32[96,384]{1,0:T(8,128)}, u32[]{:S(2)}) copy-start(f32[96,384]{1,0:T(8,128)} %copy.133) | copy-start | bytes 442372
  210.2 6.0 %copy-start.24 = (f32[96,384]{1,0:T(8,128)S(1)}, f32[96,384]{1,0:T(8,128)}, u32[]{:S(2)}) copy-start(f32[96,384]{1,0:T(8,128)} %copy.136) | copy-start | bytes 442372
  210.2 6.0 %copy-start.27 = (f32[96,384]{1,0:T(8,128)S(1)}, f32[96,384]{1,0:T(8,128)}, u32[]{:S(2)}) copy-start(f32[96,384]{1,0:T(8,128)} %copy.139) | copy-start | bytes 442372
  210.2 6.0 %copy-start.30 = (f32[96,384]{1,0:T(8,128)S(1)}, f32[96,384]{1,0:T(8,128)}, u32[]{:S(2)}) copy-start(f32[96,384]{1,0:T(8,128)} %copy.142) | copy-start | bytes 442372
  210.2 6.0 %copy-start.33 = (f32[96,384]{1,0:T(8,128)S(1)}, f32[96,384]{1,0:T(8,128)}, u32[]{:S(2)}) copy-start(f32[96,384]{1,0:T(8,128)} %copy.145) | copy-start | bytes 442372
  210.2 6.0 %copy-start.36 = (f32[96,384]{1,0:T(8,128)S(1)}, f32[96,384]{1,0:T(8,128)}, u32[]{:S(2)}) copy-start(f32[96,384]{1,0:T(8,128)} %copy.148) | copy-start | bytes 442372
  210.2 6.0 %copy-start.39 = (f32[96,384]{1,0:T(8,128)S(1)}, f32[96,384]{1,0:T(8,128)}, u32[]{:S(2)}) copy-start(f32[96,384]{1,0:T(8,128)} %copy.125) | copy-start | bytes 442372
  210.2 6.0 %copy-start.42 = (f32[96,384]{1,0:T(8,128)S(1)}, f32[96,384]{1,0:T(8,128)}, u32[]{:S(2)}) copy-start(f32[96,384]{1,0:T(8,128)} %copy.126) | copy-start | bytes 442372
  (62 other events, 309.5 us)
where the time goes:
time: 226 us; the launch traced here: 222 us
  local copies, waits for them, and re-layouts  86.2 us (38%)
  other arithmetic  70.8 us (31%)
  starting transfers between devices  52.2 us (23%)
  waiting for transfers between devices  9.41 us (4%)
  between operations  2.96 us (1%)
    ppermute x6, starting transfers between devices, padded_2(): lax.ppermute(lax.slice_in_dim(block, block.shape[dim] - width, None, axis...  23.1 us
    add x3, other arithmetic, relax(): driven + south_face * padded_adj[..., 1:-1, :-2]  15.9 us
    scatter-add x1, other arithmetic, per_device(): jnp.zeros(surface.shape, jnp.float32).at[:, cells_flat].add(contrib)  13.2 us
    unnamed x202, local copies, waits for them, and re-layouts  11.3 us
    ppermute x6, starting transfers between devices, padded_2(): lax.ppermute(lax.slice_in_dim(block, 0, width, axis=dim), axis, backward)  10.9 us
    add x1, other arithmetic, column_factors(): diagonal = west_face + east_face + south_face + north_face  10.6 us
    squeeze x10, local copies, waits for them, and re-layouts, column_factors(): entry = entry + upper_face[level]  10.6 us
    div x9, local copies, waits for them, and re-layouts, column_factors(): ratios.append(-upper_face[level] / entry)  10.4 us
  transfers between devices with their start and end apart: 16, of which 5 were waited for; matrix products, arithmetic and copies ran while one was open for 42% of the time, Pallas kernels for 0%

commit v1 on v0

v1 whole, which is shorter than its diff:
```python
import functools

import jax
import jax.numpy as jnp
from jax import lax
from jax.experimental import pallas as pl
from jax.experimental.pallas import tpu as pltpu
from jax.sharding import PartitionSpec as P

VERTICAL_GAIN = 2.0
RELAX_WEIGHT = 0.8

TOP = 16
FACES = 6


def lanes_of(shape):
    return lax.broadcasted_iota(jnp.int32, shape, len(shape) - 1)


def three_parts(value):
    high = value.astype(jnp.bfloat16)
    rest = value - high.astype(jnp.float32)
    middle = rest.astype(jnp.bfloat16)
    low = (rest - middle.astype(jnp.float32)).astype(jnp.bfloat16)
    return jnp.concatenate([high, middle, low], axis=-1)


def sum_parts(value):
    width = value.shape[-1] // 3
    return value[:, :width] + value[:, width : 2 * width] + value[:, 2 * width :]


def pick(onehot, value):
    return sum_parts(jnp.dot(onehot, three_parts(value), preferred_element_type=jnp.float32))


def spread(onehot, value):
    dims = (((0,), (0,)), ((), ()))
    return sum_parts(
        lax.dot_general(onehot, three_parts(value), dims, preferred_element_type=jnp.float32)
    )


def pack_kernel(
    owners_x, owners_y, count_ref, ice_ref, tiles_ref, cells_ref, low_ref, high_ref, low_fric, high_fric, out_ref, xlo_ref, xhi_ref
):
    layers = low_ref.shape[0]
    slots, lanes = tiles_ref.shape[2], tiles_ref.shape[3]
    lane = lanes_of((slots, lanes))
    slot = lax.broadcasted_iota(jnp.int32, (slots, lanes), 0)
    icefield = jnp.full((4, low_fric.shape[1]), ice_ref[0, 0], jnp.int32).astype(jnp.float32)
    for k in range(layers):
        xlo_ref[k] = low_ref[k, 0:4]
        xhi_ref[k] = high_ref[k, 4:8]
    xlo_ref[layers] = low_fric[0:4]
    xhi_ref[layers] = high_fric[4:8]
    xlo_ref[layers + 1] = icefield
    xhi_ref[layers + 1] = icefield
    zero = jnp.zeros((slots, lanes), jnp.float32)
    for ox in range(owners_x):
        firsts, lasts, owns = [], [], []
        for oy in range(owners_y):
            owner = ox * owners_y + oy
            u = tiles_ref[owner, 0]
            v = tiles_ref[owner, 1]
            w = jnp.where(slot < count_ref[ox, oy], tiles_ref[owner, 2], 0.0)
            cell = jnp.broadcast_to(cells_ref[oy, :, ox : ox + 1], (slots, lanes)).astype(jnp.float32)
            out_ref[owner, 0:slots] = u
            out_ref[owner, slots : 2 * slots] = v
            out_ref[owner, 2 * slots : 3 * slots] = w
            first = jnp.where(lane < 4, pltpu.roll(v, 2, 1), jnp.where(lane < 6, pltpu.roll(w, 4, 1), cell))
            firsts.append(jnp.where(lane < 2, u, first))
            last = jnp.where(
                lane >= lanes - 4,
                pltpu.roll(v, lanes - 2, 1),
                jnp.where(lane >= lanes - 6, pltpu.roll(w, lanes - 4, 1), cell),
            )
            lasts.append(jnp.where(lane >= lanes - 2, u, last))
            owns.append(cell)
        for oy in range(owners_y):
            after = firsts[oy + 1] if oy + 1 < owners_y else zero
            before = lasts[oy - 1] if oy > 0 else zero
            meta = jnp.where(lane < 16, after, jnp.where(lane >= lanes - 16, before, owns[oy]))
            out_ref[ox * owners_y + oy, 3 * slots : 4 * slots] = meta


def columns_kernel(
    ice_ref, visc_first, visc_last, fric_first, fric_last, vel_first, vel_last, before_ref, after_ref, first_ref, last_ref
):
    layers, rows, lanes = visc_first.shape
    lane = lanes_of((rows, lanes))
    lane_4 = lanes_of((4, lanes))
    icefield = jnp.full((rows, lanes), ice_ref[0, 0], jnp.int32).astype(jnp.float32)
    cols = before_ref.shape[2]
    first_ref[...] = jnp.zeros(first_ref.shape, jnp.float32)
    last_ref[...] = jnp.zeros(last_ref.shape, jnp.float32)
    first = jnp.zeros((rows, lanes), jnp.float32)
    last = jnp.zeros((rows, lanes), jnp.float32)
    edges = [jnp.zeros((4, lanes), jnp.float32) for _ in range(4)]
    for k in range(layers + 4):
        if k < layers:
            mine = (visc_first[k], visc_last[k])
        elif k == layers:
            mine = (fric_first[...], fric_last[...])
        elif k == layers + 1:
            mine = (icefield, icefield)
        else:
            mine = (vel_first[k - layers - 2, 0], vel_last[k - layers - 2, 0])
        here = (lane >= 3 * k) & (lane < 3 * k + 3)
        first = jnp.where(here, pltpu.roll(mine[0], 3 * k, 1), first)
        there = (lane >= lanes - 3 - 3 * k) & (lane < lanes - 3 * k)
        last = jnp.where(there, pltpu.roll(mine[1], (lanes - 3 * k) % lanes, 1), last)
        if k < layers + 2:
            here_4 = (lane_4 >= 3 * k) & (lane_4 < 3 * k + 3)
            there_4 = (lane_4 >= lanes - 3 - 3 * k) & (lane_4 < lanes - 3 * k)
            for n, ref in enumerate((before_ref, after_ref)):
                edges[n] = jnp.where(here_4, pltpu.roll(ref[k, :, 0:lanes], 3 * k, 1), edges[n])
                edges[n + 2] = jnp.where(
                    there_4, pltpu.roll(ref[k, :, cols - lanes : cols], (lanes - 3 * k) % lanes, 1), edges[n + 2]
                )
    first_ref[TOP : TOP + rows] = first
    last_ref[TOP : TOP + rows] = last
    first_ref[TOP - 4 : TOP] = edges[0]
    first_ref[TOP + rows : TOP + rows + 4] = edges[1]
    last_ref[TOP - 4 : TOP] = edges[2]
    last_ref[TOP + rows : TOP + rows + 4] = edges[3]


def side_tile(before, after, k):
    lanes = before.shape[-1]
    lane = lanes_of(before.shape)
    left = pltpu.roll(before, (3 * k) % lanes, 1)
    right = pltpu.roll(after, (lanes - 3 * k) % lanes, 1)
    return jnp.where(lane < 3, right, jnp.where(lane >= lanes - 3, left, 0.0))


def ring_pair(load, tile, tiles):
    here = load(tile)
    lanes = here.shape[-1]
    lane = lanes_of(here.shape)
    before = pltpu.roll(jnp.where(lane == lanes - 1, load((tile - 1) % tiles), here), 1, 1)
    after = pltpu.roll(jnp.where(lane == 0, load((tile + 1) % tiles), here), lanes - 1, 1)
    return here, before, after


def factors_kernel(
    ice_ref, visc_ref, fric_ref, xbefore_ref, xafter_ref, ybefore_ref, yafter_ref, coef_ref, field
):
    layers, rows, cols = visc_ref.shape
    tiles = field.shape[1]
    lanes = field.shape[3]
    high = rows + TOP
    icefield = jnp.full((rows, lanes), ice_ref[0, 0], jnp.int32).astype(jnp.float32)
    edge = jnp.zeros((TOP, lanes), jnp.float32)
    for k in range(layers + 2):
        for t in range(tiles - 1):
            span = slice(t * lanes, (t + 1) * lanes)
            field[k, t, 0:TOP] = edge
            field[k, t, high : high + TOP] = edge
            field[k, t, TOP - 4 : TOP] = xbefore_ref[k, :, span]
            field[k, t, high : high + 4] = xafter_ref[k, :, span]
            if k < layers:
                field[k, t, TOP:high] = visc_ref[k, :, span]
            elif k == layers:
                field[k, t, TOP:high] = fric_ref[:, span]
            else:
                field[k, t, TOP:high] = icefield
        field[k, tiles - 1] = side_tile(ybefore_ref[...], yafter_ref[...], k)

    def chunk(c, carry):
        row = 8 + 8 * c
        for t in range(tiles):
            gain = (0.5 * RELAX_WEIGHT) * field[layers + 1, t, pl.ds(row, 8)]
            up = None
            ratio = None
            for k in range(layers):
                here, south, north = ring_pair(lambda s: field[k, s, pl.ds(row, 8)], t, tiles)
                west = here + field[k, t, pl.ds(row - 1, 8)]
                east = here + field[k, t, pl.ds(row + 1, 8)]
                south = here + south
                north = here + north
                entry = 0.5 * (west + east + south + north)
                if k == 0:
                    entry = entry + field[layers, t, pl.ds(row, 8)]
                if k > 0:
                    entry = entry + (up - up * ratio)
                if k < layers - 1:
                    above = (0.5 * VERTICAL_GAIN) * (here + field[k + 1, t, pl.ds(row, 8)])
                    entry = entry + above
                inverse = jnp.where(entry > 0.0, 1.0 / entry, 0.0)
                scale = gain * inverse
                coef_ref[c, t, 0, k] = west * scale
                coef_ref[c, t, 1, k] = east * scale
                coef_ref[c, t, 2, k] = south * scale
                coef_ref[c, t, 3, k] = north * scale
                if k > 0:
                    coef_ref[c, t, 4, k] = up * inverse
                if k < layers - 1:
                    up = above
                    ratio = up * inverse
                    coef_ref[c, t, 5, k] = ratio
                else:
                    coef_ref[c, t, 4, 0] = 2.0 * scale
                    coef_ref[c, t, 5, k] = scale
        return carry

    lax.fori_loop(0, coef_ref.shape[0], chunk, 0)


def sources_kernel(slots, layers, tiles_ref, vel_ref, ybefore_ref, yafter_ref, rhs_ref, low_ref, high_ref):
    rows, cols = vel_ref.shape[2], vel_ref.shape[3]
    lanes = tiles_ref.shape[1]
    owners = tiles_ref.shape[0] // (4 * slots)
    blocks = cols // lanes

    def channel(c):
        return jnp.concatenate(
            [tiles_ref[pl.ds(c * slots + s, owners, stride=4 * slots), :] for s in range(slots)], axis=0
        )

    seen_u, seen_v, weight, meta = channel(0), channel(1), channel(2), channel(3)
    count = owners * slots
    lane = lanes_of((count, lanes))
    row = lanes_of((count, rows))

    def onehot(column, b):
        cell = jnp.broadcast_to(column.astype(jnp.int32), (count, rows))
        return (cell == row * blocks + b).astype(jnp.bfloat16)

    own = meta[:, lanes // 2 : lanes // 2 + 1]
    marks = jnp.concatenate([onehot(own, b) for b in range(blocks)], axis=1)
    surface = jnp.concatenate(
        [
            jnp.concatenate([vel_ref[c, 0, :, b * lanes : (b + 1) * lanes] for b in range(blocks)], axis=0)
            for c in range(2)
        ],
        axis=1,
    )
    sampled = pick(marks, surface)
    weights = jnp.concatenate([weight, weight], axis=1)
    terms = weights * (sampled - jnp.concatenate([seen_u, seen_v], axis=1))
    top = spread(marks, terms)
    for c in range(2):
        for b in range(blocks):
            plane = top[b * rows : (b + 1) * rows, c * lanes : (c + 1) * lanes]
            rhs_ref[c, b] = plane
            low_ref[c * (blocks + 1) + b] = plane[0:2]
            high_ref[c * (blocks + 1) + b] = plane[rows - 2 : rows]

    beside = jnp.concatenate(
        [
            side_tile(ybefore_ref[TOP : TOP + rows], yafter_ref[TOP : TOP + rows], layers + 2 + c)
            for c in range(2)
        ],
        axis=1,
    )
    mark_after = onehot(meta[:, 8:9], 0)
    mark_before = onehot(meta[:, lanes - 8 : lanes - 7], blocks - 1)
    weight_after = jnp.where(lane < 2, pltpu.roll(meta, lanes - 4, 1), 0.0)
    weight_before = jnp.where(lane >= lanes - 2, pltpu.roll(meta, 4, 1), 0.0)
    after = jnp.concatenate([meta, pltpu.roll(meta, lanes - 2, 1)], axis=1)
    before = jnp.concatenate([meta, pltpu.roll(meta, 2, 1)], axis=1)
    terms_after = jnp.concatenate([weight_after] * 2, axis=1) * (pick(mark_after, beside) - after)
    terms_before = jnp.concatenate([weight_before] * 2, axis=1) * (pick(mark_before, beside) - before)
    side = spread(mark_after, terms_after) + spread(mark_before, terms_before)
    for c in range(2):
        plane = side[:, c * lanes : (c + 1) * lanes]
        rhs_ref[c, blocks] = plane
        low_ref[c * (blocks + 1) + blocks] = plane[0:2]
        high_ref[c * (blocks + 1) + blocks] = plane[rows - 2 : rows]


def sweeps_kernel(
    ice_ref, coef_hbm, rhs_ref, before_ref, after_ref, vel_ref, adj_hbm, grad_ref, coef, rhs, one, two, three, sem_in, sem_out
):
    chunks, tiles, _, layers = coef.shape[:4]
    rows, cols = grad_ref.shape
    lanes = coef.shape[5]
    edge = jnp.zeros((8, lanes), jnp.float32)

    def load_copy(c):
        return pltpu.make_async_copy(coef_hbm.at[c], coef.at[c], sem_in.at[c])

    def store_copy(c):
        span = pl.ds(pl.multiple_of(8 * c, 8), 8)
        return pltpu.make_async_copy(three.at[:, :, span, :], adj_hbm.at[:, :, span, :], sem_out.at[c])

    def begin(c, carry):
        load_copy(c).start()
        return carry

    lax.fori_loop(0, chunks, begin, 0)
    for c in range(2):
        for t in range(tiles):
            rhs[c, t, 8:16] = edge
            rhs[c, t, 16 + rows : 24 + rows] = edge
            rhs[c, t, 14:16] = before_ref[c * tiles + t]
            rhs[c, t, 16 + rows : 18 + rows] = after_ref[c * tiles + t]
            rhs[c, t, 16 : 16 + rows] = rhs_ref[c, t]
            for k in range(layers):
                one[c, k, t, 0:8] = edge
                one[c, k, t, 24 + rows : 32 + rows] = edge
                two[c, k, t, 0:8] = edge
                two[c, k, t, 24 + rows : 32 + rows] = edge

    def first_sweep(c, carry):
        load_copy(c).wait()
        row = 8 + 8 * c
        for t in range(tiles):
            scale = coef[c, t, 4, 0]
            for n in range(2):
                value = rhs[n, t, pl.ds(row, 8)] * scale
                one[n, layers - 1, t, pl.ds(row, 8)] = value
                for k in range(layers - 2, -1, -1):
                    value = coef[c, t, 5, k] * value
                    one[n, k, t, pl.ds(row, 8)] = value
        return carry

    lax.fori_loop(0, chunks, first_sweep, 0)

    def relax(c, t, old, write):
        row = 8 + 8 * c
        centers, forward = [], []
        for n in range(2):
            centers.append([])
            forward.append([])
        for k in range(layers):
            west, east, south, north = (coef[c, t, f, k] for f in range(4))
            for n in range(2):
                here, before, after = ring_pair(lambda s: old[n, k, s, pl.ds(row, 8)], t, tiles)
                value = west * old[n, k, t, pl.ds(row - 1, 8)] + east * old[n, k, t, pl.ds(row + 1, 8)]
                value = value + (south * before + north * after)
                if k > 0:
                    value = value + coef[c, t, 4, k] * forward[n][k - 1]
                if k == layers - 1:
                    value = value + rhs[n, t, pl.ds(row, 8)] * coef[c, t, 4, 0]
                forward[n].append(value)
        for n in range(2):
            value = forward[n][layers - 1]
            for k in range(layers - 1, -1, -1):
                if k < layers - 1:
                    value = forward[n][k] + coef[c, t, 5, k] * value
                write(n, k, (1.0 - RELAX_WEIGHT) * old[n, k, t, pl.ds(row, 8)] + value)

    def second_sweep(c, carry):
        row = 8 + 8 * c
        for t in range(tiles):

            def write(n, k, value):
                two[n, k, t, pl.ds(row, 8)] = value

            relax(c, t, one, write)
        return carry

    lax.fori_loop(0, chunks, second_sweep, 0)
    icefield = jnp.full((8, lanes), ice_ref[0, 0], jnp.int32).astype(jnp.float32)

    def third_sweep(c, carry):
        row = pl.multiple_of(8 * c, 8)
        for t in range(tiles - 1):
            span = slice(t * lanes, (t + 1) * lanes)

            def write(n, k, value):
                three[n, k, pl.ds(row, 8), span] = value

            relax(c + 1, t, two, write)
            product = three[0, 0, pl.ds(row, 8), span] * vel_ref[0, 0, pl.ds(row, 8), span]
            product = product + three[1, 0, pl.ds(row, 8), span] * vel_ref[1, 0, pl.ds(row, 8), span]
            grad_ref[pl.ds(row, 8), span] = -icefield * product
        store_copy(c).start()
        return carry

    lax.fori_loop(0, chunks - 2, third_sweep, 0)

    def finish(c, carry):
        store_copy(c).wait()
        return carry

    lax.fori_loop(0, chunks - 2, finish, 0)


def whole(space=pltpu.VMEM):
    return pl.BlockSpec(memory_space=space)


def per_device(velocity, viscosity, friction, ice_mask, obs_tiles, obs_cell, obs_count):
    layers, rows, cols = viscosity.shape
    owners_x, owners_y, slots, channels, lanes = obs_tiles.shape[2:]
    blocks = cols // lanes
    tiles = blocks + 1
    owners = owners_x * owners_y
    chunks = rows // 8 + 2
    tall = rows + 2 * TOP
    f32 = jnp.float32

    def shift(value, axis, step):
        size = lax.axis_size(axis)
        pairs = [(i, i + step) for i in range(size) if 0 <= i + step < size]
        return lax.ppermute(value, axis, pairs)

    tiles_in = jnp.transpose(obs_tiles.reshape(owners, slots, channels, lanes), (0, 2, 1, 3))
    cells_in = jnp.transpose(obs_cell[0, 0], (1, 2, 0))
    counts_in = obs_count[0, 0]

    def part(shape, index):
        return pl.BlockSpec(shape, lambda i: index)

    side = jax.ShapeDtypeStruct((layers + 2, 4, cols), f32)
    packed, xlow, xhigh = pl.pallas_call(
        functools.partial(pack_kernel, owners_x, owners_y),
        grid=(1,),
        out_shape=(jax.ShapeDtypeStruct((owners, 4 * slots, lanes), f32), side, side),
        in_specs=[
            whole(pltpu.SMEM),
            whole(pltpu.SMEM),
            whole(),
            whole(),
            part((layers, 8, cols), (0, 0, 0)),
            part((layers, 8, cols), (0, rows // 8 - 1, 0)),
            part((8, cols), (0, 0)),
            part((8, cols), (rows // 8 - 1, 0)),
        ],
        out_specs=(whole(), whole(), whole()),
        name="pack",
    )(counts_in, ice_mask, tiles_in, cells_in, viscosity, viscosity, friction, friction)
    arrived = lax.all_to_all(packed, ("gx", "gy"), split_axis=0, concat_axis=0, tiled=True)
    xbefore = shift(xhigh, "gx", 1)
    xafter = shift(xlow, "gx", -1)

    plane = jax.ShapeDtypeStruct((tall, lanes), f32)
    yfirst, ylast = pl.pallas_call(
        columns_kernel,
        grid=(1,),
        out_shape=(plane, plane),
        in_specs=[
            whole(pltpu.SMEM),
            part((layers, rows, lanes), (0, 0, 0)),
            part((layers, rows, lanes), (0, 0, blocks - 1)),
            part((rows, lanes), (0, 0)),
            part((rows, lanes), (0, blocks - 1)),
            part((2, 1, rows, lanes), (0, layers - 1, 0, 0)),
            part((2, 1, rows, lanes), (0, layers - 1, 0, blocks - 1)),
            whole(),
            whole(),
        ],
        out_specs=(whole(), whole()),
        name="columns",
    )(ice_mask, viscosity, viscosity, friction, friction, velocity, velocity, xbefore, xafter)
    ybefore = shift(ylast, "gy", 1)
    yafter = shift(yfirst, "gy", -1)

    coef = pl.pallas_call(
        factors_kernel,
        out_shape=jax.ShapeDtypeStruct((chunks, tiles, FACES, layers, 8, lanes), f32),
        in_specs=[whole(pltpu.SMEM)] + [whole()] * 6,
        out_specs=whole(),
        scratch_shapes=[pltpu.VMEM((layers + 2, tiles, tall, lanes), f32)],
        compiler_params=pltpu.CompilerParams(vmem_limit_bytes=40 * 2**20),
        name="factors",
    )(ice_mask, viscosity, friction, xbefore, xafter, ybefore, yafter)

    pair = jax.ShapeDtypeStruct((2 * tiles, 2, lanes), f32)
    rhs, low, high = pl.pallas_call(
        functools.partial(sources_kernel, slots, layers),
        grid=(1,),
        out_shape=(jax.ShapeDtypeStruct((2, tiles, rows, lanes), f32), pair, pair),
        in_specs=[whole(), part((2, 1, rows, cols), (0, layers - 1, 0, 0)), whole(), whole()],
        out_specs=(whole(), whole(), whole()),
        name="sources",
    )(arrived.reshape(owners * 4 * slots, lanes), velocity, ybefore, yafter)
    before = shift(high, "gx", 1)
    after = shift(low, "gx", -1)

    return pl.pallas_call(
        sweeps_kernel,
        grid=(1,),
        out_shape=(
            jax.ShapeDtypeStruct(velocity.shape, f32),
            jax.ShapeDtypeStruct(friction.shape, f32),
        ),
        in_specs=[whole(pltpu.SMEM), whole(pl.ANY)] + [whole()] * 3 + [part((2, 1, rows, cols), (0, 0, 0, 0))],
        out_specs=(whole(pl.ANY), whole()),
        scratch_shapes=[
            pltpu.VMEM(coef.shape, f32),
            pltpu.VMEM((2, tiles, tall, lanes), f32),
            pltpu.VMEM((2, layers, tiles, tall, lanes), f32),
            pltpu.VMEM((2, layers, tiles, tall, lanes), f32),
            pltpu.VMEM((2, layers, rows, cols), f32),
            pltpu.SemaphoreType.DMA((chunks,)),
            pltpu.SemaphoreType.DMA((chunks - 2,)),
        ],
        compiler_params=pltpu.CompilerParams(vmem_limit_bytes=48 * 2**20),
        name="sweeps",
    )(ice_mask, coef, rhs, before, after, velocity)


def solution(mesh):
    placed = (
        P(None, None, "gx", "gy"),
        P(None, "gx", "gy"),
        P("gx", "gy"),
        P("gx", "gy"),
        P("gx", "gy", None, None, None, None, None),
        P("gx", "gy", None, None, None),
        P("gx", "gy", None, None),
    )
    return jax.shard_map(
        per_device,
        mesh=mesh,
        in_specs=placed,
        out_specs=(P(None, None, "gx", "gy"), P("gx", "gy")),
        check_vma=False,
    )
```

time: 226 us -> 68.2 us (0.30)
  the two profiles are of different devices: /device:TPU:1 before, /device:TPU:4 now
where the time goes in v1:
time: 68.2 us; the launch traced here: 67.7 us
  Pallas kernels  30.4 us (45%)
  starting transfers between devices  24.1 us (35%)
  waiting for transfers between devices  7.44 us (11%)
  local copies, waits for them, and re-layouts  4.4 us (6%)
  between operations  1.43 us (2%)
    ppermute x6, starting transfers between devices, shift(): return lax.ppermute(value, axis, pairs)  18 us
    pallas_call x1, Pallas kernels, per_device(): pl.pallas_call(sweeps_kernel, grid=(1,), out_shape=(jax.ShapeDtypeStruct(...  14.4 us
    pallas_call x1, Pallas kernels, per_device(): pl.pallas_call(factors_kernel, out_shape=jax.ShapeDtypeStruct((chunks, ti...  8.66 us
    ppermute x6, waiting for transfers between devices, shift(): return lax.ppermute(value, axis, pairs)  7.43 us
    all_to_all x1, starting transfers between devices, per_device(): lax.all_to_all(packed, ('gx', 'gy'), split_axis=0, concat_axis=0, tiled=T...  6.1 us
    unnamed x26, local copies, waits for them, and re-layouts  3.06 us
    pallas_call x1, Pallas kernels, per_device(): pl.pallas_call(functools.partial(sources_kernel, slots, layers), grid=(1,...  2.9 us
    pallas_call x1, Pallas kernels, per_device(): pl.pallas_call(columns_kernel, grid=(1,), out_shape=(plane, plane), in_sp...  2.37 us
  transfers between devices with their start and end apart: 7, of which 4 were waited for; matrix products, arithmetic and copies ran while one was open for 0% of the time, Pallas kernels for 16%

profile of v1, /device:TPU:4, one launch (start us, length us, event | category | flops | bytes accessed | tf_op | source)
XLA Modules:
  0.0 67.7 jit_solution(6902038958141142942)
XLA Ops:
  1.3 1.3 %copy.9.count_ref = s32[8,4]{1,0:T(8,128)} copy(s32[8,4]{0,1:T(4,128)} %bitcast.11) | data formatting | bytes 256 | tf_op jit(solution)/shard_map/squeeze | solution.py:404
  2.6 2.0 %pack.1 = (f32[32,16,128]{2,1,0:T(8,128)}, f32[12,4,384]{2,1,0:T(4,128)}, f32[12,4,384]{2,1,0:T(4,128)}) custom-call(s32[8,4]{1,0:T(8,128)} %copy.9.count_ref, s32[1,1]{1,0:T(1,128)S(6)} %copy.10.ice_ref, f32[32,3,4,128]{3,2,1,0:T(4,128)} %bitcast.9, s32[4,4,8]{2,1,0:T(4,128)} %bitcast.10, f32[10,96,384]{2,1,0:T(8,128)} %visc_ref.1, ...), custom_call_target="tpu_custom_call" | custom-call | tf_op jit(solution)/shard_map/pack/pallas_call | solution.py:410
  4.6 6.1 %all-to-all-start = ((f32[32,16,128]{2,1,0:T(8,128)}), f32[32,16,128]{2,1,0:T(8,128)S(1)}, u32[]{:S(2)}, u32[]{:S(2)}) async-start(f32[32,16,128]{2,1,0:T(8,128)} %get-tuple-element.14), calls=%async_computation | async-start | bytes 524288 | tf_op jit(solution)/shard_map/all_to_all | solution.py:427
  10.7 2.1 %collective-permute-start = (f32[12,4,384]{2,1,0:T(4,128)}, f32[12,4,384]{2,1,0:T(4,128)S(1)}, u32[]{:S(2)}, u32[]{:S(2)}) collective-permute-start(f32[12,4,384]{2,1,0:T(4,128)} %get-tuple-element.10), channel_id=1, source_target_pairs={{0,4},{4,8},{8,12},{12,16},{16,20},{20,24},{24,28},{1,5},{5,9},{9,... | collective-permute-start | bytes 221192 | tf_op jit(solution)/shard_map/ppermute | solution.py:400
  12.8 4.4 %collective-permute-start.1 = (f32[12,4,384]{2,1,0:T(4,128)}, f32[12,4,384]{2,1,0:T(4,128)S(1)}, u32[]{:S(2)}, u32[]{:S(2)}) collective-permute-start(f32[12,4,384]{2,1,0:T(4,128)} %get-tuple-element.11), channel_id=1, source_target_pairs={{4,0},{8,4},{12,8},{16,12},{20,16},{24,20},{28,24},{5,1},{9,5},{13... | collective-permute-start | bytes 221192 | tf_op jit(solution)/shard_map/ppermute | solution.py:400
  17.2 0.4 collective-permute-done.before_ref.xbefore_ref
  17.7 0.0 copy-start.4
  17.7 1.9 %collective-permute-done.1.after_ref.xafter_ref = f32[12,4,384]{2,1,0:T(4,128)S(1)} collective-permute-done((f32[12,4,384]{2,1,0:T(4,128)}, f32[12,4,384]{2,1,0:T(4,128)S(1)}, u32[]{:S(2)}, u32[]{:S(2)}) %collective-permute-start.1) | collective-permute-done | bytes 73760 | tf_op jit(solution)/shard_map/ppermute | solution.py:400
  19.5 0.0 copy-done.4
  19.5 0.0 copy-start.6
  19.5 0.6 copy-done.6
  20.1 2.4 %columns.1 = (f32[128,128]{1,0:T(8,128)}, f32[128,128]{1,0:T(8,128)}) custom-call(s32[1,1]{1,0:T(1,128)S(6)} %copy.10.ice_ref, f32[10,96,384]{2,1,0:T(8,128)} %visc_ref.1, f32[10,96,384]{2,1,0:T(8,128)} %visc_ref.1, f32[96,384]{1,0:T(8,128)} %fric_ref.1, f32[96,384]{1,0:T(8,128)} %fric_ref.1, f32[2,10,96,384]{3,2,1,0:T(8,128)} %vel_ref.3, ...), custom_call_target="tpu_custom_call" | custom-call | tf_op jit(solution)/shard_map/columns/pallas_call | solution.py:432
  22.5 0.0 copy-start.1
  22.5 0.0 copy-start.2
  22.5 0.0 copy-start.5
  22.5 0.0 copy-start.7
  22.5 3.5 %collective-permute-start.2 = (f32[128,128]{1,0:T(8,128)}, f32[128,128]{1,0:T(8,128)S(1)}, u32[]{:S(2)}, u32[]{:S(2)}) collective-permute-start(f32[128,128]{1,0:T(8,128)} %get-tuple-element.12), channel_id=1, source_target_pairs={{0,1},{1,2},{2,3},{4,5},{5,6},{6,7},{8,9},{9,10},{10,11},{12,13},{... | collective-permute-start | bytes 196616 | tf_op jit(solution)/shard_map/ppermute | solution.py:400
  26.0 1.3 %collective-permute-start.3 = (f32[128,128]{1,0:T(8,128)}, f32[128,128]{1,0:T(8,128)S(1)}, u32[]{:S(2)}, u32[]{:S(2)}) collective-permute-start(f32[128,128]{1,0:T(8,128)} %get-tuple-element.13), channel_id=1, source_target_pairs={{1,0},{2,1},{3,2},{5,4},{6,5},{7,6},{9,8},{10,9},{11,10},{13,12},{... | collective-permute-start | bytes 196616 | tf_op jit(solution)/shard_map/ppermute | solution.py:400
  27.3 1.1 %collective-permute-done.2.ybefore_ref = f32[128,128]{1,0:T(8,128)S(1)} collective-permute-done((f32[128,128]{1,0:T(8,128)}, f32[128,128]{1,0:T(8,128)S(1)}, u32[]{:S(2)}, u32[]{:S(2)}) %collective-permute-start.2) | collective-permute-done | bytes 65568 | tf_op jit(solution)/shard_map/ppermute | solution.py:400
  28.5 0.0 copy-start.8
  28.5 4.0 %collective-permute-done.3.yafter_ref = f32[128,128]{1,0:T(8,128)S(1)} collective-permute-done((f32[128,128]{1,0:T(8,128)}, f32[128,128]{1,0:T(8,128)S(1)}, u32[]{:S(2)}, u32[]{:S(2)}) %collective-permute-start.3) | collective-permute-done | bytes 65568 | tf_op jit(solution)/shard_map/ppermute | solution.py:400
  32.5 0.0 copy-start.10
  32.5 0.0 all-to-all-done
  32.5 0.0 copy-start.12
  32.5 0.0 copy-done.8
  32.5 0.6 copy-done.10
  33.1 0.1 copy-done.12
  33.2 2.9 %sources.1 = (f32[2,4,96,128]{3,2,1,0:T(8,128)}, f32[8,2,128]{2,1,0:T(2,128)}, f32[8,2,128]{2,1,0:T(2,128)}) custom-call(f32[512,128]{1,0:T(8,128)} %bitcast.8, f32[2,10,96,384]{3,2,1,0:T(8,128)} %vel_ref.3, f32[128,128]{1,0:T(8,128)} %copy-done.8, f32[128,128]{1,0:T(8,128)} %copy-done.10), custom_call_target="tpu_custom_call" | custom-call | tf_op jit(solution)/shard_map/sources/pallas_call | solution.py:464
  36.1 1.9 %collective-permute-start.4 = (f32[8,2,128]{2,1,0:T(2,128)}, f32[8,2,128]{2,1,0:T(2,128)S(1)}, u32[]{:S(2)}, u32[]{:S(2)}) collective-permute-start(f32[8,2,128]{2,1,0:T(2,128)} %get-tuple-element.16), channel_id=1, source_target_pairs={{0,4},{4,8},{8,12},{12,16},{16,20},{20,24},{24,28},{1,5},{5,9},{9,... | collective-permute-start | bytes 24584 | tf_op jit(solution)/shard_map/ppermute | solution.py:400
  38.0 0.0 copy-start
  38.0 0.0 copy-start.3
  38.1 4.8 %collective-permute-start.5 = (f32[8,2,128]{2,1,0:T(2,128)}, f32[8,2,128]{2,1,0:T(2,128)S(1)}, u32[]{:S(2)}, u32[]{:S(2)}) collective-permute-start(f32[8,2,128]{2,1,0:T(2,128)} %get-tuple-element.17), channel_id=1, source_target_pairs={{4,0},{8,4},{12,8},{16,12},{20,16},{24,20},{28,24},{5,1},{9,5},{13... | collective-permute-start | bytes 24584 | tf_op jit(solution)/shard_map/ppermute | solution.py:400
  42.9 0.0 copy-done.1
  42.9 0.0 copy-done.2
  42.9 0.0 copy-done.5
  42.9 0.0 copy-done.7
  42.9 0.0 copy-start.9
  42.9 0.8 %copy-done.9 = f32[128,128]{1,0:T(8,128)S(1)} copy-done((f32[128,128]{1,0:T(8,128)S(1)}, f32[128,128]{1,0:T(8,128)}, u32[]{:S(2)}) %copy-start.9) | copy-done | bytes 65560
  43.7 0.0 copy-start.11
  43.7 0.8 %copy-done.11 = f32[128,128]{1,0:T(8,128)S(1)} copy-done((f32[128,128]{1,0:T(8,128)S(1)}, f32[128,128]{1,0:T(8,128)}, u32[]{:S(2)}) %copy-start.11) | copy-done | bytes 65560
  44.6 8.7 %factors.1.coef_hbm = f32[14,4,6,10,8,128]{5,4,3,2,1,0:T(8,128)} custom-call(s32[1,1]{1,0:T(1,128)S(6)} %copy.10.ice_ref, f32[10,96,384]{2,1,0:T(8,128)S(1)} %copy-done.1, f32[96,384]{1,0:T(8,128)S(1)} %copy-done.2, f32[12,4,384]{2,1,0:T(4,128)S(1)} %copy-done.5, f32[12,4,384]{2,1,0:T(4,128)S(1)} %copy-done.7, f32[128,128]{1,0:T(8,128)S(1)} %copy-done.9, ...), custom_call_target="tpu_custom_call" | custom-call | tf_op jit(solution)/shard_map/factors/pallas_call | solution.py:453
  53.2 0.0 collective-permute-done.4.before_ref
  53.2 0.0 collective-permute-done.5.after_ref
  53.3 0.0 copy-done
  53.3 0.0 copy-done.3
  53.3 14.4 %sweeps.1 = (f32[2,10,96,384]{3,2,1,0:T(8,128)}, f32[96,384]{1,0:T(8,128)}) custom-call(s32[1,1]{1,0:T(1,128)S(6)} %copy.10.ice_ref, f32[14,4,6,10,8,128]{5,4,3,2,1,0:T(8,128)} %factors.1.coef_hbm, f32[2,4,96,128]{3,2,1,0:T(8,128)S(1)} %copy-done.3, f32[8,2,128]{2,1,0:T(2,128)S(1)} %collective-permute-done.4.before_ref, ...), custom_call_target="tpu_custom_call" | custom-call | tf_op jit(solution)/shard_map/sweeps/pallas_call | solution.py:475
Async XLA Ops:
  4.6 27.9 %all-to-all-start = ((f32[32,16,128]{2,1,0:T(8,128)}), f32[32,16,128]{2,1,0:T(8,128)S(1)}, u32[]{:S(2)}, u32[]{:S(2)}) async-start(f32[32,16,128]{2,1,0:T(8,128)} %get-tuple-element.14), calls=%async_computation | async-start | bytes 524288 | tf_op jit(solution)/shard_map/all_to_all | solution.py:427
  10.7 6.9 %collective-permute-start = (f32[12,4,384]{2,1,0:T(4,128)}, f32[12,4,384]{2,1,0:T(4,128)S(1)}, u32[]{:S(2)}, u32[]{:S(2)}) collective-permute-start(f32[12,4,384]{2,1,0:T(4,128)} %get-tuple-element.10), channel_id=1, source_target_pairs={{0,4},{4,8},{8,12},{12,16},{16,20},{20,24},{24,28},{1,5},{5,9},{9,... | collective-permute-start | bytes 221192 | tf_op jit(solution)/shard_map/ppermute | solution.py:400
  12.8 6.7 %collective-permute-start.1 = (f32[12,4,384]{2,1,0:T(4,128)}, f32[12,4,384]{2,1,0:T(4,128)S(1)}, u32[]{:S(2)}, u32[]{:S(2)}) collective-permute-start(f32[12,4,384]{2,1,0:T(4,128)} %get-tuple-element.11), channel_id=1, source_target_pairs={{4,0},{8,4},{12,8},{16,12},{20,16},{24,20},{28,24},{5,1},{9,5},{13... | collective-permute-start | bytes 221192 | tf_op jit(solution)/shard_map/ppermute | solution.py:400
  17.7 1.9 %copy-start.4 = (f32[12,4,384]{2,1,0:T(4,128)}, f32[12,4,384]{2,1,0:T(4,128)S(1)}, u32[]{:S(2)}) copy-start(f32[12,4,384]{2,1,0:T(4,128)S(1)} %collective-permute-done.before_ref.xbefore_ref) | copy-start | bytes 221188
  19.5 0.6 copy-start.6
  22.5 20.4 %copy-start.1 = (f32[10,96,384]{2,1,0:T(8,128)S(1)}, f32[10,96,384]{2,1,0:T(8,128)}, u32[]{:S(2)}) copy-start(f32[10,96,384]{2,1,0:T(8,128)} %visc_ref.1) | copy-start | bytes 4423684
  22.5 20.4 %copy-start.2 = (f32[96,384]{1,0:T(8,128)S(1)}, f32[96,384]{1,0:T(8,128)}, u32[]{:S(2)}) copy-start(f32[96,384]{1,0:T(8,128)} %fric_ref.1) | copy-start | bytes 442372
  22.5 20.4 %copy-start.5 = (f32[12,4,384]{2,1,0:T(4,128)S(1)}, f32[12,4,384]{2,1,0:T(4,128)}, u32[]{:S(2)}) copy-start(f32[12,4,384]{2,1,0:T(4,128)} %copy-done.4) | copy-start | bytes 221188
  22.5 20.4 %copy-start.7 = (f32[12,4,384]{2,1,0:T(4,128)S(1)}, f32[12,4,384]{2,1,0:T(4,128)}, u32[]{:S(2)}) copy-start(f32[12,4,384]{2,1,0:T(4,128)} %copy-done.6) | copy-start | bytes 221188
  22.5 5.9 %collective-permute-start.2 = (f32[128,128]{1,0:T(8,128)}, f32[128,128]{1,0:T(8,128)S(1)}, u32[]{:S(2)}, u32[]{:S(2)}) collective-permute-start(f32[128,128]{1,0:T(8,128)} %get-tuple-element.12), channel_id=1, source_target_pairs={{0,1},{1,2},{2,3},{4,5},{5,6},{6,7},{8,9},{9,10},{10,11},{12,13},{... | collective-permute-start | bytes 196616 | tf_op jit(solution)/shard_map/ppermute | solution.py:400
  26.0 6.4 %collective-permute-start.3 = (f32[128,128]{1,0:T(8,128)}, f32[128,128]{1,0:T(8,128)S(1)}, u32[]{:S(2)}, u32[]{:S(2)}) collective-permute-start(f32[128,128]{1,0:T(8,128)} %get-tuple-element.13), channel_id=1, source_target_pairs={{1,0},{2,1},{3,2},{5,4},{6,5},{7,6},{9,8},{10,9},{11,10},{13,12},{... | collective-permute-start | bytes 196616 | tf_op jit(solution)/shard_map/ppermute | solution.py:400
  28.5 4.0 %copy-start.8 = (f32[128,128]{1,0:T(8,128)}, f32[128,128]{1,0:T(8,128)S(1)}, u32[]{:S(2)}) copy-start(f32[128,128]{1,0:T(8,128)S(1)} %collective-permute-done.2.ybefore_ref) | copy-start | bytes 196612
  32.5 0.6 copy-start.10
  32.5 0.7 %copy-start.12 = (f32[32,16,128]{2,1,0:T(8,128)}, f32[32,16,128]{2,1,0:T(8,128)S(1)}, u32[]{:S(2)}) copy-start(f32[32,16,128]{2,1,0:T(8,128)S(1)} %all-to-all-done) | copy-start | bytes 786436
  36.1 17.1 %collective-permute-start.4 = (f32[8,2,128]{2,1,0:T(2,128)}, f32[8,2,128]{2,1,0:T(2,128)S(1)}, u32[]{:S(2)}, u32[]{:S(2)}) collective-permute-start(f32[8,2,128]{2,1,0:T(2,128)} %get-tuple-element.16), channel_id=1, source_target_pairs={{0,4},{4,8},{8,12},{12,16},{16,20},{20,24},{24,28},{1,5},{5,9},{9,... | collective-permute-start | bytes 24584 | tf_op jit(solution)/shard_map/ppermute | solution.py:400
  38.0 15.2 %copy-start = (f32[2,10,96,384]{3,2,1,0:T(8,128)S(1)}, f32[2,10,96,384]{3,2,1,0:T(8,128)}, u32[]{:S(2)}) copy-start(f32[2,10,96,384]{3,2,1,0:T(8,128)} %vel_ref.3) | copy-start | bytes 8847364
  38.0 15.2 %copy-start.3 = (f32[2,4,96,128]{3,2,1,0:T(8,128)S(1)}, f32[2,4,96,128]{3,2,1,0:T(8,128)}, u32[]{:S(2)}) copy-start(f32[2,4,96,128]{3,2,1,0:T(8,128)} %get-tuple-element.15.rhs_ref) | copy-start | bytes 1179652
  38.1 15.2 %collective-permute-start.5 = (f32[8,2,128]{2,1,0:T(2,128)}, f32[8,2,128]{2,1,0:T(2,128)S(1)}, u32[]{:S(2)}, u32[]{:S(2)}) collective-permute-start(f32[8,2,128]{2,1,0:T(2,128)} %get-tuple-element.17), channel_id=1, source_target_pairs={{4,0},{8,4},{12,8},{16,12},{20,16},{24,20},{28,24},{5,1},{9,5},{13... | collective-permute-start | bytes 24584 | tf_op jit(solution)/shard_map/ppermute | solution.py:400
  42.9 0.8 %copy-start.9 = (f32[128,128]{1,0:T(8,128)S(1)}, f32[128,128]{1,0:T(8,128)}, u32[]{:S(2)}) copy-start(f32[128,128]{1,0:T(8,128)} %copy-done.8) | copy-start | bytes 196612
  43.7 0.8 %copy-start.11 = (f32[128,128]{1,0:T(8,128)S(1)}, f32[128,128]{1,0:T(8,128)}, u32[]{:S(2)}) copy-start(f32[128,128]{1,0:T(8,128)} %copy-done.10) | copy-start | bytes 196612

commit v2 on v0

v2 whole, which is shorter than its diff:
```python
import functools

import jax
import jax.numpy as jnp
from jax import lax
from jax.experimental import pallas as pl
from jax.experimental.pallas import tpu as pltpu
from jax.sharding import PartitionSpec as P

VERTICAL_GAIN = 2.0
RELAX_WEIGHT = 0.8

MARGIN = 8
FACES = 6
MIB = 2**20


def lanes_of(shape):
    return lax.broadcasted_iota(jnp.int32, shape, len(shape) - 1)


def three_parts(value):
    high = value.astype(jnp.bfloat16)
    rest = value - high.astype(jnp.float32)
    middle = rest.astype(jnp.bfloat16)
    low = (rest - middle.astype(jnp.float32)).astype(jnp.bfloat16)
    return jnp.concatenate([high, middle, low], axis=-1)


def sum_parts(value):
    width = value.shape[-1] // 3
    return value[:, :width] + value[:, width : 2 * width] + value[:, 2 * width :]


def pick(onehot, value):
    return sum_parts(jnp.dot(onehot, three_parts(value), preferred_element_type=jnp.float32))


def spread(onehot, value):
    dims = (((0,), (0,)), ((), ()))
    return sum_parts(
        lax.dot_general(onehot, three_parts(value), dims, preferred_element_type=jnp.float32)
    )


def filled(ref, shape):
    return jnp.broadcast_to(ref[...], shape).astype(jnp.float32)


def fetch_all(copies):
    for copy in copies:
        copy.start()


def wait_all(copies):
    for copy in copies:
        copy.wait()


def pack_kernel(
    count_hbm, tiles_hbm, cells_hbm, ice_hbm, visc_hbm, fric_hbm, vel_hbm, out_ref, first_ref, last_ref,
    counts, tiles, cells, ice, visc, fric, vel, sems,
):
    owners_y, owners_x = counts.shape
    slots, lanes = tiles.shape[2], tiles.shape[3]
    layers, rows, cols = visc_hbm.shape
    top = vel_hbm.at[:, vel_hbm.shape[1] - 1]
    ends = (pl.ds(0, lanes), pl.ds(cols - lanes, lanes))
    pairs = [(count_hbm, counts), (cells_hbm, cells), (tiles_hbm, tiles), (ice_hbm, ice)]
    for side, span in enumerate(ends):
        pairs.append((visc_hbm.at[:, :, span], visc.at[side]))
        pairs.append((fric_hbm.at[:, span], fric.at[side]))
        pairs.append((top.at[:, :, span], vel.at[side]))
    copies = [pltpu.make_async_copy(a, b, sems.at[n]) for n, (a, b) in enumerate(pairs)]
    fetch_all(copies)
    wait_all(copies[:3])
    lane = lanes_of((slots, lanes))
    slot = lax.broadcasted_iota(jnp.int32, (slots, lanes), 0)
    zero = jnp.zeros((slots, lanes), jnp.float32)
    for ox in range(owners_x):
        firsts, lasts, owns = [], [], []
        for oy in range(owners_y):
            owner = ox * owners_y + oy
            u = tiles[owner, 0]
            v = tiles[owner, 1]
            count = jnp.broadcast_to(counts[oy : oy + 1, ox : ox + 1], (slots, lanes))
            w = jnp.where(slot < count, tiles[owner, 2], 0.0)
            cell = jnp.broadcast_to(cells[oy, :, ox : ox + 1], (slots, lanes)).astype(jnp.float32)
            out_ref[owner, 0:slots] = u
            out_ref[owner, slots : 2 * slots] = v
            out_ref[owner, 2 * slots : 3 * slots] = w
            first = jnp.where(lane < 4, pltpu.roll(v, 2, 1), jnp.where(lane < 6, pltpu.roll(w, 4, 1), cell))
            firsts.append(jnp.where(lane < 2, u, first))
            last = jnp.where(
                lane >= lanes - 4,
                pltpu.roll(v, lanes - 2, 1),
                jnp.where(lane >= lanes - 6, pltpu.roll(w, lanes - 4, 1), cell),
            )
            lasts.append(jnp.where(lane >= lanes - 2, u, last))
            owns.append(cell)
        for oy in range(owners_y):
            after = firsts[oy + 1] if oy + 1 < owners_y else zero
            before = lasts[oy - 1] if oy > 0 else zero
            meta = jnp.where(lane < 16, after, jnp.where(lane >= lanes - 16, before, owns[oy]))
            out_ref[ox * owners_y + oy, 3 * slots : 4 * slots] = meta

    wait_all(copies[3:])
    lane = lanes_of((rows, lanes))
    icefield = filled(ice, (rows, lanes))
    first = jnp.zeros((rows, lanes), jnp.float32)
    last = jnp.zeros((rows, lanes), jnp.float32)
    for k in range(layers + 4):
        if k < layers:
            mine = (visc[0, k], visc[1, k])
        elif k == layers:
            mine = (fric[0], fric[1])
        elif k == layers + 1:
            mine = (icefield, icefield)
        else:
            mine = (vel[0, k - layers - 2], vel[1, k - layers - 2])
        here = (lane >= 3 * k) & (lane < 3 * k + 3)
        first = jnp.where(here, pltpu.roll(mine[0], 3 * k, 1), first)
        there = (lane >= lanes - 3 - 3 * k) & (lane < lanes - 3 * k)
        last = jnp.where(there, pltpu.roll(mine[1], (lanes - 3 * k) % lanes, 1), last)
    first_ref[...] = first
    last_ref[...] = last


def side_tile(before, after, k):
    lanes = before.shape[-1]
    lane = lanes_of(before.shape)
    left = pltpu.roll(before, (3 * k) % lanes, 1)
    right = pltpu.roll(after, (lanes - 3 * k) % lanes, 1)
    return jnp.where(lane < 3, right, jnp.where(lane >= lanes - 3, left, 0.0))


def ring_pair(load, tile, tiles):
    here = load(tile)
    lanes = here.shape[-1]
    lane = lanes_of(here.shape)
    before = pltpu.roll(jnp.where(lane == lanes - 1, load((tile - 1) % tiles), here), 1, 1)
    after = pltpu.roll(jnp.where(lane == 0, load((tile + 1) % tiles), here), lanes - 1, 1)
    return here, before, after


def factor_columns(layers, tile, tiles, load, store):
    gain = (0.5 * RELAX_WEIGHT) * load(layers + 1, tile, 0)
    up = None
    ratio = None
    for k in range(layers):
        here, south, north = ring_pair(lambda s: load(k, s, 0), tile, tiles)
        west = here + load(k, tile, -1)
        east = here + load(k, tile, 1)
        south = here + south
        north = here + north
        entry = 0.5 * (west + east + south + north)
        if k == 0:
            entry = entry + load(layers, tile, 0)
        if k > 0:
            entry = entry + (up - up * ratio)
        if k < layers - 1:
            above = (0.5 * VERTICAL_GAIN) * (here + load(k + 1, tile, 0))
            entry = entry + above
        inverse = jnp.where(entry > 0.0, 1.0 / entry, 0.0)
        scale = gain * inverse
        store(0, k, west * scale)
        store(1, k, east * scale)
        store(2, k, south * scale)
        store(3, k, north * scale)
        if k > 0:
            store(4, k, up * inverse)
        if k < layers - 1:
            up = above
            ratio = up * inverse
            store(5, k, ratio)
        else:
            store(4, 0, 2.0 * scale)


def first_columns(layers, rhs, coef, store):
    for n in range(2):
        value = rhs(n) * coef(4, 0)
        store(n, layers - 1, value)
        for k in range(layers - 2, -1, -1):
            value = coef(5, k) * value
            store(n, k, value)


def relax_columns(layers, tile, tiles, old, rhs, coef, store):
    forward = [[], []]
    for k in range(layers):
        west, east, south, north = (coef(f, k) for f in range(4))
        for n in range(2):
            here, before, after = ring_pair(lambda s: old(n, k, s, 0), tile, tiles)
            value = west * old(n, k, tile, -1) + east * old(n, k, tile, 1)
            value = value + (south * before + north * after)
            if k > 0:
                value = value + coef(4, k) * forward[n][k - 1]
            if k == layers - 1:
                value = value + rhs(n) * coef(4, 0)
            forward[n].append(value)
    for n in range(2):
        value = forward[n][layers - 1]
        for k in range(layers - 1, -1, -1):
            if k < layers - 1:
                value = forward[n][k] + coef(5, k) * value
            store(n, k, (1.0 - RELAX_WEIGHT) * old(n, k, tile, 0) + value)


def sources_kernel(
    slots, ice_hbm, tiles_ref, visc_hbm, fric_hbm, vel_hbm, before_any, after_any,
    rhs_ref, low_ref, high_ref, xlow_ref, xhigh_ref, ice, visc, fric, vel, before_ref, after_ref, sems,
):
    layers, rows, cols = visc_hbm.shape
    lanes = tiles_ref.shape[1]
    owners = tiles_ref.shape[0] // (4 * slots)
    blocks = cols // lanes
    pairs = [(vel_hbm.at[:, layers - 1], vel), (before_any, before_ref), (after_any, after_ref), (ice_hbm, ice)]
    for side, at in enumerate((0, rows - 8)):
        pairs.append((visc_hbm.at[:, pl.ds(at, 8), :], visc.at[side]))
        pairs.append((fric_hbm.at[pl.ds(at, 8), :], fric.at[side]))
    copies = [pltpu.make_async_copy(a, b, sems.at[n]) for n, (a, b) in enumerate(pairs)]
    fetch_all(copies)

    def channel(c):
        return jnp.concatenate(
            [tiles_ref[pl.ds(c * slots + s, owners, stride=4 * slots), :] for s in range(slots)], axis=0
        )

    seen_u, seen_v, weight, meta = channel(0), channel(1), channel(2), channel(3)
    count = owners * slots
    lane = lanes_of((count, lanes))
    row = lanes_of((count, rows))

    def onehot(column, b):
        cell = jnp.broadcast_to(column.astype(jnp.int32), (count, rows))
        return (cell == row * blocks + b).astype(jnp.bfloat16)

    def put(c, t, plane):
        rhs_ref[c, t] = plane
        xlow_ref[layers + 2 + c, t] = plane[0:4]
        xhigh_ref[layers + 2 + c, t] = plane[rows - 4 : rows]

    own = meta[:, lanes // 2 : lanes // 2 + 1]
    marks = jnp.concatenate([onehot(own, b) for b in range(blocks)], axis=1)
    wait_all(copies[:1])
    surface = jnp.concatenate(
        [
            jnp.concatenate([vel[c, :, b * lanes : (b + 1) * lanes] for b in range(blocks)], axis=0)
            for c in range(2)
        ],
        axis=1,
    )
    weights = jnp.concatenate([weight, weight], axis=1)
    terms = weights * (pick(marks, surface) - jnp.concatenate([seen_u, seen_v], axis=1))
    total = spread(marks, terms)
    for c in range(2):
        for b in range(blocks):
            put(c, b, total[b * rows : (b + 1) * rows, c * lanes : (c + 1) * lanes])

    wait_all(copies[1:3])
    beside = jnp.concatenate(
        [side_tile(before_ref[...], after_ref[...], layers + 2 + c) for c in range(2)], axis=1
    )
    mark_after = onehot(meta[:, 8:9], 0)
    mark_before = onehot(meta[:, lanes - 8 : lanes - 7], blocks - 1)
    weight_after = jnp.where(lane < 2, pltpu.roll(meta, lanes - 4, 1), 0.0)
    weight_before = jnp.where(lane >= lanes - 2, pltpu.roll(meta, 4, 1), 0.0)
    after = jnp.concatenate([meta, pltpu.roll(meta, lanes - 2, 1)], axis=1)
    before = jnp.concatenate([meta, pltpu.roll(meta, 2, 1)], axis=1)
    terms_after = jnp.concatenate([weight_after] * 2, axis=1) * (pick(mark_after, beside) - after)
    terms_before = jnp.concatenate([weight_before] * 2, axis=1) * (pick(mark_before, beside) - before)
    side = spread(mark_after, terms_after) + spread(mark_before, terms_before)
    for c in range(2):
        put(c, blocks, side[:, c * lanes : (c + 1) * lanes])

    wait_all(copies[3:])
    icefield = filled(ice, (8, lanes))
    for k in range(layers + 2):
        for t in range(blocks + 1):
            span = slice(t * lanes, (t + 1) * lanes)
            if t == blocks:
                low = side_tile(before_ref[0:8], after_ref[0:8], k)
                high = side_tile(before_ref[rows - 8 : rows], after_ref[rows - 8 : rows], k)
            elif k < layers:
                low, high = visc[0, k, :, span], visc[1, k, :, span]
            elif k == layers:
                low, high = fric[0, :, span], fric[1, :, span]
            else:
                low, high = icefield, icefield
            low_ref[k, t] = low
            high_ref[k, t] = high
            xlow_ref[k, t] = low[0:4]
            xhigh_ref[k, t] = high[4:8]


def inner_kernel(
    ice_hbm, visc_hbm, fric_hbm, before_any, after_any, rhs_any, adj_hbm, low_ref, high_ref, base_ref,
    ice, field, before, after, rhs, coef, one, two, three, sem_in, sem_out,
):
    steps, tiles, _, layers, _, lanes = coef.shape
    rows = three.shape[3]
    middle = pl.ds(MARGIN, rows)
    pairs = [(ice_hbm, ice), (before_any, before), (after_any, after)]
    for t in range(tiles - 1):
        span = pl.ds(t * lanes, lanes)
        pairs.append((visc_hbm.at[:, :, span], field.at[pl.ds(0, layers), t, middle, :]))
        pairs.append((fric_hbm.at[:, span], field.at[layers, t, middle, :]))
    pairs.append((rhs_any, rhs))
    copies = [pltpu.make_async_copy(a, b, sem_in.at[n]) for n, (a, b) in enumerate(pairs)]
    fetch_all(copies)
    edge = jnp.zeros((MARGIN, lanes), jnp.float32)
    for k in range(layers):
        for t in range(tiles):
            field[k, t, 0:MARGIN] = edge
            field[k, t, MARGIN + rows : 2 * MARGIN + rows] = edge
    wait_all(copies[:3])
    icefield = filled(ice, (rows, lanes))
    for t in range(tiles - 1):
        field[layers + 1, t, middle] = icefield
    for k in range(layers + 2):
        field[k, tiles - 1, middle] = side_tile(before[...], after[...], k)
    wait_all(copies[3:-1])

    def factors(r, carry):
        for t in range(tiles):

            def load(k, s, move):
                return field[k, s, pl.ds(MARGIN + r + move, 8, stride=steps), :]

            def store(f, k, value):
                coef[r, t, f, k] = value

            factor_columns(layers, t, tiles, load, store)
        return carry

    lax.fori_loop(0, steps, factors, 0)
    wait_all(copies[-1:])
    sublane = lax.broadcasted_iota(jnp.int32, (8, lanes), 0)

    def wrap(ref):
        for n in range(2):
            for k in range(layers):
                for t in range(tiles):
                    last = pltpu.roll(ref[n, k, t, steps], 1, 0)
                    ref[n, k, t, 0] = jnp.where(sublane == 0, 0.0, last)
                    first = pltpu.roll(ref[n, k, t, 1], 7, 0)
                    ref[n, k, t, steps + 1] = jnp.where(sublane == 7, 0.0, first)

    def rhs_of(r, t):
        return lambda n: rhs[n, t, pl.ds(r, 8, stride=steps), :]

    def coef_of(r, t):
        return lambda f, k: coef[r, t, f, k]

    def first_sweep(r, carry):
        for t in range(tiles):

            def store(n, k, value):
                one[n, k, t, r + 1] = value

            first_columns(layers, rhs_of(r, t), coef_of(r, t), store)
        return carry

    lax.fori_loop(0, steps, first_sweep, 0, unroll=2)
    wrap(one)

    def second_sweep(r, carry):
        for t in range(tiles):

            def old(n, k, s, move):
                return one[n, k, s, r + 1 + move]

            def store(n, k, value):
                two[n, k, t, r + 1] = value

            relax_columns(layers, t, tiles, old, rhs_of(r, t), coef_of(r, t), store)
        return carry

    lax.fori_loop(0, steps, second_sweep, 0, unroll=2)
    wrap(two)

    def result(t):
        middle = pl.ds(8, rows - 16)
        span = pl.ds(t * lanes, lanes)
        return pltpu.make_async_copy(three.at[:, :, t, middle, :], adj_hbm.at[:, :, middle, span], sem_out.at[t])

    for t in range(tiles - 1):

        def third_sweep(r, carry):
            def old(n, k, s, move):
                return two[n, k, s, r + 1 + move]

            def store(n, k, value):
                three[n, k, t, pl.ds(r, 8, stride=steps), :] = value

            relax_columns(layers, t, tiles, old, rhs_of(r, t), coef_of(r, t), store)
            return carry

        lax.fori_loop(0, steps, third_sweep, 0, unroll=4)
        result(t).start()
        for n in range(2):
            for k in range(layers):
                low_ref[n, k, t] = three[n, k, t, 0:8]
                high_ref[n, k, t] = three[n, k, t, rows - 8 : rows]
        for n in range(2):
            base_ref[n, :, t * lanes : (t + 1) * lanes] = three[n, 0, t]
    for t in range(tiles - 1):
        result(t).wait()


def edges_kernel(
    ice_hbm, own_low, own_high, before_ref, after_ref, rhs_ref, low_ref, high_ref, base_ref, vel_hbm, adj_in,
    adj_hbm, grad_ref, ice, field, coefs, rhs, one, two, patch, vel, sem_in, sem_out,
):
    tiles, _, layers = coefs.shape[1:4]
    rows, cols = grad_ref.shape
    lanes = coefs.shape[5]
    blocks = tiles - 1
    fetches = [
        pltpu.make_async_copy(vel_hbm.at[:, 0], vel, sem_in.at[0]),
        pltpu.make_async_copy(ice_hbm, ice, sem_in.at[1]),
    ]
    fetch_all(fetches)
    for k in range(layers + 4):
        for t in range(tiles):
            if k < layers + 2:
                field[0, k, t, 0:4] = before_ref[k, t]
                field[0, k, t, 4:12] = own_low[k, t]
                field[1, k, t, 4:12] = own_high[k, t]
                field[1, k, t, 12:16] = after_ref[k, t]
            else:
                n = k - layers - 2
                rhs[0, n, t, 0:4] = before_ref[k, t]
                rhs[0, n, t, 4:12] = rhs_ref[n, t, 0:8]
                rhs[1, n, t, 4:12] = rhs_ref[n, t, rows - 8 : rows]
                rhs[1, n, t, 12:16] = after_ref[k, t]
    starts = (2, 6)

    def at(ref, start):
        return lambda *index: ref[(*index, pl.ds(start, 8), slice(None))]

    for t in range(tiles):
        for side in range(2):

            def load(k, s, move):
                return field[side, k, s, pl.ds(starts[side] + move, 8), :]

            def store(f, k, value):
                coefs[side, t, f, k, pl.ds(starts[side], 8), :] = value

            factor_columns(layers, t, tiles, load, store)

    def sides(t, start, side):
        def rhs_of(n):
            return rhs[side, n, t, pl.ds(start, 8), :]

        def coef(f, k):
            return coefs[side, t, f, k, pl.ds(start, 8), :]

        return rhs_of, coef

    for t in range(tiles):
        for side in range(2):
            rhs_of, coef = sides(t, starts[side], side)

            def store(n, k, value):
                one[side, n, k, t, pl.ds(starts[side], 8), :] = value

            first_columns(layers, rhs_of, coef, store)
    for t in range(tiles):
        for side in range(2):
            rhs_of, coef = sides(t, starts[side], side)

            def old(n, k, s, move):
                return one[side, n, k, s, pl.ds(starts[side] + move, 8), :]

            def store(n, k, value):
                two[side, n, k, t, pl.ds(starts[side], 8), :] = value

            relax_columns(layers, t, tiles, old, rhs_of, coef, store)

    def result(side):
        return pltpu.make_async_copy(
            patch.at[side], adj_hbm.at[:, :, pl.ds(side * (rows - 8), 8), :], sem_out.at[side]
        )

    sublane = lax.broadcasted_iota(jnp.int32, (8, lanes), 0)
    wrong = (sublane < 3, sublane >= 5)
    inner = (low_ref, high_ref)
    for side in range(2):
        for t in range(blocks):
            rhs_of, coef = sides(t, 4, side)
            span = slice(t * lanes, (t + 1) * lanes)

            def old(n, k, s, move):
                return two[side, n, k, s, pl.ds(4 + move, 8), :]

            def store(n, k, value):
                patch[side, n, k, :, span] = jnp.where(wrong[side], value, inner[side][n, k, t])

            relax_columns(layers, t, tiles, old, rhs_of, coef, store)
        result(side).start()
    wait_all(fetches)
    icefield = filled(ice, (rows, cols))
    product = base_ref[0] * vel[0] + base_ref[1] * vel[1]
    grad_ref[...] = -icefield * product
    for side in range(2):
        span = slice(side * (rows - 8), side * (rows - 8) + 8)
        product = patch[side, 0, 0] * vel[0, span] + patch[side, 1, 0] * vel[1, span]
        grad_ref[span] = -icefield[0:8] * product
    for side in range(2):
        result(side).wait()


def whole(space=pltpu.VMEM):
    return pl.BlockSpec(memory_space=space)


def per_device(velocity, viscosity, friction, ice_mask, obs_tiles, obs_cell, obs_count):
    layers, rows, cols = viscosity.shape
    owners_x, owners_y, slots, channels, lanes = obs_tiles.shape[2:]
    blocks = cols // lanes
    tiles = blocks + 1
    owners = owners_x * owners_y
    steps = rows // 8
    f32 = jnp.float32

    def shape(*dims):
        return jax.ShapeDtypeStruct(dims, f32)

    def grant(mib):
        return pltpu.CompilerParams(vmem_limit_bytes=int(mib * MIB))

    def shift(value, axis, step):
        size = lax.axis_size(axis)
        pairs = [(i, i + step) for i in range(size) if 0 <= i + step < size]
        return lax.ppermute(value, axis, pairs)

    tiles_in = jnp.transpose(obs_tiles.reshape(owners, slots, channels, lanes), (0, 2, 1, 3))
    cells_in = jnp.transpose(obs_cell[0, 0], (1, 2, 0))
    counts_in = jnp.transpose(obs_count[0, 0], (1, 0))
    def part(dims, *index):
        return pl.BlockSpec(dims, lambda i: index)

    i32 = jnp.int32
    plane = shape(rows, lanes)
    hbm = whole(pltpu.HBM)
    anywhere = whole(pl.ANY)
    packed, yfirst, ylast = pl.pallas_call(
        pack_kernel,
        out_shape=(shape(owners, 4 * slots, lanes), plane, plane),
        in_specs=[hbm] * 7,
        out_specs=(whole(),) * 3,
        scratch_shapes=[
            pltpu.VMEM(counts_in.shape, i32),
            pltpu.VMEM(tiles_in.shape, f32),
            pltpu.VMEM(cells_in.shape, i32),
            pltpu.VMEM((1, 1), i32),
            pltpu.VMEM((2, layers, rows, lanes), f32),
            pltpu.VMEM((2, rows, lanes), f32),
            pltpu.VMEM((2, 2, rows, lanes), f32),
            pltpu.SemaphoreType.DMA((10,)),
        ],
        compiler_params=grant(62.5),
        cost_estimate=pl.CostEstimate(flops=4 * 10**9, transcendentals=0, bytes_accessed=0),
        name="pack",
    )(counts_in, tiles_in, cells_in, ice_mask, viscosity, friction, velocity)
    arrived = lax.all_to_all(packed, ("gx", "gy"), split_axis=0, concat_axis=0, tiled=True)
    ybefore = shift(ylast, "gy", 1)
    yafter = shift(yfirst, "gy", -1)

    own = shape(layers + 2, tiles, 8, lanes)
    edge = shape(layers + 4, tiles, 4, lanes)
    rhs, own_low, own_high, xlow, xhigh = pl.pallas_call(
        functools.partial(sources_kernel, slots),
        out_shape=(shape(2, tiles, rows, lanes), own, own, edge, edge),
        in_specs=[hbm, whole(), hbm, hbm, hbm, anywhere, anywhere],
        out_specs=(whole(),) * 5,
        scratch_shapes=[
            pltpu.VMEM((1, 1), i32),
            pltpu.VMEM((2, layers, 8, cols), f32),
            pltpu.VMEM((2, 8, cols), f32),
            pltpu.VMEM((2, rows, cols), f32),
            pltpu.VMEM((rows, lanes), f32),
            pltpu.VMEM((rows, lanes), f32),
            pltpu.SemaphoreType.DMA((8,)),
        ],
        compiler_params=grant(12 + (owners * slots) // 64),
        cost_estimate=pl.CostEstimate(flops=4 * 10**9, transcendentals=0, bytes_accessed=0),
        name="sources",
    )(ice_mask, arrived.reshape(owners * 4 * slots, lanes), viscosity, friction, velocity, ybefore, yafter)
    xbefore = shift(xhigh, "gx", 1)
    xafter = shift(xlow, "gx", -1)

    ends = shape(2, layers, blocks, 8, lanes)
    wide = pltpu.VMEM((2, layers, tiles, steps + 2, 8, lanes), f32)
    adjoint, low, high, base = pl.pallas_call(
        inner_kernel,
        out_shape=(shape(*velocity.shape), ends, ends, shape(2, rows, cols)),
        in_specs=[hbm, hbm, hbm, anywhere, anywhere, anywhere],
        out_specs=(hbm, whole(), whole(), whole()),
        scratch_shapes=[
            pltpu.VMEM((1, 1), i32),
            pltpu.VMEM((layers + 2, tiles, rows + 2 * MARGIN, lanes), f32),
            pltpu.VMEM((rows, lanes), f32),
            pltpu.VMEM((rows, lanes), f32),
            pltpu.VMEM((2, tiles, rows, lanes), f32),
            pltpu.VMEM((steps, tiles, FACES, layers, 8, lanes), f32),
            wide,
            wide,
            pltpu.VMEM((2, layers, blocks, rows, lanes), f32),
            pltpu.SemaphoreType.DMA((2 * blocks + 4,)),
            pltpu.SemaphoreType.DMA((blocks,)),
        ],
        compiler_params=grant(30),
        cost_estimate=pl.CostEstimate(flops=4 * 10**9, transcendentals=0, bytes_accessed=0),
        name="inner",
    )(ice_mask, viscosity, friction, ybefore, yafter, rhs)

    return pl.pallas_call(
        edges_kernel,
        out_shape=(shape(*velocity.shape), shape(rows, cols)),
        in_specs=[hbm] + [whole()] * 8 + [hbm, hbm],
        out_specs=(hbm, whole()),
        scratch_shapes=[
            pltpu.VMEM((1, 1), i32),
            pltpu.VMEM((2, layers + 2, tiles, 16, lanes), f32),
            pltpu.VMEM((2, tiles, FACES, layers, 16, lanes), f32),
            pltpu.VMEM((2, 2, tiles, 16, lanes), f32),
            pltpu.VMEM((2, 2, layers, tiles, 16, lanes), f32),
            pltpu.VMEM((2, 2, layers, tiles, 16, lanes), f32),
            pltpu.VMEM((2, 2, layers, 8, cols), f32),
            pltpu.VMEM((2, rows, cols), f32),
            pltpu.SemaphoreType.DMA((2,)),
            pltpu.SemaphoreType.DMA((2,)),
        ],
        input_output_aliases={10: 0},
        compiler_params=grant(14),
        cost_estimate=pl.CostEstimate(flops=4 * 10**9, transcendentals=0, bytes_accessed=0),
        name="edges",
    )(ice_mask, own_low, own_high, xbefore, xafter, rhs, low, high, base, velocity, adjoint)


def solution(mesh):
    placed = (
        P(None, None, "gx", "gy"),
        P(None, "gx", "gy"),
        P("gx", "gy"),
        P("gx", "gy"),
        P("gx", "gy", None, None, None, None, None),
        P("gx", "gy", None, None, None),
        P("gx", "gy", None, None),
    )
    return jax.shard_map(
        per_device,
        mesh=mesh,
        in_specs=placed,
        out_specs=(P(None, None, "gx", "gy"), P("gx", "gy")),
        check_vma=False,
    )
```

time: 226 us -> 44.4 us (0.20); the launches traced: 222 us -> 44 us
  local copies, waits for them, and re-layouts: 86.2 us -> 2.76 us
  other arithmetic: 70.8 us -> 0 us
  starting transfers between devices: 52.2 us -> 16.4 us
  Pallas kernels: 0 us -> 17.7 us
  waiting for transfers between devices: 9.41 us -> 5.74 us
    add x9 -> x0, other arithmetic: 34.8 us -> none  [the longest x3 15.9 us: relax(): driven + south_face * padded_adj[..., 1:-1, :-2]]
    ppermute x12 -> x4, starting transfers between devices: 34 us -> 9.3 us  [shift(): return lax.ppermute(value, axis, pairs)]
    pallas_call x0 -> x4, Pallas kernels: none -> 17.7 us  [the longest x1 10.3 us: per_device(): pl.pallas_call(inner_kernel, out_shape=(shape(*velocity.shape), ends, end...]
    ppermute x6 -> x0, local copies, waits for them, and re-layouts: 13.6 us -> none  [the longest x3 6.86 us: padded_2(): lax.ppermute(lax.slice_in_dim(block, block.shape[dim] - width, None, axis...]
    scatter-add x1 -> x0, other arithmetic: 13.2 us -> none  [per_device(): jnp.zeros(surface.shape, jnp.float32).at[:, cells_flat].add(contrib)]
    mul x6 -> x0, other arithmetic: 12.6 us -> none  [the longest x3 10.1 us: relax(): west_face * padded_adj[..., :-2, 1:-1]]
    all_to_all x4 -> x1, starting transfers between devices: 18.2 us -> 7.1 us  [per_device(): lax.all_to_all(packed, ('gx', 'gy'), split_axis=0, concat_axis=0, tiled=T...]
    squeeze x10 -> x0, local copies, waits for them, and re-layouts: 10.6 us -> none  [column_factors(): entry = entry + upper_face[level]]
  transfers between devices with their start and end apart: 16 -> 5, of which waited for: 5 -> 3; matrix products, arithmetic and copies ran while one was open for 42% -> 0% of each run, Pallas kernels for 0% -> 23%
where the time goes in v2:
time: 44.4 us; the launch traced here: 44 us
  Pallas kernels  17.7 us (40%)
  starting transfers between devices  16.4 us (37%)
  waiting for transfers between devices  5.74 us (13%)
  local copies, waits for them, and re-layouts  2.76 us (6%)
  between operations  1.39 us (3%)
    pallas_call x1, Pallas kernels, per_device(): pl.pallas_call(inner_kernel, out_shape=(shape(*velocity.shape), ends, end...  10.3 us
    ppermute x4, starting transfers between devices, shift(): return lax.ppermute(value, axis, pairs)  9.3 us
    all_to_all x1, starting transfers between devices, per_device(): lax.all_to_all(packed, ('gx', 'gy'), split_axis=0, concat_axis=0, tiled=T...  7.1 us
    ppermute x4, waiting for transfers between devices, shift(): return lax.ppermute(value, axis, pairs)  4.52 us
    pallas_call x1, Pallas kernels, per_device(): pl.pallas_call(edges_kernel, out_shape=(shape(*velocity.shape), shape(row...  3 us
    unnamed x10, local copies, waits for them, and re-layouts  2.76 us
    pallas_call x1, Pallas kernels, per_device(): pl.pallas_call(pack_kernel, out_shape=(shape(owners, 4 * slots, lanes), p...  2.6 us
    pallas_call x1, Pallas kernels, per_device(): pl.pallas_call(functools.partial(sources_kernel, slots), out_shape=(shape...  1.87 us
  transfers between devices with their start and end apart: 5, of which 3 were waited for; matrix products, arithmetic and copies ran while one was open for 0% of the time, Pallas kernels for 23%

profile of v2, /device:TPU:1, one launch (start us, length us, event | category | flops | bytes accessed | tf_op | source)
XLA Modules:
  0.0 44.0 jit_solution(1327432192371052420)
XLA Ops:
  1.3 0.0 copy-start.2
  1.3 2.6 %pack.1 = (f32[32,16,128]{2,1,0:T(8,128)}, f32[96,128]{1,0:T(8,128)}, f32[96,128]{1,0:T(8,128)}) custom-call(s32[4,8]{1,0:T(4,128)} %bitcast.13, f32[32,3,4,128]{3,2,1,0:T(4,128)} %bitcast.11, s32[4,4,8]{2,1,0:T(4,128)} %bitcast.12, s32[1,1]{1,0:T(1,128)S(6)} %copy.11.ice_hbm, f32[10,96,384]{2,1,0:T(8,128)} %visc_hbm.5, f32[96,384]{1,0:T(8,128)} %fric_hbm.5, ...), custom_call_target="tpu_custom_call" | custom-call | flops 4000000000 | tf_op jit(solution)/shard_map/pack/pallas_call | solution.py:550
  3.9 7.1 %all-to-all-start = ((f32[32,16,128]{2,1,0:T(8,128)}), f32[32,16,128]{2,1,0:T(8,128)S(1)}, u32[]{:S(2)}, u32[]{:S(2)}) async-start(f32[32,16,128]{2,1,0:T(8,128)} %get-tuple-element.14), calls=%async_computation | async-start | bytes 524288 | tf_op jit(solution)/shard_map/all_to_all | solution.py:569
  11.0 3.3 %collective-permute-start = (f32[96,128]{1,0:T(8,128)}, f32[96,128]{1,0:T(8,128)S(1)}, u32[]{:S(2)}, u32[]{:S(2)}) collective-permute-start(f32[96,128]{1,0:T(8,128)} %get-tuple-element.15), channel_id=1, source_target_pairs={{0,1},{1,2},{2,3},{4,5},{5,6},{6,7},{8,9},{9,10},{10,11},{12,13},{... | collective-permute-start | bytes 147464 | tf_op jit(solution)/shard_map/ppermute | solution.py:538
  14.3 1.3 %collective-permute-start.1 = (f32[96,128]{1,0:T(8,128)}, f32[96,128]{1,0:T(8,128)S(1)}, u32[]{:S(2)}, u32[]{:S(2)}) collective-permute-start(f32[96,128]{1,0:T(8,128)} %get-tuple-element.16), channel_id=1, source_target_pairs={{1,0},{2,1},{3,2},{5,4},{6,5},{7,6},{9,8},{10,9},{11,10},{13,12},{... | collective-permute-start | bytes 147464 | tf_op jit(solution)/shard_map/ppermute | solution.py:538
  15.6 1.1 %collective-permute-done.before_any = f32[96,128]{1,0:T(8,128)S(1)} collective-permute-done((f32[96,128]{1,0:T(8,128)}, f32[96,128]{1,0:T(8,128)S(1)}, u32[]{:S(2)}, u32[]{:S(2)}) %collective-permute-start) | collective-permute-done | bytes 49184 | tf_op jit(solution)/shard_map/ppermute | solution.py:538
  16.7 3.5 %collective-permute-done.1.after_any = f32[96,128]{1,0:T(8,128)S(1)} collective-permute-done((f32[96,128]{1,0:T(8,128)}, f32[96,128]{1,0:T(8,128)S(1)}, u32[]{:S(2)}, u32[]{:S(2)}) %collective-permute-start.1) | collective-permute-done | bytes 49184 | tf_op jit(solution)/shard_map/ppermute | solution.py:538
  20.1 1.2 %all-to-all-done = f32[32,16,128]{2,1,0:T(8,128)S(1)} async-done(((f32[32,16,128]{2,1,0:T(8,128)}), f32[32,16,128]{2,1,0:T(8,128)S(1)}, u32[]{:S(2)}, u32[]{:S(2)}) %all-to-all-start) | async-done | bytes 262176 | tf_op jit(solution)/shard_map/all_to_all | solution.py:569
  21.3 0.0 copy-done.2
  21.3 0.0 copy-start
  21.4 1.8 %copy-done = f32[2,10,96,384]{3,2,1,0:T(8,128)S(1)} copy-done((f32[2,10,96,384]{3,2,1,0:T(8,128)S(1)}, f32[2,10,96,384]{3,2,1,0:T(8,128)}, u32[]{:S(2)}) %copy-start) | copy-done | bytes 2949144
  23.2 0.0 copy-start.3
  23.2 0.9 %copy-done.3 = f32[96,384]{1,0:T(8,128)S(1)} copy-done((f32[96,384]{1,0:T(8,128)S(1)}, f32[96,384]{1,0:T(8,128)}, u32[]{:S(2)}) %copy-start.3) | copy-done | bytes 147480
  24.1 0.0 copy-start.4
  24.1 1.9 %sources.1 = (f32[2,4,96,128]{3,2,1,0:T(8,128)S(1)}, f32[12,4,8,128]{3,2,1,0:T(8,128)S(1)}, f32[12,4,8,128]{3,2,1,0:T(8,128)S(1)}, f32[14,4,4,128]{3,2,1,0:T(4,128)S(1)}, f32[14,4,4,128]{3,2,1,0:T(4,128)S(1)}) custom-call(s32[1,1]{1,0:T(1,128)S(6)} %copy.11.ice_hbm, f32[512,128]{1,0:T(8,128)S(1)} %bitcast.10, f32[10,96,384]{2,1,0:T(8,128)S(1)} %copy-done.2, ...), custom_call_target="tpu_custom_call" | custom-call | flops 4000000000 | tf_op jit(solution)/shard_map/sources/pallas_call | solution.py:575
  26.0 2.8 %collective-permute-start.2 = (f32[14,4,4,128]{3,2,1,0:T(4,128)S(1)}, f32[14,4,4,128]{3,2,1,0:T(4,128)S(1)}, u32[]{:S(2)}, u32[]{:S(2)}) collective-permute-start(f32[14,4,4,128]{3,2,1,0:T(4,128)S(1)} %get-tuple-element.19), channel_id=1, source_target_pairs={{0,4},{4,8},{8,12},{12,16},{16,20},{20,24},{24,28},{1,5},{5,9},{9,... | collective-permute-start | bytes 344072 | tf_op jit(solution)/shard_map/ppermute | solution.py:538
  28.8 1.9 %collective-permute-start.3 = (f32[14,4,4,128]{3,2,1,0:T(4,128)S(1)}, f32[14,4,4,128]{3,2,1,0:T(4,128)S(1)}, u32[]{:S(2)}, u32[]{:S(2)}) collective-permute-start(f32[14,4,4,128]{3,2,1,0:T(4,128)S(1)} %get-tuple-element.20), channel_id=1, source_target_pairs={{4,0},{8,4},{12,8},{16,12},{20,16},{24,20},{28,24},{5,1},{9,5},{13... | collective-permute-start | bytes 344072 | tf_op jit(solution)/shard_map/ppermute | solution.py:538
  30.7 0.0 copy-done.4
  30.7 0.0 copy-start.1
  30.7 10.3 %inner.1 = (f32[2,10,96,384]{3,2,1,0:T(8,128)}, f32[2,10,3,8,128]{4,3,2,1,0:T(8,128)S(1)}, f32[2,10,3,8,128]{4,3,2,1,0:T(8,128)S(1)}, f32[2,96,384]{2,1,0:T(8,128)S(1)}) custom-call(s32[1,1]{1,0:T(1,128)S(6)} %copy.11.ice_hbm, f32[10,96,384]{2,1,0:T(8,128)S(1)} %copy-done.2, f32[96,384]{1,0:T(8,128)S(1)} %copy-done.4, ...), custom_call_target="tpu_custom_call" | custom-call | flops 4000000000 | tf_op jit(solution)/shard_map/inner/pallas_call | solution.py:598
  41.0 0.0 collective-permute-done.2.before_ref
  41.0 0.0 collective-permute-done.3.after_ref
  41.0 0.0 copy-done.1
  41.0 3.0 %edges.1 = (f32[2,10,96,384]{3,2,1,0:T(8,128)}, f32[96,384]{1,0:T(8,128)}) custom-call(s32[1,1]{1,0:T(1,128)S(6)} %copy.11.ice_hbm, f32[12,4,8,128]{3,2,1,0:T(8,128)S(1)} %get-tuple-element.17.own_low, f32[12,4,8,128]{3,2,1,0:T(8,128)S(1)} %get-tuple-element.18.own_high, ...), custom_call_target="tpu_custom_call", output_to_operand_aliasing={{0}: (10, {})} | custom-call | flops 4000000000 | tf_op jit(solution)/shard_map/edges/pallas_call | solution.py:621
Async XLA Ops:
  1.3 20.1 %copy-start.2 = (f32[10,96,384]{2,1,0:T(8,128)S(1)}, f32[10,96,384]{2,1,0:T(8,128)}, u32[]{:S(2)}) copy-start(f32[10,96,384]{2,1,0:T(8,128)} %visc_hbm.5) | copy-start | bytes 4423684
  3.9 17.5 %all-to-all-start = ((f32[32,16,128]{2,1,0:T(8,128)}), f32[32,16,128]{2,1,0:T(8,128)S(1)}, u32[]{:S(2)}, u32[]{:S(2)}) async-start(f32[32,16,128]{2,1,0:T(8,128)} %get-tuple-element.14), calls=%async_computation | async-start | bytes 524288 | tf_op jit(solution)/shard_map/all_to_all | solution.py:569
  11.0 5.7 %collective-permute-start = (f32[96,128]{1,0:T(8,128)}, f32[96,128]{1,0:T(8,128)S(1)}, u32[]{:S(2)}, u32[]{:S(2)}) collective-permute-start(f32[96,128]{1,0:T(8,128)} %get-tuple-element.15), channel_id=1, source_target_pairs={{0,1},{1,2},{2,3},{4,5},{5,6},{6,7},{8,9},{9,10},{10,11},{12,13},{... | collective-permute-start | bytes 147464 | tf_op jit(solution)/shard_map/ppermute | solution.py:538
  14.3 5.8 %collective-permute-start.1 = (f32[96,128]{1,0:T(8,128)}, f32[96,128]{1,0:T(8,128)S(1)}, u32[]{:S(2)}, u32[]{:S(2)}) collective-permute-start(f32[96,128]{1,0:T(8,128)} %get-tuple-element.16), channel_id=1, source_target_pairs={{1,0},{2,1},{3,2},{5,4},{6,5},{7,6},{9,8},{10,9},{11,10},{13,12},{... | collective-permute-start | bytes 147464 | tf_op jit(solution)/shard_map/ppermute | solution.py:538
  21.3 1.8 %copy-start = (f32[2,10,96,384]{3,2,1,0:T(8,128)S(1)}, f32[2,10,96,384]{3,2,1,0:T(8,128)}, u32[]{:S(2)}) copy-start(f32[2,10,96,384]{3,2,1,0:T(8,128)} %vel_hbm.5) | copy-start | bytes 8847364
  23.2 0.9 %copy-start.3 = (f32[96,384]{1,0:T(8,128)S(1)}, f32[96,384]{1,0:T(8,128)}, u32[]{:S(2)}) copy-start(f32[96,384]{1,0:T(8,128)} %fric_hbm.5) | copy-start | bytes 442372
  24.1 6.6 %copy-start.4 = (f32[96,384]{1,0:T(8,128)S(1)}, f32[96,384]{1,0:T(8,128)}, u32[]{:S(2)}) copy-start(f32[96,384]{1,0:T(8,128)} %fric_hbm.5) | copy-start | bytes 442372
  26.0 15.0 %collective-permute-start.2 = (f32[14,4,4,128]{3,2,1,0:T(4,128)S(1)}, f32[14,4,4,128]{3,2,1,0:T(4,128)S(1)}, u32[]{:S(2)}, u32[]{:S(2)}) collective-permute-start(f32[14,4,4,128]{3,2,1,0:T(4,128)S(1)} %get-tuple-element.19), channel_id=1, source_target_pairs={{0,4},{4,8},{8,12},{12,16},{16,20},{20,24},{24,28},{1,5},{5,9},{9,... | collective-permute-start | bytes 344072 | tf_op jit(solution)/shard_map/ppermute | solution.py:538
  28.8 12.2 %collective-permute-start.3 = (f32[14,4,4,128]{3,2,1,0:T(4,128)S(1)}, f32[14,4,4,128]{3,2,1,0:T(4,128)S(1)}, u32[]{:S(2)}, u32[]{:S(2)}) collective-permute-start(f32[14,4,4,128]{3,2,1,0:T(4,128)S(1)} %get-tuple-element.20), channel_id=1, source_target_pairs={{4,0},{8,4},{12,8},{16,12},{20,16},{24,20},{28,24},{5,1},{9,5},{13... | collective-permute-start | bytes 344072 | tf_op jit(solution)/shard_map/ppermute | solution.py:538
  30.7 10.3 %copy-start.1 = (f32[2,10,96,384]{3,2,1,0:T(8,128)S(1)}, f32[2,10,96,384]{3,2,1,0:T(8,128)}, u32[]{:S(2)}) copy-start(f32[2,10,96,384]{3,2,1,0:T(8,128)} %vel_hbm.5) | copy-start | bytes 8847364

commit v3 on v2

--- a/solution.py
+++ b/solution.py
@@ -47,6 +47,15 @@
     return jnp.broadcast_to(ref[...], shape).astype(jnp.float32)
 
 
+def is_even(axis):
+    return lax.rem(lax.axis_index(axis), 2) == 0
+
+
+def received(axis, one, two):
+    even = is_even(axis)
+    return jnp.where(even, two, one), jnp.where(even, one, two)
+
+
 def fetch_all(copies):
     for copy in copies:
         copy.start()
@@ -57,23 +66,13 @@
         copy.wait()
 
 
-def pack_kernel(
-    count_hbm, tiles_hbm, cells_hbm, ice_hbm, visc_hbm, fric_hbm, vel_hbm, out_ref, first_ref, last_ref,
-    counts, tiles, cells, ice, visc, fric, vel, sems,
-):
+def pack_kernel(count_hbm, tiles_hbm, cells_hbm, out_ref, counts, tiles, cells, sems):
     owners_y, owners_x = counts.shape
     slots, lanes = tiles.shape[2], tiles.shape[3]
-    layers, rows, cols = visc_hbm.shape
-    top = vel_hbm.at[:, vel_hbm.shape[1] - 1]
-    ends = (pl.ds(0, lanes), pl.ds(cols - lanes, lanes))
-    pairs = [(count_hbm, counts), (cells_hbm, cells), (tiles_hbm, tiles), (ice_hbm, ice)]
-    for side, span in enumerate(ends):
-        pairs.append((visc_hbm.at[:, :, span], visc.at[side]))
-        pairs.append((fric_hbm.at[:, span], fric.at[side]))
-        pairs.append((top.at[:, :, span], vel.at[side]))
+    pairs = [(count_hbm, counts), (cells_hbm, cells), (tiles_hbm, tiles)]
     copies = [pltpu.make_async_copy(a, b, sems.at[n]) for n, (a, b) in enumerate(pairs)]
     fetch_all(copies)
-    wait_all(copies[:3])
+    wait_all(copies)
     lane = lanes_of((slots, lanes))
     slot = lax.broadcasted_iota(jnp.int32, (slots, lanes), 0)
     zero = jnp.zeros((slots, lanes), jnp.float32)
@@ -104,7 +103,19 @@
             meta = jnp.where(lane < 16, after, jnp.where(lane >= lanes - 16, before, owns[oy]))
             out_ref[ox * owners_y + oy, 3 * slots : 4 * slots] = meta
 
-    wait_all(copies[3:])
+
+def columns_kernel(ice_hbm, visc_hbm, fric_hbm, vel_hbm, one_ref, two_ref, ice, visc, fric, vel, sems):
+    layers, rows, cols = visc_hbm.shape
+    lanes = one_ref.shape[1]
+    top = vel_hbm.at[:, vel_hbm.shape[1] - 1]
+    pairs = [(ice_hbm, ice)]
+    for side, span in enumerate((pl.ds(0, lanes), pl.ds(cols - lanes, lanes))):
+        pairs.append((visc_hbm.at[:, :, span], visc.at[side]))
+        pairs.append((fric_hbm.at[:, span], fric.at[side]))
+        pairs.append((top.at[:, :, span], vel.at[side]))
+    copies = [pltpu.make_async_copy(a, b, sems.at[n]) for n, (a, b) in enumerate(pairs)]
+    fetch_all(copies)
+    wait_all(copies)
     lane = lanes_of((rows, lanes))
     icefield = filled(ice, (rows, lanes))
     first = jnp.zeros((rows, lanes), jnp.float32)
@@ -122,8 +133,9 @@
         first = jnp.where(here, pltpu.roll(mine[0], 3 * k, 1), first)
         there = (lane >= lanes - 3 - 3 * k) & (lane < lanes - 3 * k)
         last = jnp.where(there, pltpu.roll(mine[1], (lanes - 3 * k) % lanes, 1), last)
-    first_ref[...] = first
-    last_ref[...] = last
+    even = is_even("gy")
+    one_ref[...] = jnp.where(even, last, first)
+    two_ref[...] = jnp.where(even, first, last)
 
 
 def side_tile(before, after, k):
@@ -208,14 +220,14 @@
 
 
 def sources_kernel(
-    slots, ice_hbm, tiles_ref, visc_hbm, fric_hbm, vel_hbm, before_any, after_any,
-    rhs_ref, low_ref, high_ref, xlow_ref, xhigh_ref, ice, visc, fric, vel, before_ref, after_ref, sems,
+    slots, ice_hbm, tiles_ref, visc_hbm, fric_hbm, vel_hbm, one_any, two_any,
+    rhs_ref, low_ref, high_ref, xone_ref, xtwo_ref, ice, visc, fric, vel, one, two, sems,
 ):
     layers, rows, cols = visc_hbm.shape
     lanes = tiles_ref.shape[1]
     owners = tiles_ref.shape[0] // (4 * slots)
     blocks = cols // lanes
-    pairs = [(vel_hbm.at[:, layers - 1], vel), (before_any, before_ref), (after_any, after_ref), (ice_hbm, ice)]
+    pairs = [(vel_hbm.at[:, layers - 1], vel), (one_any, one), (two_any, two), (ice_hbm, ice)]
     for side, at in enumerate((0, rows - 8)):
         pairs.append((visc_hbm.at[:, pl.ds(at, 8), :], visc.at[side]))
         pairs.append((fric_hbm.at[pl.ds(at, 8), :], fric.at[side]))
@@ -236,10 +248,15 @@
         cell = jnp.broadcast_to(column.astype(jnp.int32), (count, rows))
         return (cell == row * blocks + b).astype(jnp.bfloat16)
 
+    even = is_even("gx")
+
+    def send(k, t, low, high):
+        xone_ref[k, t] = jnp.where(even, high, low)
+        xtwo_ref[k, t] = jnp.where(even, low, high)
+
     def put(c, t, plane):
         rhs_ref[c, t] = plane
-        xlow_ref[layers + 2 + c, t] = plane[0:4]
-        xhigh_ref[layers + 2 + c, t] = plane[rows - 4 : rows]
+        send(layers + 2 + c, t, plane[0:4], plane[rows - 4 : rows])
 
     own = meta[:, lanes // 2 : lanes // 2 + 1]
     marks = jnp.concatenate([onehot(own, b) for b in range(blocks)], axis=1)
@@ -259,8 +276,9 @@
             put(c, b, total[b * rows : (b + 1) * rows, c * lanes : (c + 1) * lanes])
 
     wait_all(copies[1:3])
+    before_ref, after_ref = received("gy", one[...], two[...])
     beside = jnp.concatenate(
-        [side_tile(before_ref[...], after_ref[...], layers + 2 + c) for c in range(2)], axis=1
+        [side_tile(before_ref, after_ref, layers + 2 + c) for c in range(2)], axis=1
     )
     mark_after = onehot(meta[:, 8:9], 0)
     mark_before = onehot(meta[:, lanes - 8 : lanes - 7], blocks - 1)
@@ -290,18 +308,17 @@
                 low, high = icefield, icefield
             low_ref[k, t] = low
             high_ref[k, t] = high
-            xlow_ref[k, t] = low[0:4]
-            xhigh_ref[k, t] = high[4:8]
+            send(k, t, low[0:4], high[4:8])
 
 
 def inner_kernel(
-    ice_hbm, visc_hbm, fric_hbm, before_any, after_any, rhs_any, adj_hbm, low_ref, high_ref, base_ref,
-    ice, field, before, after, rhs, coef, one, two, three, sem_in, sem_out,
+    ice_hbm, visc_hbm, fric_hbm, one_any, two_any, rhs_any, adj_hbm, low_ref, high_ref, base_ref,
+    ice, field, swap_one, swap_two, rhs, coef, one, two, three, sem_in, sem_out,
 ):
     steps, tiles, _, layers, _, lanes = coef.shape
     rows = three.shape[3]
     middle = pl.ds(MARGIN, rows)
-    pairs = [(ice_hbm, ice), (before_any, before), (after_any, after)]
+    pairs = [(ice_hbm, ice), (one_any, swap_one), (two_any, swap_two)]
     for t in range(tiles - 1):
         span = pl.ds(t * lanes, lanes)
         pairs.append((visc_hbm.at[:, :, span], field.at[pl.ds(0, layers), t, middle, :]))
@@ -318,8 +335,9 @@
     icefield = filled(ice, (rows, lanes))
     for t in range(tiles - 1):
         field[layers + 1, t, middle] = icefield
+    before, after = received("gy", swap_one[...], swap_two[...])
     for k in range(layers + 2):
-        field[k, tiles - 1, middle] = side_tile(before[...], after[...], k)
+        field[k, tiles - 1, middle] = side_tile(before, after, k)
     wait_all(copies[3:-1])
 
     def factors(r, carry):
@@ -334,7 +352,7 @@
             factor_columns(layers, t, tiles, load, store)
         return carry
 
-    lax.fori_loop(0, steps, factors, 0)
+    lax.fori_loop(0, steps, factors, 0, unroll=3)
     wait_all(copies[-1:])
     sublane = lax.broadcasted_iota(jnp.int32, (8, lanes), 0)
 
@@ -377,7 +395,7 @@
             relax_columns(layers, t, tiles, old, rhs_of(r, t), coef_of(r, t), store)
         return carry
 
-    lax.fori_loop(0, steps, second_sweep, 0, unroll=2)
+    lax.fori_loop(0, steps, second_sweep, 0, unroll=4)
     wrap(two)
 
     def result(t):
@@ -397,7 +415,7 @@
             relax_columns(layers, t, tiles, old, rhs_of(r, t), coef_of(r, t), store)
             return carry
 
-        lax.fori_loop(0, steps, third_sweep, 0, unroll=4)
+        lax.fori_loop(0, steps, third_sweep, 0, unroll=12)
         result(t).start()
         for n in range(2):
             for k in range(layers):
@@ -410,7 +428,7 @@
 
 
 def edges_kernel(
-    ice_hbm, own_low, own_high, before_ref, after_ref, rhs_ref, low_ref, high_ref, base_ref, vel_hbm, adj_in,
+    ice_hbm, own_low, own_high, one_ref, two_ref, rhs_ref, low_ref, high_ref, base_ref, vel_hbm, adj_in,
     adj_hbm, grad_ref, ice, field, coefs, rhs, one, two, patch, vel, sem_in, sem_out,
 ):
     tiles, _, layers = coefs.shape[1:4]
@@ -424,17 +442,18 @@
     fetch_all(fetches)
     for k in range(layers + 4):
         for t in range(tiles):
+            before, after = received("gx", one_ref[k, t], two_ref[k, t])
             if k < layers + 2:
-                field[0, k, t, 0:4] = before_ref[k, t]
+                field[0, k, t, 0:4] = before
                 field[0, k, t, 4:12] = own_low[k, t]
                 field[1, k, t, 4:12] = own_high[k, t]
-                field[1, k, t, 12:16] = after_ref[k, t]
+                field[1, k, t, 12:16] = after
             else:
                 n = k - layers - 2
-                rhs[0, n, t, 0:4] = before_ref[k, t]
+                rhs[0, n, t, 0:4] = before
                 rhs[0, n, t, 4:12] = rhs_ref[n, t, 0:8]
                 rhs[1, n, t, 4:12] = rhs_ref[n, t, rows - 8 : rows]
-                rhs[1, n, t, 12:16] = after_ref[k, t]
+                rhs[1, n, t, 12:16] = after
     starts = (2, 6)
 
     def at(ref, start):
@@ -532,9 +551,10 @@
     def grant(mib):
         return pltpu.CompilerParams(vmem_limit_bytes=int(mib * MIB))
 
-    def shift(value, axis, step):
-        size = lax.axis_size(axis)
-        pairs = [(i, i + step) for i in range(size) if 0 <= i + step < size]
+    def swap(value, axis, first):
+        pairs = []
+        for i in range(first, lax.axis_size(axis) - 1, 2):
+            pairs += [(i, i + 1), (i + 1, i)]
         return lax.ppermute(value, axis, pairs)
 
     tiles_in = jnp.transpose(obs_tiles.reshape(owners, slots, channels, lanes), (0, 2, 1, 3))
@@ -547,32 +567,44 @@
     plane = shape(rows, lanes)
     hbm = whole(pltpu.HBM)
     anywhere = whole(pl.ANY)
-    packed, yfirst, ylast = pl.pallas_call(
+    packed = pl.pallas_call(
         pack_kernel,
-        out_shape=(shape(owners, 4 * slots, lanes), plane, plane),
-        in_specs=[hbm] * 7,
-        out_specs=(whole(),) * 3,
+        out_shape=shape(owners, 4 * slots, lanes),
+        in_specs=[hbm] * 3,
+        out_specs=whole(),
         scratch_shapes=[
             pltpu.VMEM(counts_in.shape, i32),
             pltpu.VMEM(tiles_in.shape, f32),
             pltpu.VMEM(cells_in.shape, i32),
+            pltpu.SemaphoreType.DMA((3,)),
+        ],
+        compiler_params=grant(62.5),
+        cost_estimate=pl.CostEstimate(flops=4 * 10**9, transcendentals=0, bytes_accessed=0),
+        name="pack",
+    )(counts_in, tiles_in, cells_in)
+    arrived = lax.all_to_all(packed, ("gx", "gy"), split_axis=0, concat_axis=0, tiled=True)
+    ysend_one, ysend_two = pl.pallas_call(
+        columns_kernel,
+        out_shape=(plane, plane),
+        in_specs=[hbm] * 4,
+        out_specs=(whole(), whole()),
+        scratch_shapes=[
             pltpu.VMEM((1, 1), i32),
             pltpu.VMEM((2, layers, rows, lanes), f32),
             pltpu.VMEM((2, rows, lanes), f32),
             pltpu.VMEM((2, 2, rows, lanes), f32),
-            pltpu.SemaphoreType.DMA((10,)),
+            pltpu.SemaphoreType.DMA((7,)),
         ],
         compiler_params=grant(62.5),
         cost_estimate=pl.CostEstimate(flops=4 * 10**9, transcendentals=0, bytes_accessed=0),
-        name="pack",
-    )(counts_in, tiles_in, cells_in, ice_mask, viscosity, friction, velocity)
-    arrived = lax.all_to_all(packed, ("gx", "gy"), split_axis=0, concat_axis=0, tiled=True)
-    ybefore = shift(ylast, "gy", 1)
-    yafter = shift(yfirst, "gy", -1)
+        name="columns",
+    )(ice_mask, viscosity, friction, velocity)
+    yone = swap(ysend_one, "gy", 0)
+    ytwo = swap(ysend_two, "gy", 1)
 
     own = shape(layers + 2, tiles, 8, lanes)
     edge = shape(layers + 4, tiles, 4, lanes)
-    rhs, own_low, own_high, xlow, xhigh = pl.pallas_call(
+    rhs, own_low, own_high, xsend_one, xsend_two = pl.pallas_call(
         functools.partial(sources_kernel, slots),
         out_shape=(shape(2, tiles, rows, lanes), own, own, edge, edge),
         in_specs=[hbm, whole(), hbm, hbm, hbm, anywhere, anywhere],
@@ -586,12 +618,12 @@
             pltpu.VMEM((rows, lanes), f32),
             pltpu.SemaphoreType.DMA((8,)),
         ],
-        compiler_params=grant(12 + (owners * slots) // 64),
+        compiler_params=grant(52),
         cost_estimate=pl.CostEstimate(flops=4 * 10**9, transcendentals=0, bytes_accessed=0),
         name="sources",
-    )(ice_mask, arrived.reshape(owners * 4 * slots, lanes), viscosity, friction, velocity, ybefore, yafter)
-    xbefore = shift(xhigh, "gx", 1)
-    xafter = shift(xlow, "gx", -1)
+    )(ice_mask, arrived.reshape(owners * 4 * slots, lanes), viscosity, friction, velocity, yone, ytwo)
+    xone = swap(xsend_one, "gx", 0)
+    xtwo = swap(xsend_two, "gx", 1)
 
     ends = shape(2, layers, blocks, 8, lanes)
     wide = pltpu.VMEM((2, layers, tiles, steps + 2, 8, lanes), f32)
@@ -616,7 +648,7 @@
         compiler_params=grant(30),
         cost_estimate=pl.CostEstimate(flops=4 * 10**9, transcendentals=0, bytes_accessed=0),
         name="inner",
-    )(ice_mask, viscosity, friction, ybefore, yafter, rhs)
+    )(ice_mask, viscosity, friction, yone, ytwo, rhs)
 
     return pl.pallas_call(
         edges_kernel,
@@ -639,7 +671,7 @@
         compiler_params=grant(14),
         cost_estimate=pl.CostEstimate(flops=4 * 10**9, transcendentals=0, bytes_accessed=0),
         name="edges",
-    )(ice_mask, own_low, own_high, xbefore, xafter, rhs, low, high, base, velocity, adjoint)
+    )(ice_mask, own_low, own_high, xone, xtwo, rhs, low, high, base, velocity, adjoint)
 
 
 def solution(mesh):

time: 44.4 us -> 38 us (0.86)
  starting transfers between devices: 16.4 us -> 12.7 us
  local copies, waits for them, and re-layouts: 2.76 us -> 0.02 us
  Pallas kernels: 17.7 us -> 18.7 us
  waiting for transfers between devices: 5.74 us -> 4.91 us
    ppermute x4, starting transfers between devices: 9.3 us -> 5.58 us  [swap(): return lax.ppermute(value, axis, pairs)]
    unnamed x10 -> x6, local copies, waits for them, and re-layouts: 2.76 us -> 0.02 us
    ppermute x4, waiting for transfers between devices: 4.52 us -> 2.34 us  [swap(): return lax.ppermute(value, axis, pairs)]
    pallas_call x1 -> x2, Pallas kernels: 2.6 us -> 4.43 us  [the longest x1 2.39 us: per_device(): pl.pallas_call(columns_kernel, out_shape=(plane, plane), in_specs=[hbm] *...]
    pallas_call x1, Pallas kernels: 10.3 us -> 8.65 us  [per_device(): pl.pallas_call(inner_kernel, out_shape=(shape(*velocity.shape), ends, end...]
    all_to_all x1, waiting for transfers between devices: 1.23 us -> 2.57 us  [per_device(): lax.all_to_all(packed, ('gx', 'gy'), split_axis=0, concat_axis=0, tiled=T...]
    pallas_call x1, Pallas kernels: 1.87 us -> 2.56 us  [per_device(): pl.pallas_call(functools.partial(sources_kernel, slots), out_shape=(shape...]
  transfers between devices with their start and end apart: 5 -> 5, of which waited for: 3 -> 2; matrix products, arithmetic and copies ran while one was open for 0% -> 0% of each run, Pallas kernels for 23% -> 29%
where the time goes in v3:
time: 38 us; the launch traced here: 37.7 us
  Pallas kernels  18.7 us (49%)
  starting transfers between devices  12.7 us (33%)
  waiting for transfers between devices  4.91 us (13%)
  between operations  1.38 us (4%)
    pallas_call x1, Pallas kernels, per_device(): pl.pallas_call(inner_kernel, out_shape=(shape(*velocity.shape), ends, end...  8.65 us
    all_to_all x1, starting transfers between devices, per_device(): lax.all_to_all(packed, ('gx', 'gy'), split_axis=0, concat_axis=0, tiled=T...  7.1 us
    ppermute x4, starting transfers between devices, swap(): return lax.ppermute(value, axis, pairs)  5.58 us
    pallas_call x1, Pallas kernels, per_device(): pl.pallas_call(edges_kernel, out_shape=(shape(*velocity.shape), shape(row...  3.05 us
    all_to_all x1, waiting for transfers between devices, per_device(): lax.all_to_all(packed, ('gx', 'gy'), split_axis=0, concat_axis=0, tiled=T...  2.57 us
    pallas_call x1, Pallas kernels, per_device(): pl.pallas_call(functools.partial(sources_kernel, slots), out_shape=(shape...  2.56 us
    pallas_call x1, Pallas kernels, per_device(): pl.pallas_call(columns_kernel, out_shape=(plane, plane), in_specs=[hbm] *...  2.39 us
    ppermute x4, waiting for transfers between devices, swap(): return lax.ppermute(value, axis, pairs)  2.34 us
  transfers between devices with their start and end apart: 5, of which 2 were waited for; matrix products, arithmetic and copies ran while one was open for 0% of the time, Pallas kernels for 29%

profile of v3, /device:TPU:1, one launch (start us, length us, event | category | flops | bytes accessed | tf_op | source)
XLA Modules:
  0.0 37.7 jit_solution(1623846877107656612)
XLA Ops:
  0.6 2.0 %pack.1 = f32[32,16,128]{2,1,0:T(8,128)} custom-call(s32[4,8]{1,0:T(4,128)} %bitcast.13, f32[32,3,4,128]{3,2,1,0:T(4,128)} %bitcast.11, s32[4,4,8]{2,1,0:T(4,128)} %bitcast.12), custom_call_target="tpu_custom_call" | custom-call | flops 4000000000 | tf_op jit(solution)/shard_map/pack/pallas_call | solution.py:570
  2.7 7.1 %all-to-all-start = ((f32[32,16,128]{2,1,0:T(8,128)}), f32[32,16,128]{2,1,0:T(8,128)S(1)}, u32[]{:S(2)}, u32[]{:S(2)}) async-start(f32[32,16,128]{2,1,0:T(8,128)} %pack.1), calls=%async_computation | async-start | bytes 524288 | tf_op jit(solution)/shard_map/all_to_all | solution.py:585
  10.4 0.0 copy-start.2
  10.4 2.4 %columns.1 = (f32[96,128]{1,0:T(8,128)}, f32[96,128]{1,0:T(8,128)}) custom-call(s32[1,1]{1,0:T(1,128)S(6)} %copy.11.ice_hbm, f32[10,96,384]{2,1,0:T(8,128)} %visc_hbm.5, f32[96,384]{1,0:T(8,128)} %fric_hbm.5, f32[2,10,96,384]{3,2,1,0:T(8,128)} %vel_hbm.5), custom_call_target="tpu_custom_call" | custom-call | flops 4000000000 | tf_op jit(solution)/shard_map/columns/pallas_call | solution.py:586
  12.8 1.5 %collective-permute-start = (f32[96,128]{1,0:T(8,128)}, f32[96,128]{1,0:T(8,128)S(1)}, u32[]{:S(2)}, u32[]{:S(2)}) collective-permute-start(f32[96,128]{1,0:T(8,128)} %get-tuple-element.13), channel_id=1, source_target_pairs={{0,1},{1,0},{2,3},{3,2},{4,5},{5,4},{6,7},{7,6},{8,9},{9,8},{10,11... | collective-permute-start | bytes 147464 | tf_op jit(solution)/shard_map/ppermute | solution.py:558
  14.3 0.7 %collective-permute-start.1 = (f32[96,128]{1,0:T(8,128)}, f32[96,128]{1,0:T(8,128)S(1)}, u32[]{:S(2)}, u32[]{:S(2)}) collective-permute-start(f32[96,128]{1,0:T(8,128)} %get-tuple-element.14), channel_id=1, source_target_pairs={{1,2},{2,1},{5,6},{6,5},{9,10},{10,9},{13,14},{14,13},{17,18},{18,... | collective-permute-start | bytes 147464 | tf_op jit(solution)/shard_map/ppermute | solution.py:558
  15.0 2.3 %collective-permute-done.one_any = f32[96,128]{1,0:T(8,128)S(1)} collective-permute-done((f32[96,128]{1,0:T(8,128)}, f32[96,128]{1,0:T(8,128)S(1)}, u32[]{:S(2)}, u32[]{:S(2)}) %collective-permute-start) | collective-permute-done | bytes 49184 | tf_op jit(solution)/shard_map/ppermute | solution.py:558
  17.3 0.0 collective-permute-done.1.two_any
  17.3 2.6 %all-to-all-done = f32[32,16,128]{2,1,0:T(8,128)S(1)} async-done(((f32[32,16,128]{2,1,0:T(8,128)}), f32[32,16,128]{2,1,0:T(8,128)S(1)}, u32[]{:S(2)}, u32[]{:S(2)}) %all-to-all-start) | async-done | bytes 262176 | tf_op jit(solution)/shard_map/all_to_all | solution.py:585
  19.9 0.0 copy-done.2
  19.9 0.0 copy-start.1
  19.9 2.6 %sources.1 = (f32[2,4,96,128]{3,2,1,0:T(8,128)S(1)}, f32[12,4,8,128]{3,2,1,0:T(8,128)S(1)}, f32[12,4,8,128]{3,2,1,0:T(8,128)S(1)}, f32[14,4,4,128]{3,2,1,0:T(4,128)S(1)}, f32[14,4,4,128]{3,2,1,0:T(4,128)S(1)}) custom-call(s32[1,1]{1,0:T(1,128)S(6)} %copy.11.ice_hbm, f32[512,128]{1,0:T(8,128)S(1)} %bitcast.10, f32[10,96,384]{2,1,0:T(8,128)} %visc_hbm.5, ...), custom_call_target="tpu_custom_call" | custom-call | flops 4000000000 | tf_op jit(solution)/shard_map/sources/pallas_call | solution.py:607
  22.4 0.4 %collective-permute-start.2 = (f32[14,4,4,128]{3,2,1,0:T(4,128)S(1)}, f32[14,4,4,128]{3,2,1,0:T(4,128)S(1)}, u32[]{:S(2)}, u32[]{:S(2)}) collective-permute-start(f32[14,4,4,128]{3,2,1,0:T(4,128)S(1)} %get-tuple-element.17), channel_id=1, source_target_pairs={{0,4},{4,0},{8,12},{12,8},{16,20},{20,16},{24,28},{28,24},{1,5},{5... | collective-permute-start | bytes 344072 | tf_op jit(solution)/shard_map/ppermute | solution.py:558
  22.9 3.0 %collective-permute-start.3 = (f32[14,4,4,128]{3,2,1,0:T(4,128)S(1)}, f32[14,4,4,128]{3,2,1,0:T(4,128)S(1)}, u32[]{:S(2)}, u32[]{:S(2)}) collective-permute-start(f32[14,4,4,128]{3,2,1,0:T(4,128)S(1)} %get-tuple-element.18), channel_id=1, source_target_pairs={{4,8},{8,4},{12,16},{16,12},{20,24},{24,20},{5,9},{9,5},{13,17},{1... | collective-permute-start | bytes 344072 | tf_op jit(solution)/shard_map/ppermute | solution.py:558
  25.9 0.0 copy-done.1
  25.9 0.0 copy-start
  26.0 8.7 %inner.1 = (f32[2,10,96,384]{3,2,1,0:T(8,128)}, f32[2,10,3,8,128]{4,3,2,1,0:T(8,128)S(1)}, f32[2,10,3,8,128]{4,3,2,1,0:T(8,128)S(1)}, f32[2,96,384]{2,1,0:T(8,128)S(1)}) custom-call(s32[1,1]{1,0:T(1,128)S(6)} %copy.11.ice_hbm, f32[10,96,384]{2,1,0:T(8,128)S(1)} %copy-done.1, f32[96,384]{1,0:T(8,128)S(1)} %copy-done.2, ...), custom_call_target="tpu_custom_call" | custom-call | flops 4000000000 | tf_op jit(solution)/shard_map/inner/pallas_call | solution.py:630
  34.6 0.0 collective-permute-done.2.one_ref
  34.6 0.0 collective-permute-done.3.two_ref
  34.6 0.0 copy-done
  34.6 3.1 %edges.1 = (f32[2,10,96,384]{3,2,1,0:T(8,128)}, f32[96,384]{1,0:T(8,128)}) custom-call(s32[1,1]{1,0:T(1,128)S(6)} %copy.11.ice_hbm, f32[12,4,8,128]{3,2,1,0:T(8,128)S(1)} %get-tuple-element.15.own_low, f32[12,4,8,128]{3,2,1,0:T(8,128)S(1)} %get-tuple-element.16.own_high, ...), custom_call_target="tpu_custom_call", output_to_operand_aliasing={{0}: (10, {})} | custom-call | flops 4000000000 | tf_op jit(solution)/shard_map/edges/pallas_call | solution.py:653
Async XLA Ops:
  2.7 17.2 %all-to-all-start = ((f32[32,16,128]{2,1,0:T(8,128)}), f32[32,16,128]{2,1,0:T(8,128)S(1)}, u32[]{:S(2)}, u32[]{:S(2)}) async-start(f32[32,16,128]{2,1,0:T(8,128)} %pack.1), calls=%async_computation | async-start | bytes 524288 | tf_op jit(solution)/shard_map/all_to_all | solution.py:585
  10.4 9.4 %copy-start.2 = (f32[96,384]{1,0:T(8,128)S(1)}, f32[96,384]{1,0:T(8,128)}, u32[]{:S(2)}) copy-start(f32[96,384]{1,0:T(8,128)} %fric_hbm.5) | copy-start | bytes 442372
  12.8 4.4 %collective-permute-start = (f32[96,128]{1,0:T(8,128)}, f32[96,128]{1,0:T(8,128)S(1)}, u32[]{:S(2)}, u32[]{:S(2)}) collective-permute-start(f32[96,128]{1,0:T(8,128)} %get-tuple-element.13), channel_id=1, source_target_pairs={{0,1},{1,0},{2,3},{3,2},{4,5},{5,4},{6,7},{7,6},{8,9},{9,8},{10,11... | collective-permute-start | bytes 147464 | tf_op jit(solution)/shard_map/ppermute | solution.py:558
  14.3 3.0 %collective-permute-start.1 = (f32[96,128]{1,0:T(8,128)}, f32[96,128]{1,0:T(8,128)S(1)}, u32[]{:S(2)}, u32[]{:S(2)}) collective-permute-start(f32[96,128]{1,0:T(8,128)} %get-tuple-element.14), channel_id=1, source_target_pairs={{1,2},{2,1},{5,6},{6,5},{9,10},{10,9},{13,14},{14,13},{17,18},{18,... | collective-permute-start | bytes 147464 | tf_op jit(solution)/shard_map/ppermute | solution.py:558
  19.9 6.1 %copy-start.1 = (f32[10,96,384]{2,1,0:T(8,128)S(1)}, f32[10,96,384]{2,1,0:T(8,128)}, u32[]{:S(2)}) copy-start(f32[10,96,384]{2,1,0:T(8,128)} %visc_hbm.5) | copy-start | bytes 4423684
  22.4 12.2 %collective-permute-start.2 = (f32[14,4,4,128]{3,2,1,0:T(4,128)S(1)}, f32[14,4,4,128]{3,2,1,0:T(4,128)S(1)}, u32[]{:S(2)}, u32[]{:S(2)}) collective-permute-start(f32[14,4,4,128]{3,2,1,0:T(4,128)S(1)} %get-tuple-element.17), channel_id=1, source_target_pairs={{0,4},{4,0},{8,12},{12,8},{16,20},{20,16},{24,28},{28,24},{1,5},{5... | collective-permute-start | bytes 344072 | tf_op jit(solution)/shard_map/ppermute | solution.py:558
  22.9 11.7 %collective-permute-start.3 = (f32[14,4,4,128]{3,2,1,0:T(4,128)S(1)}, f32[14,4,4,128]{3,2,1,0:T(4,128)S(1)}, u32[]{:S(2)}, u32[]{:S(2)}) collective-permute-start(f32[14,4,4,128]{3,2,1,0:T(4,128)S(1)} %get-tuple-element.18), channel_id=1, source_target_pairs={{4,8},{8,4},{12,16},{16,12},{20,24},{24,20},{5,9},{9,5},{13,17},{1... | collective-permute-start | bytes 344072 | tf_op jit(solution)/shard_map/ppermute | solution.py:558
  25.9 8.7 %copy-start = (f32[2,10,96,384]{3,2,1,0:T(8,128)S(1)}, f32[2,10,96,384]{3,2,1,0:T(8,128)}, u32[]{:S(2)}) copy-start(f32[2,10,96,384]{3,2,1,0:T(8,128)} %vel_hbm.5) | copy-start | bytes 8847364

commit v4 on v3

--- a/solution.py
+++ b/solution.py
@@ -221,18 +221,25 @@
 
 def sources_kernel(
     slots, ice_hbm, tiles_ref, visc_hbm, fric_hbm, vel_hbm, one_any, two_any,
-    rhs_ref, low_ref, high_ref, xone_ref, xtwo_ref, ice, visc, fric, vel, one, two, sems,
+    rhs_ref, field, low_ref, high_ref, xone_ref, xtwo_ref, ice, vel, one, two, sems,
 ):
     layers, rows, cols = visc_hbm.shape
     lanes = tiles_ref.shape[1]
     owners = tiles_ref.shape[0] // (4 * slots)
     blocks = cols // lanes
+    middle = pl.ds(MARGIN, rows)
     pairs = [(vel_hbm.at[:, layers - 1], vel), (one_any, one), (two_any, two), (ice_hbm, ice)]
-    for side, at in enumerate((0, rows - 8)):
-        pairs.append((visc_hbm.at[:, pl.ds(at, 8), :], visc.at[side]))
-        pairs.append((fric_hbm.at[pl.ds(at, 8), :], fric.at[side]))
+    for t in range(blocks):
+        span = pl.ds(t * lanes, lanes)
+        pairs.append((visc_hbm.at[:, :, span], field.at[pl.ds(0, layers), t, middle, :]))
+        pairs.append((fric_hbm.at[:, span], field.at[layers, t, middle, :]))
     copies = [pltpu.make_async_copy(a, b, sems.at[n]) for n, (a, b) in enumerate(pairs)]
     fetch_all(copies)
+    edge = jnp.zeros((MARGIN, lanes), jnp.float32)
+    for k in range(layers):
+        for t in range(blocks + 1):
+            field[k, t, 0:MARGIN] = edge
+            field[k, t, MARGIN + rows : 2 * MARGIN + rows] = edge
 
     def channel(c):
         return jnp.concatenate(
@@ -275,10 +282,16 @@
         for b in range(blocks):
             put(c, b, total[b * rows : (b + 1) * rows, c * lanes : (c + 1) * lanes])
 
-    wait_all(copies[1:3])
-    before_ref, after_ref = received("gy", one[...], two[...])
+    wait_all(copies[1:4])
+    icefield = filled(ice, (rows, lanes))
+    from_before, from_after = received("gy", one[...], two[...])
+    for k in range(layers + 2):
+        field[k, blocks, middle] = side_tile(from_before, from_after, k)
+        for t in range(blocks):
+            if k == layers + 1:
+                field[k, t, middle] = icefield
     beside = jnp.concatenate(
-        [side_tile(before_ref, after_ref, layers + 2 + c) for c in range(2)], axis=1
+        [side_tile(from_before, from_after, layers + 2 + c) for c in range(2)], axis=1
     )
     mark_after = onehot(meta[:, 8:9], 0)
     mark_before = onehot(meta[:, lanes - 8 : lanes - 7], blocks - 1)
@@ -292,54 +305,19 @@
     for c in range(2):
         put(c, blocks, side[:, c * lanes : (c + 1) * lanes])
 
-    wait_all(copies[3:])
-    icefield = filled(ice, (8, lanes))
+    wait_all(copies[4:])
     for k in range(layers + 2):
         for t in range(blocks + 1):
-            span = slice(t * lanes, (t + 1) * lanes)
-            if t == blocks:
-                low = side_tile(before_ref[0:8], after_ref[0:8], k)
-                high = side_tile(before_ref[rows - 8 : rows], after_ref[rows - 8 : rows], k)
-            elif k < layers:
-                low, high = visc[0, k, :, span], visc[1, k, :, span]
-            elif k == layers:
-                low, high = fric[0, :, span], fric[1, :, span]
-            else:
-                low, high = icefield, icefield
+            low = field[k, t, MARGIN : MARGIN + 8]
+            high = field[k, t, MARGIN + rows - 8 : MARGIN + rows]
             low_ref[k, t] = low
             high_ref[k, t] = high
             send(k, t, low[0:4], high[4:8])
 
 
-def inner_kernel(
-    ice_hbm, visc_hbm, fric_hbm, one_any, two_any, rhs_any, adj_hbm, low_ref, high_ref, base_ref,
-    ice, field, swap_one, swap_two, rhs, coef, one, two, three, sem_in, sem_out,
-):
+def inner_kernel(field, rhs, adj_hbm, low_ref, high_ref, base_ref, coef, one, two, three, sem_out):
     steps, tiles, _, layers, _, lanes = coef.shape
     rows = three.shape[3]
-    middle = pl.ds(MARGIN, rows)
-    pairs = [(ice_hbm, ice), (one_any, swap_one), (two_any, swap_two)]
-    for t in range(tiles - 1):
-        span = pl.ds(t * lanes, lanes)
-        pairs.append((visc_hbm.at[:, :, span], field.at[pl.ds(0, layers), t, middle, :]))
-        pairs.append((fric_hbm.at[:, span], field.at[layers, t, middle, :]))
-    pairs.append((rhs_any, rhs))
-    copies = [pltpu.make_async_copy(a, b, sem_in.at[n]) for n, (a, b) in enumerate(pairs)]
-    fetch_all(copies)
-    edge = jnp.zeros((MARGIN, lanes), jnp.float32)
-    for k in range(layers):
-        for t in range(tiles):
-            field[k, t, 0:MARGIN] = edge
-            field[k, t, MARGIN + rows : 2 * MARGIN + rows] = edge
-    wait_all(copies[:3])
-    icefield = filled(ice, (rows, lanes))
-    for t in range(tiles - 1):
-        field[layers + 1, t, middle] = icefield
-    before, after = received("gy", swap_one[...], swap_two[...])
-    for k in range(layers + 2):
-        field[k, tiles - 1, middle] = side_tile(before, after, k)
-    wait_all(copies[3:-1])
-
     def factors(r, carry):
         for t in range(tiles):
 
@@ -353,7 +331,7 @@
         return carry
 
     lax.fori_loop(0, steps, factors, 0, unroll=3)
-    wait_all(copies[-1:])
+
     sublane = lax.broadcasted_iota(jnp.int32, (8, lanes), 0)
 
     def wrap(ref):
@@ -429,12 +407,17 @@
 
 def edges_kernel(
     ice_hbm, own_low, own_high, one_ref, two_ref, rhs_ref, low_ref, high_ref, base_ref, vel_hbm, adj_in,
-    adj_hbm, grad_ref, ice, field, coefs, rhs, one, two, patch, vel, sem_in, sem_out,
+    adj_hbm, grad_hbm, ice, field, coefs, rhs, one, two, patch, vel, grad, sem_in, sem_out,
 ):
     tiles, _, layers = coefs.shape[1:4]
-    rows, cols = grad_ref.shape
+    rows, cols = grad.shape
     lanes = coefs.shape[5]
     blocks = tiles - 1
+    spans = [pl.ds(0, 8), pl.ds(rows - 8, 8), pl.ds(8, rows - 16)]
+    gradients = [
+        pltpu.make_async_copy(grad.at[span, :], grad_hbm.at[span, :], sem_out.at[2 + n])
+        for n, span in enumerate(spans)
+    ]
     fetches = [
         pltpu.make_async_copy(vel_hbm.at[:, 0], vel, sem_in.at[0]),
         pltpu.make_async_copy(ice_hbm, ice, sem_in.at[1]),
@@ -454,6 +437,11 @@
                 rhs[0, n, t, 4:12] = rhs_ref[n, t, 0:8]
                 rhs[1, n, t, 4:12] = rhs_ref[n, t, rows - 8 : rows]
                 rhs[1, n, t, 12:16] = after
+    wait_all(fetches)
+    inside = spans[2]
+    product = base_ref[0, inside] * vel[0, inside] + base_ref[1, inside] * vel[1, inside]
+    grad[inside] = -filled(ice, (rows - 16, cols)) * product
+    gradients[2].start()
     starts = (2, 6)
 
     def at(ref, start):
@@ -520,14 +508,11 @@
 
             relax_columns(layers, t, tiles, old, rhs_of, coef, store)
         result(side).start()
-    wait_all(fetches)
-    icefield = filled(ice, (rows, cols))
-    product = base_ref[0] * vel[0] + base_ref[1] * vel[1]
-    grad_ref[...] = -icefield * product
     for side in range(2):
-        span = slice(side * (rows - 8), side * (rows - 8) + 8)
-        product = patch[side, 0, 0] * vel[0, span] + patch[side, 1, 0] * vel[1, span]
-        grad_ref[span] = -icefield[0:8] * product
+        product = patch[side, 0, 0] * vel[0, spans[side]] + patch[side, 1, 0] * vel[1, spans[side]]
+        grad[spans[side]] = -filled(ice, (8, cols)) * product
+        gradients[side].start()
+    wait_all(gradients)
     for side in range(2):
         result(side).wait()
 
@@ -578,7 +563,7 @@
             pltpu.VMEM(cells_in.shape, i32),
             pltpu.SemaphoreType.DMA((3,)),
         ],
-        compiler_params=grant(62.5),
+        compiler_params=grant(61.5),
         cost_estimate=pl.CostEstimate(flops=4 * 10**9, transcendentals=0, bytes_accessed=0),
         name="pack",
     )(counts_in, tiles_in, cells_in)
@@ -595,7 +580,7 @@
             pltpu.VMEM((2, 2, rows, lanes), f32),
             pltpu.SemaphoreType.DMA((7,)),
         ],
-        compiler_params=grant(62.5),
+        compiler_params=grant(61.5),
         cost_estimate=pl.CostEstimate(flops=4 * 10**9, transcendentals=0, bytes_accessed=0),
         name="columns",
     )(ice_mask, viscosity, friction, velocity)
@@ -604,24 +589,31 @@
 
     own = shape(layers + 2, tiles, 8, lanes)
     edge = shape(layers + 4, tiles, 4, lanes)
-    rhs, own_low, own_high, xsend_one, xsend_two = pl.pallas_call(
+    rhs, field, own_low, own_high, xsend_one, xsend_two = pl.pallas_call(
         functools.partial(sources_kernel, slots),
-        out_shape=(shape(2, tiles, rows, lanes), own, own, edge, edge),
+        out_shape=(
+            shape(2, tiles, rows, lanes),
+            shape(layers + 2, tiles, rows + 2 * MARGIN, lanes),
+            own,
+            own,
+            edge,
+            edge,
+        ),
         in_specs=[hbm, whole(), hbm, hbm, hbm, anywhere, anywhere],
-        out_specs=(whole(),) * 5,
+        out_specs=(whole(),) * 6,
         scratch_shapes=[
             pltpu.VMEM((1, 1), i32),
-            pltpu.VMEM((2, layers, 8, cols), f32),
-            pltpu.VMEM((2, 8, cols), f32),
             pltpu.VMEM((2, rows, cols), f32),
             pltpu.VMEM((rows, lanes), f32),
             pltpu.VMEM((rows, lanes), f32),
-            pltpu.SemaphoreType.DMA((8,)),
+            pltpu.SemaphoreType.DMA((2 * blocks + 4,)),
         ],
-        compiler_params=grant(52),
+        compiler_params=grant(47.5),
         cost_estimate=pl.CostEstimate(flops=4 * 10**9, transcendentals=0, bytes_accessed=0),
         name="sources",
-    )(ice_mask, arrived.reshape(owners * 4 * slots, lanes), viscosity, friction, velocity, yone, ytwo)
+    )(
+        ice_mask, arrived.reshape(owners * 4 * slots, lanes), viscosity, friction, velocity, yone, ytwo
+    )
     xone = swap(xsend_one, "gx", 0)
     xtwo = swap(xsend_two, "gx", 1)
 
@@ -630,31 +622,25 @@
     adjoint, low, high, base = pl.pallas_call(
         inner_kernel,
         out_shape=(shape(*velocity.shape), ends, ends, shape(2, rows, cols)),
-        in_specs=[hbm, hbm, hbm, anywhere, anywhere, anywhere],
+        in_specs=[whole(), whole()],
         out_specs=(hbm, whole(), whole(), whole()),
         scratch_shapes=[
-            pltpu.VMEM((1, 1), i32),
-            pltpu.VMEM((layers + 2, tiles, rows + 2 * MARGIN, lanes), f32),
-            pltpu.VMEM((rows, lanes), f32),
-            pltpu.VMEM((rows, lanes), f32),
-            pltpu.VMEM((2, tiles, rows, lanes), f32),
             pltpu.VMEM((steps, tiles, FACES, layers, 8, lanes), f32),
             wide,
             wide,
             pltpu.VMEM((2, layers, blocks, rows, lanes), f32),
-            pltpu.SemaphoreType.DMA((2 * blocks + 4,)),
             pltpu.SemaphoreType.DMA((blocks,)),
         ],
-        compiler_params=grant(30),
+        compiler_params=grant(28),
         cost_estimate=pl.CostEstimate(flops=4 * 10**9, transcendentals=0, bytes_accessed=0),
         name="inner",
-    )(ice_mask, viscosity, friction, yone, ytwo, rhs)
+    )(field, rhs)
 
     return pl.pallas_call(
         edges_kernel,
         out_shape=(shape(*velocity.shape), shape(rows, cols)),
         in_specs=[hbm] + [whole()] * 8 + [hbm, hbm],
-        out_specs=(hbm, whole()),
+        out_specs=(hbm, hbm),
         scratch_shapes=[
             pltpu.VMEM((1, 1), i32),
             pltpu.VMEM((2, layers + 2, tiles, 16, lanes), f32),
@@ -664,8 +650,9 @@
             pltpu.VMEM((2, 2, layers, tiles, 16, lanes), f32),
             pltpu.VMEM((2, 2, layers, 8, cols), f32),
             pltpu.VMEM((2, rows, cols), f32),
+            pltpu.VMEM((rows, cols), f32),
             pltpu.SemaphoreType.DMA((2,)),
-            pltpu.SemaphoreType.DMA((2,)),
+            pltpu.SemaphoreType.DMA((5,)),
         ],
         input_output_aliases={10: 0},
         compiler_params=grant(14),

time: 38 us -> 36.4 us (0.958)
  Pallas kernels: 18.7 us -> 17.2 us
    pallas_call x1, Pallas kernels: 8.65 us -> 7.82 us  [per_device(): pl.pallas_call(inner_kernel, out_shape=(shape(*velocity.shape), ends, end...]
    pallas_call x1, Pallas kernels: 3.05 us -> 2.5 us  [per_device(): pl.pallas_call(edges_kernel, out_shape=(shape(*velocity.shape), shape(row...]
where the time goes in v4:
time: 36.4 us; the launch traced here: 36.1 us
  Pallas kernels  17.2 us (47%)
  starting transfers between devices  12.7 us (35%)
  waiting for transfers between devices  4.82 us (13%)
  between operations  1.38 us (4%)
    pallas_call x1, Pallas kernels, per_device(): pl.pallas_call(inner_kernel, out_shape=(shape(*velocity.shape), ends, end...  7.82 us
    all_to_all x1, starting transfers between devices, per_device(): lax.all_to_all(packed, ('gx', 'gy'), split_axis=0, concat_axis=0, tiled=T...  7.1 us
    ppermute x4, starting transfers between devices, swap(): return lax.ppermute(value, axis, pairs)  5.58 us
    all_to_all x1, waiting for transfers between devices, per_device(): lax.all_to_all(packed, ('gx', 'gy'), split_axis=0, concat_axis=0, tiled=T...  2.58 us
    pallas_call x1, Pallas kernels, per_device(): pl.pallas_call(edges_kernel, out_shape=(shape(*velocity.shape), shape(row...  2.5 us
    pallas_call x1, Pallas kernels, per_device(): pl.pallas_call(columns_kernel, out_shape=(plane, plane), in_specs=[hbm] *...  2.47 us
    pallas_call x1, Pallas kernels, per_device(): pl.pallas_call(functools.partial(sources_kernel, slots), out_shape=(shape...  2.39 us
    ppermute x4, waiting for transfers between devices, swap(): return lax.ppermute(value, axis, pairs)  2.24 us
  transfers between devices with their start and end apart: 5, of which 2 were waited for; matrix products, arithmetic and copies ran while one was open for 0% of the time, Pallas kernels for 29%

profile of v4, /device:TPU:1, one launch (start us, length us, event | category | flops | bytes accessed | tf_op | source)
XLA Modules:
  0.0 36.1 jit_solution(11032306331847984869)
XLA Ops:
  0.6 2.0 %pack.1 = f32[32,16,128]{2,1,0:T(8,128)} custom-call(s32[4,8]{1,0:T(4,128)} %bitcast.13, f32[32,3,4,128]{3,2,1,0:T(4,128)} %bitcast.11, s32[4,4,8]{2,1,0:T(4,128)} %bitcast.12), custom_call_target="tpu_custom_call" | custom-call | flops 4000000000 | tf_op jit(solution)/shard_map/pack/pallas_call | solution.py:555
  2.7 7.1 %all-to-all-start = ((f32[32,16,128]{2,1,0:T(8,128)}), f32[32,16,128]{2,1,0:T(8,128)S(1)}, u32[]{:S(2)}, u32[]{:S(2)}) async-start(f32[32,16,128]{2,1,0:T(8,128)} %pack.1), calls=%async_computation | async-start | bytes 524288 | tf_op jit(solution)/shard_map/all_to_all | solution.py:570
  10.4 0.0 copy-start.1
  10.4 0.0 copy-start.2
  10.5 2.5 %columns.1 = (f32[96,128]{1,0:T(8,128)}, f32[96,128]{1,0:T(8,128)}) custom-call(s32[1,1]{1,0:T(1,128)S(6)} %copy.11.ice_hbm, f32[10,96,384]{2,1,0:T(8,128)} %visc_hbm.3, f32[96,384]{1,0:T(8,128)} %fric_hbm.3, f32[2,10,96,384]{3,2,1,0:T(8,128)} %vel_hbm.5), custom_call_target="tpu_custom_call" | custom-call | flops 4000000000 | tf_op jit(solution)/shard_map/columns/pallas_call | solution.py:571
  12.9 1.5 %collective-permute-start = (f32[96,128]{1,0:T(8,128)}, f32[96,128]{1,0:T(8,128)S(1)}, u32[]{:S(2)}, u32[]{:S(2)}) collective-permute-start(f32[96,128]{1,0:T(8,128)} %get-tuple-element.14), channel_id=1, source_target_pairs={{0,1},{1,0},{2,3},{3,2},{4,5},{5,4},{6,7},{7,6},{8,9},{9,8},{10,11... | collective-permute-start | bytes 147464 | tf_op jit(solution)/shard_map/ppermute | solution.py:543
  14.4 0.7 %collective-permute-start.1 = (f32[96,128]{1,0:T(8,128)}, f32[96,128]{1,0:T(8,128)S(1)}, u32[]{:S(2)}, u32[]{:S(2)}) collective-permute-start(f32[96,128]{1,0:T(8,128)} %get-tuple-element.15), channel_id=1, source_target_pairs={{1,2},{2,1},{5,6},{6,5},{9,10},{10,9},{13,14},{14,13},{17,18},{18,... | collective-permute-start | bytes 147464 | tf_op jit(solution)/shard_map/ppermute | solution.py:543
  15.1 2.2 %collective-permute-done.one_any = f32[96,128]{1,0:T(8,128)S(1)} collective-permute-done((f32[96,128]{1,0:T(8,128)}, f32[96,128]{1,0:T(8,128)S(1)}, u32[]{:S(2)}, u32[]{:S(2)}) %collective-permute-start) | collective-permute-done | bytes 49184 | tf_op jit(solution)/shard_map/ppermute | solution.py:543
  17.3 0.0 collective-permute-done.1.two_any
  17.3 2.6 %all-to-all-done = f32[32,16,128]{2,1,0:T(8,128)S(1)} async-done(((f32[32,16,128]{2,1,0:T(8,128)}), f32[32,16,128]{2,1,0:T(8,128)S(1)}, u32[]{:S(2)}, u32[]{:S(2)}) %all-to-all-start) | async-done | bytes 262176 | tf_op jit(solution)/shard_map/all_to_all | solution.py:570
  19.9 0.0 copy-done.1
  19.9 0.0 copy-done.2
  19.9 2.4 %sources.1 = (f32[2,4,96,128]{3,2,1,0:T(8,128)S(1)}, f32[12,4,112,128]{3,2,1,0:T(8,128)S(1)}, f32[12,4,8,128]{3,2,1,0:T(8,128)S(1)}, f32[12,4,8,128]{3,2,1,0:T(8...) custom-call(s32[1,1]{1,0:T(1,128)S(6)} %copy.11.ice_hbm, f32[512,128]{1,0:T(8,128)S(1)} %bitcast.10, ...), custom_call_target="tpu_custom_call" | custom-call | flops 4000000000 | tf_op jit(solution)/shard_map/sources/pallas_call | solution.py:592
  22.3 0.4 %collective-permute-start.2 = (f32[14,4,4,128]{3,2,1,0:T(4,128)S(1)}, f32[14,4,4,128]{3,2,1,0:T(4,128)S(1)}, u32[]{:S(2)}, u32[]{:S(2)}) collective-permute-start(f32[14,4,4,128]{3,2,1,0:T(4,128)S(1)} %get-tuple-element.18), channel_id=1, source_target_pairs={{0,4},{4,0},{8,12},{12,8},{16,20},{20,16},{24,28},{28,24},{1,5},{5... | collective-permute-start | bytes 344072 | tf_op jit(solution)/shard_map/ppermute | solution.py:543
  22.7 3.0 %collective-permute-start.3 = (f32[14,4,4,128]{3,2,1,0:T(4,128)S(1)}, f32[14,4,4,128]{3,2,1,0:T(4,128)S(1)}, u32[]{:S(2)}, u32[]{:S(2)}) collective-permute-start(f32[14,4,4,128]{3,2,1,0:T(4,128)S(1)} %get-tuple-element.19), channel_id=1, source_target_pairs={{4,8},{8,4},{12,16},{16,12},{20,24},{24,20},{5,9},{9,5},{13,17},{1... | collective-permute-start | bytes 344072 | tf_op jit(solution)/shard_map/ppermute | solution.py:543
  25.8 0.0 copy-start
  25.8 7.8 %inner.1 = (f32[2,10,96,384]{3,2,1,0:T(8,128)}, f32[2,10,3,8,128]{4,3,2,1,0:T(8,128)S(1)}, f32[2,10,3,8,128]{4,3,2,1,0:T(8,128)S(1)}, f32[2,96,384]{2,1,0:T(8,128)S(1)}) custom-call(f32[12,4,112,128]{3,2,1,0:T(8,128)S(1)} %get-tuple-element.21.field, f32[2,4,96,128]{3,2,1,0:T(8,128)S(1)} %get-tuple-element.20.rhs.rhs_ref), custom_call_target="tpu_custom_call" | custom-call | flops 4000000000 | tf_op jit(solution)/shard_map/inner/pallas_call | solution.py:622
  33.6 0.0 collective-permute-done.2.one_ref
  33.6 0.0 collective-permute-done.3.two_ref
  33.6 0.0 copy-done
  33.6 2.5 %edges.1 = (f32[2,10,96,384]{3,2,1,0:T(8,128)}, f32[96,384]{1,0:T(8,128)}) custom-call(s32[1,1]{1,0:T(1,128)S(6)} %copy.11.ice_hbm, f32[12,4,8,128]{3,2,1,0:T(8,128)S(1)} %get-tuple-element.16.own_low, f32[12,4,8,128]{3,2,1,0:T(8,128)S(1)} %get-tuple-element.17.own_high, ...), custom_call_target="tpu_custom_call", output_to_operand_aliasing={{0}: (10, {})} | custom-call | flops 4000000000 | tf_op jit(solution)/shard_map/edges/pallas_call | solution.py:639
Async XLA Ops:
  2.7 17.2 %all-to-all-start = ((f32[32,16,128]{2,1,0:T(8,128)}), f32[32,16,128]{2,1,0:T(8,128)S(1)}, u32[]{:S(2)}, u32[]{:S(2)}) async-start(f32[32,16,128]{2,1,0:T(8,128)} %pack.1), calls=%async_computation | async-start | bytes 524288 | tf_op jit(solution)/shard_map/all_to_all | solution.py:570
  10.4 9.4 %copy-start.1 = (f32[10,96,384]{2,1,0:T(8,128)S(1)}, f32[10,96,384]{2,1,0:T(8,128)}, u32[]{:S(2)}) copy-start(f32[10,96,384]{2,1,0:T(8,128)} %visc_hbm.3) | copy-start | bytes 4423684
  10.4 9.4 %copy-start.2 = (f32[96,384]{1,0:T(8,128)S(1)}, f32[96,384]{1,0:T(8,128)}, u32[]{:S(2)}) copy-start(f32[96,384]{1,0:T(8,128)} %fric_hbm.3) | copy-start | bytes 442372
  12.9 4.3 %collective-permute-start = (f32[96,128]{1,0:T(8,128)}, f32[96,128]{1,0:T(8,128)S(1)}, u32[]{:S(2)}, u32[]{:S(2)}) collective-permute-start(f32[96,128]{1,0:T(8,128)} %get-tuple-element.14), channel_id=1, source_target_pairs={{0,1},{1,0},{2,3},{3,2},{4,5},{5,4},{6,7},{7,6},{8,9},{9,8},{10,11... | collective-permute-start | bytes 147464 | tf_op jit(solution)/shard_map/ppermute | solution.py:543
  14.4 2.9 %collective-permute-start.1 = (f32[96,128]{1,0:T(8,128)}, f32[96,128]{1,0:T(8,128)S(1)}, u32[]{:S(2)}, u32[]{:S(2)}) collective-permute-start(f32[96,128]{1,0:T(8,128)} %get-tuple-element.15), channel_id=1, source_target_pairs={{1,2},{2,1},{5,6},{6,5},{9,10},{10,9},{13,14},{14,13},{17,18},{18,... | collective-permute-start | bytes 147464 | tf_op jit(solution)/shard_map/ppermute | solution.py:543
  22.3 11.3 %collective-permute-start.2 = (f32[14,4,4,128]{3,2,1,0:T(4,128)S(1)}, f32[14,4,4,128]{3,2,1,0:T(4,128)S(1)}, u32[]{:S(2)}, u32[]{:S(2)}) collective-permute-start(f32[14,4,4,128]{3,2,1,0:T(4,128)S(1)} %get-tuple-element.18), channel_id=1, source_target_pairs={{0,4},{4,0},{8,12},{12,8},{16,20},{20,16},{24,28},{28,24},{1,5},{5... | collective-permute-start | bytes 344072 | tf_op jit(solution)/shard_map/ppermute | solution.py:543
  22.7 10.9 %collective-permute-start.3 = (f32[14,4,4,128]{3,2,1,0:T(4,128)S(1)}, f32[14,4,4,128]{3,2,1,0:T(4,128)S(1)}, u32[]{:S(2)}, u32[]{:S(2)}) collective-permute-start(f32[14,4,4,128]{3,2,1,0:T(4,128)S(1)} %get-tuple-element.19), channel_id=1, source_target_pairs={{4,8},{8,4},{12,16},{16,12},{20,24},{24,20},{5,9},{9,5},{13,17},{1... | collective-permute-start | bytes 344072 | tf_op jit(solution)/shard_map/ppermute | solution.py:543
  25.8 7.9 %copy-start = (f32[2,10,96,384]{3,2,1,0:T(8,128)S(1)}, f32[2,10,96,384]{3,2,1,0:T(8,128)}, u32[]{:S(2)}) copy-start(f32[2,10,96,384]{3,2,1,0:T(8,128)} %vel_hbm.5) | copy-start | bytes 8847364

commit v5 on v4

--- a/solution.py
+++ b/solution.py
@@ -104,31 +104,26 @@
             out_ref[ox * owners_y + oy, 3 * slots : 4 * slots] = meta
 
 
-def columns_kernel(ice_hbm, visc_hbm, fric_hbm, vel_hbm, one_ref, two_ref, ice, visc, fric, vel, sems):
-    layers, rows, cols = visc_hbm.shape
+def columns_kernel(ice_hbm, visc_ref, fric_ref, top_ref, one_ref, two_ref, ice, sem):
+    layers, rows, cols = visc_ref.shape
     lanes = one_ref.shape[1]
-    top = vel_hbm.at[:, vel_hbm.shape[1] - 1]
-    pairs = [(ice_hbm, ice)]
-    for side, span in enumerate((pl.ds(0, lanes), pl.ds(cols - lanes, lanes))):
-        pairs.append((visc_hbm.at[:, :, span], visc.at[side]))
-        pairs.append((fric_hbm.at[:, span], fric.at[side]))
-        pairs.append((top.at[:, :, span], vel.at[side]))
-    copies = [pltpu.make_async_copy(a, b, sems.at[n]) for n, (a, b) in enumerate(pairs)]
-    fetch_all(copies)
-    wait_all(copies)
+    copy = pltpu.make_async_copy(ice_hbm, ice, sem)
+    copy.start()
+    copy.wait()
+    left, right = slice(0, lanes), slice(cols - lanes, cols)
     lane = lanes_of((rows, lanes))
     icefield = filled(ice, (rows, lanes))
     first = jnp.zeros((rows, lanes), jnp.float32)
     last = jnp.zeros((rows, lanes), jnp.float32)
     for k in range(layers + 4):
         if k < layers:
-            mine = (visc[0, k], visc[1, k])
+            mine = (visc_ref[k, :, left], visc_ref[k, :, right])
         elif k == layers:
-            mine = (fric[0], fric[1])
+            mine = (fric_ref[:, left], fric_ref[:, right])
         elif k == layers + 1:
             mine = (icefield, icefield)
         else:
-            mine = (vel[0, k - layers - 2], vel[1, k - layers - 2])
+            mine = (top_ref[k - layers - 2, :, left], top_ref[k - layers - 2, :, right])
         here = (lane >= 3 * k) & (lane < 3 * k + 3)
         first = jnp.where(here, pltpu.roll(mine[0], 3 * k, 1), first)
         there = (lane >= lanes - 3 - 3 * k) & (lane < lanes - 3 * k)
@@ -220,15 +215,15 @@
 
 
 def sources_kernel(
-    slots, ice_hbm, tiles_ref, visc_hbm, fric_hbm, vel_hbm, one_any, two_any,
-    rhs_ref, field, low_ref, high_ref, xone_ref, xtwo_ref, ice, vel, one, two, sems,
+    slots, ice_hbm, tiles_ref, visc_hbm, fric_hbm, vel, one, two,
+    rhs_ref, field, low_ref, high_ref, xone_ref, xtwo_ref, ice, sems,
 ):
     layers, rows, cols = visc_hbm.shape
     lanes = tiles_ref.shape[1]
     owners = tiles_ref.shape[0] // (4 * slots)
     blocks = cols // lanes
     middle = pl.ds(MARGIN, rows)
-    pairs = [(vel_hbm.at[:, layers - 1], vel), (one_any, one), (two_any, two), (ice_hbm, ice)]
+    pairs = [(ice_hbm, ice)]
     for t in range(blocks):
         span = pl.ds(t * lanes, lanes)
         pairs.append((visc_hbm.at[:, :, span], field.at[pl.ds(0, layers), t, middle, :]))
@@ -267,7 +262,6 @@
 
     own = meta[:, lanes // 2 : lanes // 2 + 1]
     marks = jnp.concatenate([onehot(own, b) for b in range(blocks)], axis=1)
-    wait_all(copies[:1])
     surface = jnp.concatenate(
         [
             jnp.concatenate([vel[c, :, b * lanes : (b + 1) * lanes] for b in range(blocks)], axis=0)
@@ -282,7 +276,7 @@
         for b in range(blocks):
             put(c, b, total[b * rows : (b + 1) * rows, c * lanes : (c + 1) * lanes])
 
-    wait_all(copies[1:4])
+    wait_all(copies[:1])
     icefield = filled(ice, (rows, lanes))
     from_before, from_after = received("gy", one[...], two[...])
     for k in range(layers + 2):
@@ -305,7 +299,7 @@
     for c in range(2):
         put(c, blocks, side[:, c * lanes : (c + 1) * lanes])
 
-    wait_all(copies[4:])
+    wait_all(copies[1:])
     for k in range(layers + 2):
         for t in range(blocks + 1):
             low = field[k, t, MARGIN : MARGIN + 8]
@@ -567,23 +561,18 @@
         cost_estimate=pl.CostEstimate(flops=4 * 10**9, transcendentals=0, bytes_accessed=0),
         name="pack",
     )(counts_in, tiles_in, cells_in)
+    top = velocity[:, layers - 1]
     arrived = lax.all_to_all(packed, ("gx", "gy"), split_axis=0, concat_axis=0, tiled=True)
     ysend_one, ysend_two = pl.pallas_call(
         columns_kernel,
         out_shape=(plane, plane),
-        in_specs=[hbm] * 4,
+        in_specs=[hbm, whole(), whole(), whole()],
         out_specs=(whole(), whole()),
-        scratch_shapes=[
-            pltpu.VMEM((1, 1), i32),
-            pltpu.VMEM((2, layers, rows, lanes), f32),
-            pltpu.VMEM((2, rows, lanes), f32),
-            pltpu.VMEM((2, 2, rows, lanes), f32),
-            pltpu.SemaphoreType.DMA((7,)),
-        ],
-        compiler_params=grant(61.5),
+        scratch_shapes=[pltpu.VMEM((1, 1), i32), pltpu.SemaphoreType.DMA(())],
+        compiler_params=grant(52),
         cost_estimate=pl.CostEstimate(flops=4 * 10**9, transcendentals=0, bytes_accessed=0),
         name="columns",
-    )(ice_mask, viscosity, friction, velocity)
+    )(ice_mask, viscosity, friction, top)
     yone = swap(ysend_one, "gy", 0)
     ytwo = swap(ysend_two, "gy", 1)
 
@@ -599,20 +588,17 @@
             edge,
             edge,
         ),
-        in_specs=[hbm, whole(), hbm, hbm, hbm, anywhere, anywhere],
+        in_specs=[hbm, whole(), hbm, hbm, whole(), whole(), whole()],
         out_specs=(whole(),) * 6,
         scratch_shapes=[
             pltpu.VMEM((1, 1), i32),
-            pltpu.VMEM((2, rows, cols), f32),
-            pltpu.VMEM((rows, lanes), f32),
-            pltpu.VMEM((rows, lanes), f32),
-            pltpu.SemaphoreType.DMA((2 * blocks + 4,)),
+            pltpu.SemaphoreType.DMA((2 * blocks + 1,)),
         ],
         compiler_params=grant(47.5),
         cost_estimate=pl.CostEstimate(flops=4 * 10**9, transcendentals=0, bytes_accessed=0),
         name="sources",
     )(
-        ice_mask, arrived.reshape(owners * 4 * slots, lanes), viscosity, friction, velocity, yone, ytwo
+        ice_mask, arrived.reshape(owners * 4 * slots, lanes), viscosity, friction, top, yone, ytwo
     )
     xone = swap(xsend_one, "gx", 0)
     xtwo = swap(xsend_two, "gx", 1)

time: 36.4 us -> 35.8 us (0.984)
  Pallas kernels: 17.2 us -> 14.5 us
  waiting for transfers between devices: 4.82 us -> 5.9 us
  local copies, waits for them, and re-layouts: 0.02 us -> 1 us
    pallas_call x1, Pallas kernels: 2.47 us -> 0.4 us  [per_device(): pl.pallas_call(columns_kernel, out_shape=(plane, plane), in_specs=[hbm, w...]
    all_to_all x1, waiting for transfers between devices: 2.58 us -> 3.6 us  [per_device(): lax.all_to_all(packed, ('gx', 'gy'), split_axis=0, concat_axis=0, tiled=T...]
    squeeze x0 -> x1, local copies, waits for them, and re-layouts: none -> 0.99 us  [per_device(): top = velocity[:, layers - 1]]
    pallas_call x1, Pallas kernels: 2.39 us -> 1.66 us  [per_device(): pl.pallas_call(functools.partial(sources_kernel, slots), out_shape=(shape...]
  transfers between devices with their start and end apart: 5 -> 5, of which waited for: 2 -> 2; matrix products, arithmetic and copies ran while one was open for 0% -> 3% of each run, Pallas kernels for 29% -> 23%
where the time goes in v5:
time: 35.8 us; the launch traced here: 35.5 us
  Pallas kernels  14.5 us (41%)
  starting transfers between devices  12.7 us (35%)
  waiting for transfers between devices  5.9 us (16%)
  between operations  1.4 us (4%)
  local copies, waits for them, and re-layouts  1 us (3%)
    pallas_call x1, Pallas kernels, per_device(): pl.pallas_call(inner_kernel, out_shape=(shape(*velocity.shape), ends, end...  7.82 us
    all_to_all x1, starting transfers between devices, per_device(): lax.all_to_all(packed, ('gx', 'gy'), split_axis=0, concat_axis=0, tiled=T...  7.1 us
    ppermute x4, starting transfers between devices, swap(): return lax.ppermute(value, axis, pairs)  5.59 us
    all_to_all x1, waiting for transfers between devices, per_device(): lax.all_to_all(packed, ('gx', 'gy'), split_axis=0, concat_axis=0, tiled=T...  3.6 us
    pallas_call x1, Pallas kernels, per_device(): pl.pallas_call(edges_kernel, out_shape=(shape(*velocity.shape), shape(row...  2.5 us
    ppermute x4, waiting for transfers between devices, swap(): return lax.ppermute(value, axis, pairs)  2.31 us
    pallas_call x1, Pallas kernels, per_device(): pl.pallas_call(pack_kernel, out_shape=shape(owners, 4 * slots, lanes), in...  2.16 us
    pallas_call x1, Pallas kernels, per_device(): pl.pallas_call(functools.partial(sources_kernel, slots), out_shape=(shape...  1.66 us
  transfers between devices with their start and end apart: 5, of which 2 were waited for; matrix products, arithmetic and copies ran while one was open for 3% of the time, Pallas kernels for 23%

profile of v5, /device:TPU:1, one launch (start us, length us, event | category | flops | bytes accessed | tf_op | source)
XLA Modules:
  0.0 35.5 jit_solution(12676819710167960746)
XLA Ops:
  0.6 0.0 copy-start.1
  0.6 0.0 copy-start.2
  0.7 2.2 %pack.1 = f32[32,16,128]{2,1,0:T(8,128)} custom-call(s32[4,8]{1,0:T(4,128)} %bitcast.17, f32[32,3,4,128]{3,2,1,0:T(4,128)} %bitcast.15, s32[4,4,8]{2,1,0:T(4,128)} %bitcast.16), custom_call_target="tpu_custom_call" | custom-call | flops 4000000000 | tf_op jit(solution)/shard_map/pack/pallas_call | solution.py:549
  2.8 7.1 %all-to-all-start = ((f32[32,16,128]{2,1,0:T(8,128)}), f32[32,16,128]{2,1,0:T(8,128)S(1)}, u32[]{:S(2)}, u32[]{:S(2)}) async-start(f32[32,16,128]{2,1,0:T(8,128)} %pack.1), calls=%async_computation | async-start | bytes 524288 | tf_op jit(solution)/shard_map/all_to_all | solution.py:565
  9.9 1.0 %slice_bitcast_fusion.top_ref.vel = f32[2,96,384]{2,1,0:T(8,128)S(1)} fusion(f32[2,10,96,384]{3,2,1,0:T(8,128)} %vel_hbm.1), kind=kLoop, calls=%fused_computation | loop fusion | bytes 589824 | tf_op jit(solution)/shard_map/squeeze | solution.py:564
  11.6 0.0 copy-done.1
  11.6 0.0 copy-done.2
  11.6 0.4 %columns.1 = (f32[96,128]{1,0:T(8,128)S(1)}, f32[96,128]{1,0:T(8,128)S(1)}) custom-call(s32[1,1]{1,0:T(1,128)S(6)} %copy.13.ice_hbm, f32[10,96,384]{2,1,0:T(8,128)S(1)} %copy-done.1, f32[96,384]{1,0:T(8,128)S(1)} %copy-done.2, f32[2,96,384]{2,1,0:T(8,128)S(1)} %slice_bitcast_fusion.top_ref.vel), custom_call_target="tpu_custom_call" | custom-call | flops 4000000000 | tf_op jit(solution)/shard_map/columns/pallas_call | solution.py:566
  12.0 1.5 %collective-permute-start = (f32[96,128]{1,0:T(8,128)S(1)}, f32[96,128]{1,0:T(8,128)S(1)}, u32[]{:S(2)}, u32[]{:S(2)}) collective-permute-start(f32[96,128]{1,0:T(8,128)S(1)} %get-tuple-element.14), channel_id=1, source_target_pairs={{0,1},{1,0},{2,3},{3,2},{4,5},{5,4},{6,7},{7,6},{8,9},{9,8},{10,11... | collective-permute-start | bytes 147464 | tf_op jit(solution)/shard_map/ppermute | solution.py:537
  13.4 0.7 %collective-permute-start.1 = (f32[96,128]{1,0:T(8,128)S(1)}, f32[96,128]{1,0:T(8,128)S(1)}, u32[]{:S(2)}, u32[]{:S(2)}) collective-permute-start(f32[96,128]{1,0:T(8,128)S(1)} %get-tuple-element.15), channel_id=1, source_target_pairs={{1,2},{2,1},{5,6},{6,5},{9,10},{10,9},{13,14},{14,13},{17,18},{18,... | collective-permute-start | bytes 147464 | tf_op jit(solution)/shard_map/ppermute | solution.py:537
  14.1 2.3 %collective-permute-done.one = f32[96,128]{1,0:T(8,128)S(1)} collective-permute-done((f32[96,128]{1,0:T(8,128)S(1)}, f32[96,128]{1,0:T(8,128)S(1)}, u32[]{:S(2)}, u32[]{:S(2)}) %collective-permute-start) | collective-permute-done | bytes 49184 | tf_op jit(solution)/shard_map/ppermute | solution.py:537
  16.4 0.0 collective-permute-done.1.two
  16.4 3.6 %all-to-all-done = f32[32,16,128]{2,1,0:T(8,128)S(1)} async-done(((f32[32,16,128]{2,1,0:T(8,128)}), f32[32,16,128]{2,1,0:T(8,128)S(1)}, u32[]{:S(2)}, u32[]{:S(2)}) %all-to-all-start) | async-done | bytes 262176 | tf_op jit(solution)/shard_map/all_to_all | solution.py:565
  20.0 1.7 %sources.1 = (f32[2,4,96,128]{3,2,1,0:T(8,128)S(1)}, f32[12,4,112,128]{3,2,1,0:T(8,128)S(1)}, f32[12,4,8,128]{3,2,1,0:T(8,128)S(1)}, f32[12,4,8,128]{3,2,1,0:T(8...) custom-call(s32[1,1]{1,0:T(1,128)S(6)} %copy.13.ice_hbm, f32[512,128]{1,0:T(8,128)S(1)} %bitcast.14, ...), custom_call_target="tpu_custom_call" | custom-call | flops 4000000000 | tf_op jit(solution)/shard_map/sources/pallas_call | solution.py:581
  21.7 0.4 %collective-permute-start.2 = (f32[14,4,4,128]{3,2,1,0:T(4,128)S(1)}, f32[14,4,4,128]{3,2,1,0:T(4,128)S(1)}, u32[]{:S(2)}, u32[]{:S(2)}) collective-permute-start(f32[14,4,4,128]{3,2,1,0:T(4,128)S(1)} %get-tuple-element.18), channel_id=1, source_target_pairs={{0,4},{4,0},{8,12},{12,8},{16,20},{20,16},{24,28},{28,24},{1,5},{5... | collective-permute-start | bytes 344072 | tf_op jit(solution)/shard_map/ppermute | solution.py:537
  22.1 3.0 %collective-permute-start.3 = (f32[14,4,4,128]{3,2,1,0:T(4,128)S(1)}, f32[14,4,4,128]{3,2,1,0:T(4,128)S(1)}, u32[]{:S(2)}, u32[]{:S(2)}) collective-permute-start(f32[14,4,4,128]{3,2,1,0:T(4,128)S(1)} %get-tuple-element.19), channel_id=1, source_target_pairs={{4,8},{8,4},{12,16},{16,12},{20,24},{24,20},{5,9},{9,5},{13,17},{1... | collective-permute-start | bytes 344072 | tf_op jit(solution)/shard_map/ppermute | solution.py:537
  25.2 0.0 copy-start
  25.2 7.8 %inner.1 = (f32[2,10,96,384]{3,2,1,0:T(8,128)}, f32[2,10,3,8,128]{4,3,2,1,0:T(8,128)S(1)}, f32[2,10,3,8,128]{4,3,2,1,0:T(8,128)S(1)}, f32[2,96,384]{2,1,0:T(8,128)S(1)}) custom-call(f32[12,4,112,128]{3,2,1,0:T(8,128)S(1)} %get-tuple-element.21.field, f32[2,4,96,128]{3,2,1,0:T(8,128)S(1)} %get-tuple-element.20.rhs.rhs_ref), custom_call_target="tpu_custom_call" | custom-call | flops 4000000000 | tf_op jit(solution)/shard_map/inner/pallas_call | solution.py:608
  33.0 0.0 collective-permute-done.2.one_ref
  33.0 0.0 collective-permute-done.3.two_ref
  33.0 0.0 copy-done
  33.0 2.5 %edges.1 = (f32[2,10,96,384]{3,2,1,0:T(8,128)}, f32[96,384]{1,0:T(8,128)}) custom-call(s32[1,1]{1,0:T(1,128)S(6)} %copy.13.ice_hbm, f32[12,4,8,128]{3,2,1,0:T(8,128)S(1)} %get-tuple-element.16.own_low, f32[12,4,8,128]{3,2,1,0:T(8,128)S(1)} %get-tuple-element.17.own_high, ...), custom_call_target="tpu_custom_call", output_to_operand_aliasing={{0}: (10, {})} | custom-call | flops 4000000000 | tf_op jit(solution)/shard_map/edges/pallas_call | solution.py:625
Async XLA Ops:
  0.6 10.9 %copy-start.1 = (f32[10,96,384]{2,1,0:T(8,128)S(1)}, f32[10,96,384]{2,1,0:T(8,128)}, u32[]{:S(2)}) copy-start(f32[10,96,384]{2,1,0:T(8,128)} %visc_hbm.1) | copy-start | bytes 4423684
  0.6 10.9 %copy-start.2 = (f32[96,384]{1,0:T(8,128)S(1)}, f32[96,384]{1,0:T(8,128)}, u32[]{:S(2)}) copy-start(f32[96,384]{1,0:T(8,128)} %fric_hbm.1) | copy-start | bytes 442372
  2.8 17.2 %all-to-all-start = ((f32[32,16,128]{2,1,0:T(8,128)}), f32[32,16,128]{2,1,0:T(8,128)S(1)}, u32[]{:S(2)}, u32[]{:S(2)}) async-start(f32[32,16,128]{2,1,0:T(8,128)} %pack.1), calls=%async_computation | async-start | bytes 524288 | tf_op jit(solution)/shard_map/all_to_all | solution.py:565
  12.0 4.4 %collective-permute-start = (f32[96,128]{1,0:T(8,128)S(1)}, f32[96,128]{1,0:T(8,128)S(1)}, u32[]{:S(2)}, u32[]{:S(2)}) collective-permute-start(f32[96,128]{1,0:T(8,128)S(1)} %get-tuple-element.14), channel_id=1, source_target_pairs={{0,1},{1,0},{2,3},{3,2},{4,5},{5,4},{6,7},{7,6},{8,9},{9,8},{10,11... | collective-permute-start | bytes 147464 | tf_op jit(solution)/shard_map/ppermute | solution.py:537
  13.4 3.0 %collective-permute-start.1 = (f32[96,128]{1,0:T(8,128)S(1)}, f32[96,128]{1,0:T(8,128)S(1)}, u32[]{:S(2)}, u32[]{:S(2)}) collective-permute-start(f32[96,128]{1,0:T(8,128)S(1)} %get-tuple-element.15), channel_id=1, source_target_pairs={{1,2},{2,1},{5,6},{6,5},{9,10},{10,9},{13,14},{14,13},{17,18},{18,... | collective-permute-start | bytes 147464 | tf_op jit(solution)/shard_map/ppermute | solution.py:537
  21.7 11.3 %collective-permute-start.2 = (f32[14,4,4,128]{3,2,1,0:T(4,128)S(1)}, f32[14,4,4,128]{3,2,1,0:T(4,128)S(1)}, u32[]{:S(2)}, u32[]{:S(2)}) collective-permute-start(f32[14,4,4,128]{3,2,1,0:T(4,128)S(1)} %get-tuple-element.18), channel_id=1, source_target_pairs={{0,4},{4,0},{8,12},{12,8},{16,20},{20,16},{24,28},{28,24},{1,5},{5... | collective-permute-start | bytes 344072 | tf_op jit(solution)/shard_map/ppermute | solution.py:537
  22.1 10.9 %collective-permute-start.3 = (f32[14,4,4,128]{3,2,1,0:T(4,128)S(1)}, f32[14,4,4,128]{3,2,1,0:T(4,128)S(1)}, u32[]{:S(2)}, u32[]{:S(2)}) collective-permute-start(f32[14,4,4,128]{3,2,1,0:T(4,128)S(1)} %get-tuple-element.19), channel_id=1, source_target_pairs={{4,8},{8,4},{12,16},{16,12},{20,24},{24,20},{5,9},{9,5},{13,17},{1... | collective-permute-start | bytes 344072 | tf_op jit(solution)/shard_map/ppermute | solution.py:537
  25.2 7.9 %copy-start = (f32[2,10,96,384]{3,2,1,0:T(8,128)S(1)}, f32[2,10,96,384]{3,2,1,0:T(8,128)}, u32[]{:S(2)}) copy-start(f32[2,10,96,384]{3,2,1,0:T(8,128)} %vel_hbm.1) | copy-start | bytes 8847364

commit v6 on v5

--- a/solution.py
+++ b/solution.py
@@ -309,9 +309,9 @@
             send(k, t, low[0:4], high[4:8])
 
 
-def inner_kernel(field, rhs, adj_hbm, low_ref, high_ref, base_ref, coef, one, two, three, sem_out):
+def inner_kernel(field, rhs, adj_hbm, low_ref, high_ref, base_ref, last_ref, coef, one, two, three, sem_out):
     steps, tiles, _, layers, _, lanes = coef.shape
-    rows = three.shape[3]
+    rows = last_ref.shape[2]
     def factors(r, carry):
         for t in range(tiles):
 
@@ -324,7 +324,7 @@
             factor_columns(layers, t, tiles, load, store)
         return carry
 
-    lax.fori_loop(0, steps, factors, 0, unroll=3)
+    lax.fori_loop(0, steps, factors, 0, unroll=6)
 
     sublane = lax.broadcasted_iota(jnp.int32, (8, lanes), 0)
 
@@ -352,7 +352,7 @@
             first_columns(layers, rhs_of(r, t), coef_of(r, t), store)
         return carry
 
-    lax.fori_loop(0, steps, first_sweep, 0, unroll=2)
+    lax.fori_loop(0, steps, first_sweep, 0, unroll=6)
     wrap(one)
 
     def second_sweep(r, carry):
@@ -376,31 +376,33 @@
         return pltpu.make_async_copy(three.at[:, :, t, middle, :], adj_hbm.at[:, :, middle, span], sem_out.at[t])
 
     for t in range(tiles - 1):
+        found = last_ref if t == tiles - 2 else three.at[:, :, t]
 
         def third_sweep(r, carry):
             def old(n, k, s, move):
                 return two[n, k, s, r + 1 + move]
 
             def store(n, k, value):
-                three[n, k, t, pl.ds(r, 8, stride=steps), :] = value
+                found[n, k, pl.ds(r, 8, stride=steps), :] = value
 
             relax_columns(layers, t, tiles, old, rhs_of(r, t), coef_of(r, t), store)
             return carry
 
         lax.fori_loop(0, steps, third_sweep, 0, unroll=12)
-        result(t).start()
+        if t < tiles - 2:
+            result(t).start()
         for n in range(2):
             for k in range(layers):
-                low_ref[n, k, t] = three[n, k, t, 0:8]
-                high_ref[n, k, t] = three[n, k, t, rows - 8 : rows]
+                low_ref[n, k, t] = found[n, k, 0:8]
+                high_ref[n, k, t] = found[n, k, rows - 8 : rows]
         for n in range(2):
-            base_ref[n, :, t * lanes : (t + 1) * lanes] = three[n, 0, t]
-    for t in range(tiles - 1):
+            base_ref[n, :, t * lanes : (t + 1) * lanes] = found[n, 0]
+    for t in range(tiles - 2):
         result(t).wait()
 
 
 def edges_kernel(
-    ice_hbm, own_low, own_high, one_ref, two_ref, rhs_ref, low_ref, high_ref, base_ref, vel_hbm, adj_in,
+    ice_hbm, own_low, own_high, one_ref, two_ref, rhs_ref, low_ref, high_ref, base_ref, last_ref, vel_hbm, adj_in,
     adj_hbm, grad_hbm, ice, field, coefs, rhs, one, two, patch, vel, grad, sem_in, sem_out,
 ):
     tiles, _, layers = coefs.shape[1:4]
@@ -417,6 +419,11 @@
         pltpu.make_async_copy(ice_hbm, ice, sem_in.at[1]),
     ]
     fetch_all(fetches)
+    inside = spans[2]
+    rest = pltpu.make_async_copy(
+        last_ref.at[:, :, inside, :], adj_hbm.at[:, :, inside, pl.ds(cols - lanes, lanes)], sem_out.at[5]
+    )
+    rest.start()
     for k in range(layers + 4):
         for t in range(tiles):
             before, after = received("gx", one_ref[k, t], two_ref[k, t])
@@ -431,11 +438,6 @@
                 rhs[0, n, t, 4:12] = rhs_ref[n, t, 0:8]
                 rhs[1, n, t, 4:12] = rhs_ref[n, t, rows - 8 : rows]
                 rhs[1, n, t, 12:16] = after
-    wait_all(fetches)
-    inside = spans[2]
-    product = base_ref[0, inside] * vel[0, inside] + base_ref[1, inside] * vel[1, inside]
-    grad[inside] = -filled(ice, (rows - 16, cols)) * product
-    gradients[2].start()
     starts = (2, 6)
 
     def at(ref, start):
@@ -480,6 +482,11 @@
                 two[side, n, k, t, pl.ds(starts[side], 8), :] = value
 
             relax_columns(layers, t, tiles, old, rhs_of, coef, store)
+
+    wait_all(fetches)
+    product = base_ref[0, inside] * vel[0, inside] + base_ref[1, inside] * vel[1, inside]
+    grad[inside] = -filled(ice, (rows - 16, cols)) * product
+    gradients[2].start()
 
     def result(side):
         return pltpu.make_async_copy(
@@ -507,6 +514,7 @@
         grad[spans[side]] = -filled(ice, (8, cols)) * product
         gradients[side].start()
     wait_all(gradients)
+    rest.wait()
     for side in range(2):
         result(side).wait()
 
@@ -605,17 +613,17 @@
 
     ends = shape(2, layers, blocks, 8, lanes)
     wide = pltpu.VMEM((2, layers, tiles, steps + 2, 8, lanes), f32)
-    adjoint, low, high, base = pl.pallas_call(
+    adjoint, low, high, base, last = pl.pallas_call(
         inner_kernel,
-        out_shape=(shape(*velocity.shape), ends, ends, shape(2, rows, cols)),
+        out_shape=(shape(*velocity.shape), ends, ends, shape(2, rows, cols), shape(2, layers, rows, lanes)),
         in_specs=[whole(), whole()],
-        out_specs=(hbm, whole(), whole(), whole()),
+        out_specs=(hbm, whole(), whole(), whole(), whole()),
         scratch_shapes=[
             pltpu.VMEM((steps, tiles, FACES, layers, 8, lanes), f32),
             wide,
             wide,
-            pltpu.VMEM((2, layers, blocks, rows, lanes), f32),
-            pltpu.SemaphoreType.DMA((blocks,)),
+            pltpu.VMEM((2, layers, blocks - 1, rows, lanes), f32),
+            pltpu.SemaphoreType.DMA((blocks - 1,)),
         ],
         compiler_params=grant(28),
         cost_estimate=pl.CostEstimate(flops=4 * 10**9, transcendentals=0, bytes_accessed=0),
@@ -625,7 +633,7 @@
     return pl.pallas_call(
         edges_kernel,
         out_shape=(shape(*velocity.shape), shape(rows, cols)),
-        in_specs=[hbm] + [whole()] * 8 + [hbm, hbm],
+        in_specs=[hbm] + [whole()] * 9 + [hbm, hbm],
         out_specs=(hbm, hbm),
         scratch_shapes=[
             pltpu.VMEM((1, 1), i32),
@@ -638,13 +646,13 @@
             pltpu.VMEM((2, rows, cols), f32),
             pltpu.VMEM((rows, cols), f32),
             pltpu.SemaphoreType.DMA((2,)),
-            pltpu.SemaphoreType.DMA((5,)),
+            pltpu.SemaphoreType.DMA((6,)),
         ],
-        input_output_aliases={10: 0},
+        input_output_aliases={11: 0},
         compiler_params=grant(14),
         cost_estimate=pl.CostEstimate(flops=4 * 10**9, transcendentals=0, bytes_accessed=0),
         name="edges",
-    )(ice_mask, own_low, own_high, xone, xtwo, rhs, low, high, base, velocity, adjoint)
+    )(ice_mask, own_low, own_high, xone, xtwo, rhs, low, high, base, last, velocity, adjoint)
 
 
 def solution(mesh):

time: 35.8 us -> 34.9 us (0.975)
  Pallas kernels: 14.5 us -> 13.6 us
    pallas_call x1, Pallas kernels: 7.82 us -> 6.95 us  [per_device(): pl.pallas_call(inner_kernel, out_shape=(shape(*velocity.shape), ends, end...]
  transfers between devices with their start and end apart: 5 -> 5, of which waited for: 2 -> 2; matrix products, arithmetic and copies ran while one was open for 3% -> 3% of each run, Pallas kernels for 23% -> 21%
where the time goes in v6:
time: 34.9 us; the launch traced here: 34.6 us
  Pallas kernels  13.6 us (39%)
  starting transfers between devices  12.7 us (36%)
  waiting for transfers between devices  5.9 us (17%)
  between operations  1.4 us (4%)
  local copies, waits for them, and re-layouts  1 us (3%)
    all_to_all x1, starting transfers between devices, per_device(): lax.all_to_all(packed, ('gx', 'gy'), split_axis=0, concat_axis=0, tiled=T...  7.1 us
    pallas_call x1, Pallas kernels, per_device(): pl.pallas_call(inner_kernel, out_shape=(shape(*velocity.shape), ends, end...  6.95 us
    ppermute x4, starting transfers between devices, swap(): return lax.ppermute(value, axis, pairs)  5.59 us
    all_to_all x1, waiting for transfers between devices, per_device(): lax.all_to_all(packed, ('gx', 'gy'), split_axis=0, concat_axis=0, tiled=T...  3.6 us
    pallas_call x1, Pallas kernels, per_device(): pl.pallas_call(edges_kernel, out_shape=(shape(*velocity.shape), shape(row...  2.47 us
    ppermute x4, waiting for transfers between devices, swap(): return lax.ppermute(value, axis, pairs)  2.31 us
    pallas_call x1, Pallas kernels, per_device(): pl.pallas_call(pack_kernel, out_shape=shape(owners, 4 * slots, lanes), in...  2.16 us
    pallas_call x1, Pallas kernels, per_device(): pl.pallas_call(functools.partial(sources_kernel, slots), out_shape=(shape...  1.66 us
  transfers between devices with their start and end apart: 5, of which 2 were waited for; matrix products, arithmetic and copies ran while one was open for 3% of the time, Pallas kernels for 21%

profile of v6, /device:TPU:1, one launch (start us, length us, event | category | flops | bytes accessed | tf_op | source)
XLA Modules:
  0.0 34.6 jit_solution(11748744563624211130)
XLA Ops:
  0.6 0.0 copy-start.1
  0.6 0.0 copy-start.2
  0.7 2.2 %pack.1 = f32[32,16,128]{2,1,0:T(8,128)} custom-call(s32[4,8]{1,0:T(4,128)} %bitcast.17, f32[32,3,4,128]{3,2,1,0:T(4,128)} %bitcast.15, s32[4,4,8]{2,1,0:T(4,128)} %bitcast.16), custom_call_target="tpu_custom_call" | custom-call | flops 4000000000 | tf_op jit(solution)/shard_map/pack/pallas_call | solution.py:557
  2.8 7.1 %all-to-all-start = ((f32[32,16,128]{2,1,0:T(8,128)}), f32[32,16,128]{2,1,0:T(8,128)S(1)}, u32[]{:S(2)}, u32[]{:S(2)}) async-start(f32[32,16,128]{2,1,0:T(8,128)} %pack.1), calls=%async_computation | async-start | bytes 524288 | tf_op jit(solution)/shard_map/all_to_all | solution.py:573
  9.9 1.0 %slice_bitcast_fusion.top_ref.vel = f32[2,96,384]{2,1,0:T(8,128)S(1)} fusion(f32[2,10,96,384]{3,2,1,0:T(8,128)} %vel_hbm.1), kind=kLoop, calls=%fused_computation | loop fusion | bytes 589824 | tf_op jit(solution)/shard_map/squeeze | solution.py:572
  11.6 0.0 copy-done.1
  11.6 0.0 copy-done.2
  11.6 0.4 %columns.1 = (f32[96,128]{1,0:T(8,128)S(1)}, f32[96,128]{1,0:T(8,128)S(1)}) custom-call(s32[1,1]{1,0:T(1,128)S(6)} %copy.13.ice_hbm, f32[10,96,384]{2,1,0:T(8,128)S(1)} %copy-done.1, f32[96,384]{1,0:T(8,128)S(1)} %copy-done.2, f32[2,96,384]{2,1,0:T(8,128)S(1)} %slice_bitcast_fusion.top_ref.vel), custom_call_target="tpu_custom_call" | custom-call | flops 4000000000 | tf_op jit(solution)/shard_map/columns/pallas_call | solution.py:574
  12.0 1.5 %collective-permute-start = (f32[96,128]{1,0:T(8,128)S(1)}, f32[96,128]{1,0:T(8,128)S(1)}, u32[]{:S(2)}, u32[]{:S(2)}) collective-permute-start(f32[96,128]{1,0:T(8,128)S(1)} %get-tuple-element.15), channel_id=1, source_target_pairs={{0,1},{1,0},{2,3},{3,2},{4,5},{5,4},{6,7},{7,6},{8,9},{9,8},{10,11... | collective-permute-start | bytes 147464 | tf_op jit(solution)/shard_map/ppermute | solution.py:545
  13.4 0.7 %collective-permute-start.1 = (f32[96,128]{1,0:T(8,128)S(1)}, f32[96,128]{1,0:T(8,128)S(1)}, u32[]{:S(2)}, u32[]{:S(2)}) collective-permute-start(f32[96,128]{1,0:T(8,128)S(1)} %get-tuple-element.16), channel_id=1, source_target_pairs={{1,2},{2,1},{5,6},{6,5},{9,10},{10,9},{13,14},{14,13},{17,18},{18,... | collective-permute-start | bytes 147464 | tf_op jit(solution)/shard_map/ppermute | solution.py:545
  14.1 2.3 %collective-permute-done.one = f32[96,128]{1,0:T(8,128)S(1)} collective-permute-done((f32[96,128]{1,0:T(8,128)S(1)}, f32[96,128]{1,0:T(8,128)S(1)}, u32[]{:S(2)}, u32[]{:S(2)}) %collective-permute-start) | collective-permute-done | bytes 49184 | tf_op jit(solution)/shard_map/ppermute | solution.py:545
  16.4 0.0 collective-permute-done.1.two
  16.4 3.6 %all-to-all-done = f32[32,16,128]{2,1,0:T(8,128)S(1)} async-done(((f32[32,16,128]{2,1,0:T(8,128)}), f32[32,16,128]{2,1,0:T(8,128)S(1)}, u32[]{:S(2)}, u32[]{:S(2)}) %all-to-all-start) | async-done | bytes 262176 | tf_op jit(solution)/shard_map/all_to_all | solution.py:573
  20.0 1.7 %sources.1 = (f32[2,4,96,128]{3,2,1,0:T(8,128)S(1)}, f32[12,4,112,128]{3,2,1,0:T(8,128)S(1)}, f32[12,4,8,128]{3,2,1,0:T(8,128)S(1)}, f32[12,4,8,128]{3,2,1,0:T(8...) custom-call(s32[1,1]{1,0:T(1,128)S(6)} %copy.13.ice_hbm, f32[512,128]{1,0:T(8,128)S(1)} %bitcast.14, ...), custom_call_target="tpu_custom_call" | custom-call | flops 4000000000 | tf_op jit(solution)/shard_map/sources/pallas_call | solution.py:589
  21.7 0.4 %collective-permute-start.2 = (f32[14,4,4,128]{3,2,1,0:T(4,128)S(1)}, f32[14,4,4,128]{3,2,1,0:T(4,128)S(1)}, u32[]{:S(2)}, u32[]{:S(2)}) collective-permute-start(f32[14,4,4,128]{3,2,1,0:T(4,128)S(1)} %get-tuple-element.19), channel_id=1, source_target_pairs={{0,4},{4,0},{8,12},{12,8},{16,20},{20,16},{24,28},{28,24},{1,5},{5... | collective-permute-start | bytes 344072 | tf_op jit(solution)/shard_map/ppermute | solution.py:545
  22.1 3.0 %collective-permute-start.3 = (f32[14,4,4,128]{3,2,1,0:T(4,128)S(1)}, f32[14,4,4,128]{3,2,1,0:T(4,128)S(1)}, u32[]{:S(2)}, u32[]{:S(2)}) collective-permute-start(f32[14,4,4,128]{3,2,1,0:T(4,128)S(1)} %get-tuple-element.20), channel_id=1, source_target_pairs={{4,8},{8,4},{12,16},{16,12},{20,24},{24,20},{5,9},{9,5},{13,17},{1... | collective-permute-start | bytes 344072 | tf_op jit(solution)/shard_map/ppermute | solution.py:545
  25.2 0.0 copy-start
  25.2 7.0 %inner.1 = (f32[2,10,96,384]{3,2,1,0:T(8,128)}, f32[2,10,3,8,128]{4,3,2,1,0:T(8,128)S(1)}, f32[2,10,3,8,128]{4,3,2,1,0:T(8,128)S(1)}, f32[2,96,384]{2,1,0:T(8,128)S(1)}, f32[2,10,96,128]{3,2,1,0:T(8,128)S(1)}) custom-call(f32[12,4,112,128]{3,2,1,0:T(8,128)S(1)} %get-tuple-element.22.field, f32[2,4,96,128]{3,2,1,0:T(8,128)S(1)} %get-tuple-element.21.rhs.rhs_ref), custom_call_target="tpu_custom_call" | custom-call | flops 4000000000 | tf_op jit(solution)/shard_map/inner/pallas_call | solution.py:616
  32.1 0.0 collective-permute-done.2.one_ref
  32.1 0.0 collective-permute-done.3.two_ref
  32.2 0.0 copy-done
  32.2 2.5 %edges.1 = (f32[2,10,96,384]{3,2,1,0:T(8,128)}, f32[96,384]{1,0:T(8,128)}) custom-call(s32[1,1]{1,0:T(1,128)S(6)} %copy.13.ice_hbm, f32[12,4,8,128]{3,2,1,0:T(8,128)S(1)} %get-tuple-element.17.own_low, f32[12,4,8,128]{3,2,1,0:T(8,128)S(1)} %get-tuple-element.18.own_high, ...), custom_call_target="tpu_custom_call", output_to_operand_aliasing={{0}: (11, {})} | custom-call | flops 4000000000 | tf_op jit(solution)/shard_map/edges/pallas_call | solution.py:633
Async XLA Ops:
  0.6 10.9 %copy-start.1 = (f32[10,96,384]{2,1,0:T(8,128)S(1)}, f32[10,96,384]{2,1,0:T(8,128)}, u32[]{:S(2)}) copy-start(f32[10,96,384]{2,1,0:T(8,128)} %visc_hbm.1) | copy-start | bytes 4423684
  0.6 10.9 %copy-start.2 = (f32[96,384]{1,0:T(8,128)S(1)}, f32[96,384]{1,0:T(8,128)}, u32[]{:S(2)}) copy-start(f32[96,384]{1,0:T(8,128)} %fric_hbm.1) | copy-start | bytes 442372
  2.8 17.2 %all-to-all-start = ((f32[32,16,128]{2,1,0:T(8,128)}), f32[32,16,128]{2,1,0:T(8,128)S(1)}, u32[]{:S(2)}, u32[]{:S(2)}) async-start(f32[32,16,128]{2,1,0:T(8,128)} %pack.1), calls=%async_computation | async-start | bytes 524288 | tf_op jit(solution)/shard_map/all_to_all | solution.py:573
  12.0 4.4 %collective-permute-start = (f32[96,128]{1,0:T(8,128)S(1)}, f32[96,128]{1,0:T(8,128)S(1)}, u32[]{:S(2)}, u32[]{:S(2)}) collective-permute-start(f32[96,128]{1,0:T(8,128)S(1)} %get-tuple-element.15), channel_id=1, source_target_pairs={{0,1},{1,0},{2,3},{3,2},{4,5},{5,4},{6,7},{7,6},{8,9},{9,8},{10,11... | collective-permute-start | bytes 147464 | tf_op jit(solution)/shard_map/ppermute | solution.py:545
  13.4 3.0 %collective-permute-start.1 = (f32[96,128]{1,0:T(8,128)S(1)}, f32[96,128]{1,0:T(8,128)S(1)}, u32[]{:S(2)}, u32[]{:S(2)}) collective-permute-start(f32[96,128]{1,0:T(8,128)S(1)} %get-tuple-element.16), channel_id=1, source_target_pairs={{1,2},{2,1},{5,6},{6,5},{9,10},{10,9},{13,14},{14,13},{17,18},{18,... | collective-permute-start | bytes 147464 | tf_op jit(solution)/shard_map/ppermute | solution.py:545
  21.7 10.5 %collective-permute-start.2 = (f32[14,4,4,128]{3,2,1,0:T(4,128)S(1)}, f32[14,4,4,128]{3,2,1,0:T(4,128)S(1)}, u32[]{:S(2)}, u32[]{:S(2)}) collective-permute-start(f32[14,4,4,128]{3,2,1,0:T(4,128)S(1)} %get-tuple-element.19), channel_id=1, source_target_pairs={{0,4},{4,0},{8,12},{12,8},{16,20},{20,16},{24,28},{28,24},{1,5},{5... | collective-permute-start | bytes 344072 | tf_op jit(solution)/shard_map/ppermute | solution.py:545
  22.1 10.0 %collective-permute-start.3 = (f32[14,4,4,128]{3,2,1,0:T(4,128)S(1)}, f32[14,4,4,128]{3,2,1,0:T(4,128)S(1)}, u32[]{:S(2)}, u32[]{:S(2)}) collective-permute-start(f32[14,4,4,128]{3,2,1,0:T(4,128)S(1)} %get-tuple-element.20), channel_id=1, source_target_pairs={{4,8},{8,4},{12,16},{16,12},{20,24},{24,20},{5,9},{9,5},{13,17},{1... | collective-permute-start | bytes 344072 | tf_op jit(solution)/shard_map/ppermute | solution.py:545
  25.2 7.0 %copy-start = (f32[2,10,96,384]{3,2,1,0:T(8,128)S(1)}, f32[2,10,96,384]{3,2,1,0:T(8,128)}, u32[]{:S(2)}) copy-start(f32[2,10,96,384]{3,2,1,0:T(8,128)} %vel_hbm.1) | copy-start | bytes 8847364
